TPU v7x, 32 devices: a whole 2x2x4 slice. The times are simulated.
32 devices in a mesh: dp: 16 (over z, y, x), mp: 2 (over core).
Axes of the slice: x: 2, y: 2, z: 4, core: 2. Of those that a mesh axis runs over, the one named last changes fastest.
Arguments:
- tokens: bfloat16 [48, 2048, 768], P('dp', None, 'mp'), may hold values from -6 to 6
- segments: int32 [48, 2048], P('dp'), may hold values from 0 to 3, never falling along the last dimension, each value on 1 to 1024 neighbouring positions
- present: int32 [48, 2048], P('dp'), may hold values 0 or 1
- chosen: int32 [48, 256], P('dp'), may hold values from 0 to 2047, as said below
- attention: bfloat16 [3, 768, 768], P(None, 'dp', 'mp'), may hold values from -0.21875 to 0.21875
- mixing: bfloat16 [768, 768], P('mp', 'dp'), may hold values from -0.875 to 0.875
- expand: bfloat16 [768, 3072], P('dp', 'mp'), may hold values from -0.21875 to 0.21875
- contract: bfloat16 [3072, 768], P('mp', 'dp'), may hold values from -0.109375 to 0.109375
- prenorm: bfloat16 [768], P('dp'), may hold values from 0.5 to 1.5
- midnorm: bfloat16 [768], P('dp'), may hold values from 0.5 to 1.5
- router: bfloat16 [768], P('dp'), may hold values from -0.21875 to 0.21875
- cotangent: bfloat16 [48, 2048, 768], P('dp', None, 'mp'), may hold values from -6 to 6
Outputs:
- result: bfloat16 [48, 2048, 768], P('dp', None, 'mp')
- tokens_grad: bfloat16 [48, 2048, 768], P('dp', None, 'mp')
- attention_grad: float32 [3, 768, 768], P(None, 'dp', 'mp')
- mixing_grad: float32 [768, 768], P('mp', 'dp')
- expand_grad: float32 [768, 3072], P('dp', 'mp')
- contract_grad: float32 [3072, 768], P('mp', 'dp')
- prenorm_grad: float32 [768], P('dp')
- midnorm_grad: float32 [768], P('dp')
- router_grad: float32 [768], P('dp')
Inputs may be any that keep to these rules, and one draw needn't show every extreme that they name: `chosen`: in each row the 256 entries are distinct positions in increasing order.
All inputs are finite; a program needn't handle non-finite values. No bound on the sum of `present` on one device may be relied on, other than what follows from the above.
Results may differ from a plain program's by a relative error of at most 0.017.
Values may be sent and summed in bfloat16 or wider, within the bound.
No kernel may reach another device: no remote copies, remote signals or barrier semaphores. Data moves between devices by JAX's collectives and lax.ppermute only.
A program may use at most 192 MiB of HBM per device.

v0:
```python
import jax
import jax.numpy as jnp
from jax import lax
from jax.sharding import PartitionSpec as P

HD = 64


EPSILON = 1e-06


def normalize(values, scales):
    return values * lax.rsqrt(jnp.mean(values * values, axis=-1, keepdims=True) + EPSILON) * scales


def gelu_tanh(values):
    return jax.nn.gelu(values, approximate=True)


def allowed_pairs(seg_rows, keep_rows):
    length = seg_rows.shape[-1]
    slot_ids = jnp.arange(length)
    diagonal = slot_ids[None, :] == slot_ids[:, None]
    causal = slot_ids[None, :] <= slot_ids[:, None]
    same_doc = seg_rows[:, :, None] == seg_rows[:, None, :]
    open_key = (keep_rows[:, None, :] > 0) | diagonal[None]
    return (causal[None] & same_doc & open_key)[:, None]


def shards(
    tokens,
    segments,
    present,
    chosen,
    attention,
    mixing,
    expand,
    contract,
    prenorm,
    midnorm,
    router,
    cotangent,
):
    full_in, full_mix, full_up, full_down, pre_gain, mid_gain, full_router = (
        lax.all_gather(attention, "dp", axis=1, tiled=True),
        lax.all_gather(mixing, "dp", axis=1, tiled=True),
        lax.all_gather(expand, "dp", axis=0, tiled=True),
        lax.all_gather(contract, "dp", axis=1, tiled=True),
        lax.all_gather(prenorm, "dp", axis=0, tiled=True),
        lax.all_gather(midnorm, "dp", axis=0, tiled=True),
        lax.all_gather(router, "dp", axis=0, tiled=True),
    )
    row_count, length, half_width = tokens.shape
    sel_count = chosen.shape[1]
    token_count = row_count * sel_count
    row_ids = jnp.arange(row_count)[:, None]
    local_rows = tokens[row_ids, chosen]
    local_grads = cotangent[row_ids, chosen]
    states_b, upstream_b = (
        lax.all_gather(local_rows, "mp", axis=2, tiled=True),
        lax.all_gather(local_grads, "mp", axis=2, tiled=True),
    )
    width = states_b.shape[2]
    states_flat = states_b.reshape(token_count, width)
    states = states_flat.astype(jnp.float32)
    upstream = upstream_b.reshape(token_count, width).astype(jnp.float32)
    seg_sel = jnp.take_along_axis(segments, chosen, axis=1)
    keep_sel = jnp.take_along_axis(present, chosen, axis=1).astype(jnp.float32)
    keep_flat = keep_sel.reshape(token_count)
    permitted = allowed_pairs(seg_sel, keep_sel)
    heads_here = half_width // HD
    scale = HD ** (-0.5)
    pre_scale = pre_gain.astype(jnp.float32)
    mid_scale = mid_gain.astype(jnp.float32)
    router_vec = full_router.astype(jnp.float32)
    normed = normalize(states, pre_scale).astype(jnp.bfloat16)
    packed = jnp.einsum("td,cde->cte", normed, full_in, preferred_element_type=jnp.float32).astype(
        jnp.bfloat16
    )
    shaped = packed.reshape(3, row_count, sel_count, heads_here, HD)
    queries, key_rows, val_rows = (shaped[0], shaped[1], shaped[2])
    scores = (
        jnp.einsum("bqhd,bkhd->bhqk", queries, key_rows, preferred_element_type=jnp.float32) * scale
    )
    scores = jnp.where(permitted, scores, -1e30)
    row_max = jnp.max(scores, axis=-1, keepdims=True)
    exponent = jnp.exp(scores - row_max)
    totals = jnp.sum(exponent, axis=-1, keepdims=True)
    log_norm = row_max + jnp.log(totals)
    attn_weights = (exponent / totals).astype(jnp.bfloat16)
    context = jnp.einsum(
        "bhqk,bkhd->bqhd", attn_weights, val_rows, preferred_element_type=jnp.float32
    )
    context = context.astype(jnp.bfloat16).reshape(token_count, half_width)
    attended = lax.psum(jnp.dot(context, full_mix, preferred_element_type=jnp.float32), "mp")
    middle = states + attended
    normed_mid = normalize(middle, mid_scale).astype(jnp.bfloat16)
    hidden = jnp.dot(normed_mid, full_up, preferred_element_type=jnp.float32)
    activated = gelu_tanh(hidden).astype(jnp.bfloat16)
    feedfwd = lax.psum(
        jnp.dot(activated, full_down, preferred_element_type=jnp.float32).astype(jnp.bfloat16), "mp"
    ).astype(jnp.float32)
    branch = attended + feedfwd
    logits = jnp.dot(states_flat, full_router, preferred_element_type=jnp.float32)
    router_prob = jax.nn.sigmoid(logits)
    gate_value = router_prob * keep_flat
    finished = states + gate_value[:, None] * branch
    offset = lax.axis_index("mp") * half_width
    own_part = lax.dynamic_slice_in_dim(finished, offset, half_width, 1)
    result = tokens.at[row_ids, chosen].set(
        own_part.reshape(row_count, sel_count, half_width).astype(jnp.bfloat16)
    )
    back_in, back_mix, back_up, back_down = (
        lax.all_gather(attention, "dp", axis=1, tiled=True),
        lax.all_gather(mixing, "dp", axis=1, tiled=True),
        lax.all_gather(expand, "dp", axis=0, tiled=True),
        lax.all_gather(contract, "dp", axis=1, tiled=True),
    )
    gate_grad = jnp.sum(upstream * branch, axis=-1)
    logit_grad = gate_grad * keep_flat * router_prob * (1.0 - router_prob)
    router_grad = jnp.sum(logit_grad[:, None] * states, axis=0)
    branch_grad = gate_value[:, None] * upstream
    feed_grad = branch_grad.astype(jnp.bfloat16)
    act_grad = jnp.einsum("te,fe->tf", feed_grad, back_down, preferred_element_type=jnp.float32)
    _, gelu_pull = jax.vjp(gelu_tanh, hidden)
    hidden_grad = gelu_pull(act_grad)[0].astype(jnp.bfloat16)
    contract_grad = jnp.einsum(
        "tf,te->fe", activated, feed_grad, preferred_element_type=jnp.float32
    )
    expand_grad = jnp.einsum(
        "td,tf->df", normed_mid, hidden_grad, preferred_element_type=jnp.float32
    )
    mid_in_grad = lax.psum(
        jnp.einsum("tf,df->td", hidden_grad, back_up, preferred_element_type=jnp.float32).astype(
            jnp.bfloat16
        ),
        "mp",
    ).astype(jnp.float32)
    _, mid_pull = jax.vjp(normalize, middle, mid_scale)
    middle_grad, midnorm_grad = mid_pull(mid_in_grad)
    mixed_grad = (branch_grad + middle_grad).astype(jnp.bfloat16)
    mixing_grad = jnp.einsum("ti,te->ie", context, mixed_grad, preferred_element_type=jnp.float32)
    context_grad = jnp.einsum("te,ie->ti", mixed_grad, back_mix, preferred_element_type=jnp.float32)
    context_grad = context_grad.astype(jnp.bfloat16).reshape(row_count, sel_count, heads_here, HD)
    again_scores = (
        jnp.einsum("bqhd,bkhd->bhqk", queries, key_rows, preferred_element_type=jnp.float32) * scale
    )
    again_scores = jnp.where(permitted, again_scores, -1e30)
    attn_probs = jnp.exp(again_scores - log_norm)
    probs_low = attn_probs.astype(jnp.bfloat16)
    prob_grad = jnp.einsum(
        "bqhd,bkhd->bhqk", context_grad, val_rows, preferred_element_type=jnp.float32
    )
    centre = jnp.sum(attn_probs * prob_grad, axis=-1, keepdims=True)
    score_grad = (attn_probs * (prob_grad - centre)).astype(jnp.bfloat16)
    query_grad = (
        jnp.einsum("bhqk,bkhd->bqhd", score_grad, key_rows, preferred_element_type=jnp.float32)
        * scale
    ).astype(jnp.bfloat16)
    key_grad = (
        jnp.einsum("bhqk,bqhd->bkhd", score_grad, queries, preferred_element_type=jnp.float32)
        * scale
    ).astype(jnp.bfloat16)
    value_grad = jnp.einsum(
        "bhqk,bqhd->bkhd", probs_low, context_grad, preferred_element_type=jnp.float32
    ).astype(jnp.bfloat16)
    packed_grad = jnp.stack([query_grad, key_grad, value_grad]).reshape(3, token_count, half_width)
    attention_grad = jnp.einsum(
        "td,cte->cde", normed, packed_grad, preferred_element_type=jnp.float32
    )
    pre_in_grad = lax.psum(
        jnp.einsum("cte,cde->td", packed_grad, back_in, preferred_element_type=jnp.float32).astype(
            jnp.bfloat16
        ),
        "mp",
    ).astype(jnp.float32)
    _, pre_pull = jax.vjp(normalize, states, pre_scale)
    states_grad, prenorm_grad = pre_pull(pre_in_grad)
    total_grad = upstream + logit_grad[:, None] * router_vec + middle_grad + states_grad
    own_grad = lax.dynamic_slice_in_dim(total_grad, offset, half_width, 1)
    tokens_grad = cotangent.at[row_ids, chosen].set(
        own_grad.reshape(row_count, sel_count, half_width).astype(jnp.bfloat16)
    )
    attention_out, mixing_out, expand_out, contract_out, prenorm_out, midnorm_out, router_out = (
        lax.psum_scatter(attention_grad, "dp", scatter_dimension=1, tiled=True),
        lax.psum_scatter(mixing_grad, "dp", scatter_dimension=1, tiled=True),
        lax.psum_scatter(expand_grad, "dp", scatter_dimension=0, tiled=True),
        lax.psum_scatter(contract_grad, "dp", scatter_dimension=1, tiled=True),
        lax.psum_scatter(prenorm_grad, "dp", scatter_dimension=0, tiled=True),
        lax.psum_scatter(midnorm_grad, "dp", scatter_dimension=0, tiled=True),
        lax.psum_scatter(router_grad, "dp", scatter_dimension=0, tiled=True),
    )
    return (
        result,
        tokens_grad,
        attention_out,
        mixing_out,
        expand_out,
        contract_out,
        prenorm_out,
        midnorm_out,
        router_out,
    )


def solution(mesh):
    in_specs = (
        P("dp", None, "mp"),
        P("dp", None),
        P("dp", None),
        P("dp", None),
        P(None, "dp", "mp"),
        P("mp", "dp"),
        P("dp", "mp"),
        P("mp", "dp"),
        P("dp"),
        P("dp"),
        P("dp"),
        P("dp", None, "mp"),
    )
    out_specs = (
        P("dp", None, "mp"),
        P("dp", None, "mp"),
        P(None, "dp", "mp"),
        P("mp", "dp"),
        P("dp", "mp"),
        P("mp", "dp"),
        P("dp"),
        P("dp"),
        P("dp"),
    )
    return jax.shard_map(shards, mesh=mesh, in_specs=in_specs, out_specs=out_specs, check_vma=False)
```

profile of v0, /device:TPU:0, one launch (start us, length us, event | category | flops | bytes accessed | tf_op | source)
XLA Modules:
  0.0 978.4 jit_solution(425545685463876873)
XLA Ops:
  7.2 5.1 copy.120
  14.6 9.8 %gather_fusion = bf16[768,384]{1,0:T(8,128)(2,1)} fusion(bf16[3,2048,384]{2,1,0:T(8,128)(2,1)} %copy.120, s32[768]{0:T(1024)S(1)} %reshape.177), kind=kCustom, calls=%fused_computation.2 | custom fusion | bytes 1185792 | tf_op jit(solution)/shard_map/gather | solution.py:57
  25.3 10.0 %gather_fusion.1 = bf16[768,384]{1,0:T(8,128)(2,1)} fusion(bf16[3,2048,384]{2,1,0:T(8,128)(2,1)} %copy.121, s32[768]{0:T(1024)S(1)} %reshape.177), kind=kCustom, calls=%fused_computation.3 | custom fusion | bytes 1185792 | tf_op jit(solution)/shard_map/gather | solution.py:58
  38.0 44.3 %all-reduce.8 = (bf16[768]{0:T(1024)(128)(2,1)S(1)}, bf16[768]{0:T(1024)(128)(2,1)S(1)}, bf16[768]{0:T(1024)(128)(2,1)S(1)}) all-reduce(bf16[768]{0:T(1024)(128)(2,1)S(1)} %dynamic-update-slice, bf16[768]{0:T(1024)(128)(2,1)S(1)} %dynamic-update-slice.1, bf16[768]{0:T(1024)(128)(2,1)S(1)} %dynamic-update-slice.2), channel_id=1, replica_groups=mesh['dp'=16,'mp'=2] {'dp'}, use_global_device_ids=true, to_apply=%add | all-reduce | flops 2304 | bytes 9216
  82.3 6.7 gather_fusion.2
  89.0 6.7 gather_fusion.3
  96.1 41.8 %all_gather.35 = bf16[384,768]{0,1:T(8,128)(2,1)} all-gather(bf16[384,48]{0,1:T(8,128)(2,1)S(1)} %copy-done.22), channel_id=1, replica_groups=mesh['dp'=16,'mp'=2] {'dp'}, dimensions={1}, use_global_device_ids=true | all-gather | bytes 626688 | tf_op jit(solution)/shard_map/all_gather | solution.py:46
  139.6 3.6 convert_bitcast_fusion
  161.7 14.2 %all-gather.12.cloned.1.call-done = bf16[1536,768]{0,1:T(8,128)(2,1)} async-done(((bf16[1536,48]{0,1:T(8,128)(2,1)}), bf16[1536,768]{0,1:T(8,128)(2,1)}) %all-gather.12.cloned.1.call-update) | async-done | bytes 2359312 | tf_op jit(solution)/shard_map/all_gather | solution.py:48
  176.0 5.9 fusion.53
  181.8 16.8 %all-reduce.15.cloned.1.call-done = f32[768,768]{1,0:T(8,128)} async-done(((f32[768,768]{1,0:T(8,128)}), f32[768,768]{1,0:T(8,128)}) %all-reduce.15.cloned.1.call-update) | async-done | bytes 2359312 | tf_op jit(solution)/shard_map/psum | solution.py:95
  198.6 3.4 multiply_reduce_fusion.3
  202.0 63.2 %all-gather.10.cloned.1.call-done = bf16[768,1536]{1,0:T(8,128)(2,1)} async-done(((bf16[48,1536]{1,0:T(8,128)(2,1)}), bf16[768,1536]{1,0:T(8,128)(2,1)}) %all-gather.10.cloned.1.call-update) | async-done | bytes 2359312 | tf_op jit(solution)/shard_map/all_gather | solution.py:47
  265.1 10.5 %fusion.6 = (bf16[768,1536]{1,0:T(8,128)(2,1)S(1)}, f32[768,1536]{1,0:T(8,128)}) fusion(f32[768,1536]{1,0:T(8,128)} %fusion.53, bf16[768,1536]{1,0:T(8,128)(2,1)} %all-gather.10.cloned.1.call-done, f32[768,768]{1,0:T(8,128)} %get-tuple-element.54, f32[768]{0:T(1024)S(1)} %convert_element_type.125, f32[768]{0:T(1024)S(1)} %fusion.44), kind=kOutput, calls=%fused_computation.14 | convolution fusion | flops 1837301760 | bytes 16521216 | tf_op jit(solution)/shard_map/dot_general | solution.py:98
  280.2 7.0 convolution_convert_fusion.1
  287.2 11.7 %all-reduce.17.cloned.1.call-done = bf16[768,768]{1,0:T(8,128)(2,1)} async-done(((bf16[768,768]{1,0:T(8,128)(2,1)}), bf16[768,768]{1,0:T(8,128)(2,1)}) %all-reduce.17.cloned.1.call-update) | async-done | bytes 1179664 | tf_op jit(solution)/shard_map/psum | solution.py:133
  302.0 3.6 add_convert_fusion
  313.8 4.3 fusion.29
  318.1 3.5 multiply_reduce_fusion
  348.9 4.9 convolution_bitcast_fusion
  353.8 6.4 copy.84
  364.7 6.8 fusion.46
  371.7 7.0 fusion.48
  382.8 3.9 multiply_reduce_fusion.2
  387.1 3.9 fusion.15
  390.9 79.2 %all-reduce.7 = (f32[768]{0:T(1024)S(1)}, f32[768]{0:T(1024)S(1)}, f32[768]{0:T(1024)S(1)}) all-reduce(f32[768]{0:T(1024)S(1)} %get-tuple-element.39, f32[768]{0:T(1024)S(1)} %get-tuple-element.37, f32[768]{0:T(1024)S(1)} %fusion.13), channel_id=6, replica_groups=mesh['dp'=16,'mp'=2] {'dp'}, use_global_device_ids=true, to_apply=%region_19.21.clone | all-reduce | flops 2304 | bytes 18432
  471.9 3.3 fusion.33
  475.3 92.7 %scatter_fusion.1 = bf16[3,2048,384]{2,1,0:T(8,128)(2,1)} fusion(bf16[3,2048,384]{2,1,0:T(8,128)(2,1)} %copy.121, s32[768]{0:T(1024)S(1)} %reshape.189, bf16[768,384]{1,0:T(8,128)(2,1)S(1)} %get-tuple-element.57), kind=kCustom, calls=%fused_computation.5 | custom fusion | bytes 1775616 | tf_op jit(solution)/shard_map/scatter | solution.py:181
  568.0 92.5 %scatter_fusion = bf16[3,2048,384]{2,1,0:T(8,128)(2,1)} fusion(bf16[3,2048,384]{2,1,0:T(8,128)(2,1)} %copy.120, s32[768]{0:T(1024)S(1)} %reshape.189, bf16[768,384]{1,0:T(8,128)(2,1)S(1)} %get-tuple-element.58), kind=kCustom, calls=%fused_computation.4 | custom fusion | bytes 1775616 | tf_op jit(solution)/shard_map/scatter | solution.py:110
  662.2 25.9 %reduce-scatter.4.cloned.1.call-done = f32[384,48]{0,1:T(8,128)} async-done(((f32[384,768]{0,1:T(8,128)}), f32[384,48]{0,1:T(8,128)}) %reduce-scatter.4.cloned.1.call-update) | async-done | bytes 73744 | tf_op jit(solution)/shard_map/reduce_scatter | solution.py:186
  688.1 141.2 %reduce-scatter.6.cloned.1.call-done = f32[48,1536]{1,0:T(8,128)} async-done(((f32[768,1536]{1,0:T(8,128)}), f32[48,1536]{1,0:T(8,128)}) %reduce-scatter.6.cloned.1.call-update) | async-done | bytes 294928 | tf_op jit(solution)/shard_map/reduce_scatter | solution.py:187
  829.3 141.8 %reduce-scatter.8.cloned.1.call-done = f32[1536,48]{0,1:T(8,128)} async-done(((f32[1536,768]{0,1:T(8,128)}), f32[1536,48]{0,1:T(8,128)}) %reduce-scatter.8.cloned.1.call-update) | async-done | bytes 294928 | tf_op jit(solution)/shard_map/reduce_scatter | solution.py:188
  (172 shorter events, 80.1 us)
Async XLA Ops:
  7.2 75.1 %copy-start = (s32[3,2048]{1,0:T(4,128)S(1)}, s32[3,2048]{1,0:T(4,128)}, u32[]{:S(2)}) copy-start(s32[3,2048]{1,0:T(4,128)} %param.16) | copy-start | bytes 73732
  7.2 130.8 %all-gather.6.cloned.1.call-start = ((), (), s32[]{:S(2)}) async-start(), calls=%async_computation.3 | async-start | bytes 1769472 | tf_op jit(solution)/shard_map/all_gather | solution.py:60
  7.2 5.2 copy-start.12
  24.5 115.1 %all-gather.8.cloned.1.call-start = ((), (), s32[]{:S(2)}) async-start(), calls=%async_computation.4 | async-start | bytes 1880064 | tf_op jit(solution)/shard_map/all_gather | solution.py:45
  25.2 10.7 %copy-start.24 = (u32[32]{0:T(128)S(1)}, u32[32]{0:T(128)}, u32[]{:S(2)}) copy-start(u32[32]{0:T(128)} %constant.150) | copy-start | bytes 388
  25.2 12.0 %copy-start.27 = (bf16[48]{0:T(256)(128)(2,1)S(1)}, bf16[48]{0:T(256)(128)(2,1)}, u32[]{:S(2)}) copy-start(bf16[48]{0:T(256)(128)(2,1)} %param.24) | copy-start | bytes 292
  25.3 12.2 %copy-start.28 = (bf16[48]{0:T(256)(128)(2,1)S(1)}, bf16[48]{0:T(256)(128)(2,1)}, u32[]{:S(2)}) copy-start(bf16[48]{0:T(256)(128)(2,1)} %param.22) | copy-start | bytes 292
  25.3 12.5 %copy-start.29 = (bf16[48]{0:T(256)(128)(2,1)S(1)}, bf16[48]{0:T(256)(128)(2,1)}, u32[]{:S(2)}) copy-start(bf16[48]{0:T(256)(128)(2,1)} %param.23) | copy-start | bytes 292
  25.3 134.9 %all-gather.14.cloned.1.call-start = ((), (), s32[]{:S(2)}) async-start(), calls=%async_computation.8 | async-start | bytes 1769472 | tf_op jit(solution)/shard_map/all_gather | solution.py:61
  35.3 140.6 %all-gather.12.cloned.1.call-start = ((), (), s32[]{:S(2)}) async-start(), calls=%async_computation.7 | async-start | bytes 2506752 | tf_op jit(solution)/shard_map/all_gather | solution.py:48
  35.9 53.1 %copy-start.2 = (s32[3,2048]{1,0:T(4,128)S(1)}, s32[3,2048]{1,0:T(4,128)}, u32[]{:S(2)}) copy-start(s32[3,2048]{1,0:T(4,128)} %param.15) | copy-start | bytes 73732
  35.9 162.7 %all-reduce.15.cloned.1.call-start = ((), (), s32[]{:S(2)}) async-start(), calls=%async_computation.5 | async-start | bytes 4718592 | tf_op jit(solution)/shard_map/psum | solution.py:95
  89.0 7.1 copy-start.22
  146.0 5.5 copy-start.7
  158.8 106.3 %all-gather.10.cloned.1.call-start = ((), (), s32[]{:S(2)}) async-start(), calls=%async_computation.6 | async-start | bytes 2506752 | tf_op jit(solution)/shard_map/all_gather | solution.py:47
  159.4 139.5 %all-reduce.17.cloned.1.call-start = ((), (), s32[]{:S(2)}) async-start(), calls=%async_computation.9 | async-start | bytes 2359296 | tf_op jit(solution)/shard_map/psum | solution.py:133
  161.7 20.1 %copy-start.20 = (bf16[768,768]{1,0:T(8,128)(2,1)}, bf16[768,768]{1,0:T(8,128)(2,1)S(1)}, u32[]{:S(2)}) copy-start(bf16[768,768]{1,0:T(8,128)(2,1)S(1)} %multiply_convert_fusion.4) | copy-start | bytes 3538948
  265.1 11.9 %copy-start.25 = (bf16[768,1536]{1,0:T(8,128)(2,1)S(1)}, bf16[768,1536]{1,0:T(8,128)(2,1)}, u32[]{:S(2)}) copy-start(bf16[768,1536]{1,0:T(8,128)(2,1)} %all-gather.10.cloned.1.call-done) | copy-start | bytes 7077892
  280.1 102.7 %all-reduce.21.cloned.1.call-start = ((), (), s32[]{:S(2)}) async-start(), calls=%async_computation.14 | async-start | bytes 4718592 | tf_op jit(solution)/shard_map/psum | solution.py:100
  287.2 14.8 %copy-start.6 = (bf16[3,256,768]{2,1,0:T(8,128)(2,1)S(1)}, bf16[3,256,768]{2,1,0:T(8,128)(2,1)}, u32[]{:S(2)}) copy-start(bf16[3,256,768]{2,1,0:T(8,128)(2,1)} %all-gather.14.cloned.1.call-done) | copy-start | bytes 3538948
  302.0 4.6 copy-start.16
  313.8 4.3 copy-start.11
  313.8 4.3 copy-start.19
  313.8 7.8 slice-start
  331.5 5.8 copy-start.14
  339.1 5.6 copy-start.17
  342.2 3.8 copy-start.26
  348.9 311.6 %all-reduce.19.cloned.1.call-start = ((), (), s32[]{:S(2)}) async-start(), calls=%async_computation.13 | async-start | bytes 9437184
  360.3 327.9 %reduce-scatter.4.cloned.1.call-start = ((), (), s32[]{:S(2)}) async-start(), calls=%async_computation.10 | async-start | bytes 1253376 | tf_op jit(solution)/shard_map/reduce_scatter | solution.py:186
  364.4 464.8 %reduce-scatter.6.cloned.1.call-start = ((), (), s32[]{:S(2)}) async-start(), calls=%async_computation.11 | async-start | bytes 5013504 | tf_op jit(solution)/shard_map/reduce_scatter | solution.py:187
  371.6 599.5 %reduce-scatter.8.cloned.1.call-start = ((), (), s32[]{:S(2)}) async-start(), calls=%async_computation.12 | async-start | bytes 5013504 | tf_op jit(solution)/shard_map/reduce_scatter | solution.py:188
  568.0 403.2 %copy-start.1 = (s32[3,2048]{1,0:T(4,128)S(1)}, s32[3,2048]{1,0:T(4,128)}, u32[]{:S(2)}) copy-start(s32[3,2048]{1,0:T(4,128)} %param.16) | copy-start | bytes 73732
  (13 other events, 25.8 us)
Sparse Core Ops, SparseCore 0:
  24.6 11.8 all-gather.5
  39.2 62.2 all-gather.7
  103.0 6.6 all-gather.13
  112.4 63.5 all-gather.11
  178.1 20.4 all-reduce.14
  201.6 63.4 all-gather.9
  280.2 18.5 all-reduce.16
  349.0 22.8 all-reduce.20
  378.6 181.6 all-reduce.18
  565.5 122.6 reduce-scatter.3
  693.9 135.3 reduce-scatter.5
  835.7 135.3 reduce-scatter.7
where the time goes:
time: 990 us; the launch traced here: 978 us
  waiting for transfers between devices  417 us (42%)
  local copies, waits for them, and re-layouts  277 us (28%)
  blocking collectives  165 us (17%)
  matrix products  71.7 us (7%)
  other arithmetic  30.1 us (3%)
  between operations  16.6 us (2%)
    reduce_scatter x1, waiting for transfers between devices, shards(): lax.psum_scatter(contract_grad, 'dp', scatter_dimension=1, tiled=True)  142 us
    reduce_scatter x1, waiting for transfers between devices, shards(): lax.psum_scatter(expand_grad, 'dp', scatter_dimension=0, tiled=True)  141 us
    unnamed x2, blocking collectives  124 us
    scatter x1, local copies, waits for them, and re-layouts, shards(): cotangent.at[row_ids, chosen]  92.7 us
    scatter x1, local copies, waits for them, and re-layouts, shards(): tokens.at[row_ids, chosen]  92.5 us
    all_gather x1, waiting for transfers between devices, shards(): lax.all_gather(expand, 'dp', axis=0, tiled=True)  63.2 us
    all_gather x1, blocking collectives, shards(): lax.all_gather(mixing, 'dp', axis=1, tiled=True)  41.8 us
    reduce_scatter x1, waiting for transfers between devices, shards(): lax.psum_scatter(mixing_grad, 'dp', scatter_dimension=1, tiled=True)  25.9 us
  transfers between devices with their start and end apart: 12, of which 7 were waited for; matrix products, arithmetic and copies ran while one was open for 30% of the time, Pallas kernels for 0%

commit v1 on v0

v1 whole, which is shorter than its diff:
```python
import jax
import jax.numpy as jnp
from jax import lax
from jax.sharding import PartitionSpec as P

HD = 64
EPSILON = 1e-06
BF = jnp.bfloat16
F32 = jnp.float32


def normalize(values, scales):
    return values * lax.rsqrt(jnp.mean(values * values, axis=-1, keepdims=True) + EPSILON) * scales


def gelu_tanh(values):
    return jax.nn.gelu(values, approximate=True)


def allowed_pairs(seg_rows, keep_rows):
    length = seg_rows.shape[-1]
    slot_ids = jnp.arange(length)
    diagonal = slot_ids[None, :] == slot_ids[:, None]
    causal = slot_ids[None, :] <= slot_ids[:, None]
    same_doc = seg_rows[:, :, None] == seg_rows[:, None, :]
    open_key = (keep_rows[:, None, :] > 0) | diagonal[None]
    return (causal[None] & same_doc & open_key)[:, None]


class Line:
    def __init__(self, count, stride, size):
        self.count, self.stride, self.size = count, stride, size
        self.pos = (lax.axis_index("dp") // stride) % size

    def pairs(self, step):
        return [
            (i, i + step * self.stride)
            for i in range(self.count)
            if 0 <= (i // self.stride) % self.size + step < self.size
        ]

    def swap(self, value):
        return lax.ppermute(value, "dp", self.pairs(1) + self.pairs(-1))

    def gather(self, own):
        if self.size == 1:
            return own[None]
        if self.size == 2:
            other = self.swap(own)
            first = self.pos == 0
            return jnp.stack([jnp.where(first, own, other), jnp.where(first, other, own)])
        lower, upper, right, left = [], [], own, own
        for _ in range(self.size - 1):
            right = lax.ppermute(right, "dp", self.pairs(1))
            left = lax.ppermute(left, "dp", self.pairs(-1))
            lower.insert(0, right)
            upper.append(left)
        stack = jnp.stack(lower + [own] + upper)
        return lax.dynamic_slice_in_dim(stack, self.size - 1 - self.pos, self.size, 0)

    def scatter(self, value):
        def at(index):
            return lax.dynamic_index_in_dim(value, index, 0, keepdims=False)

        mine = at(self.pos)
        if self.size == 1:
            return mine
        if self.size == 2:
            return mine + self.swap(at(1 - self.pos).astype(BF)).astype(F32)
        right = left = None
        for away in range(self.size - 1, 0, -1):
            to_right = at(jnp.minimum(self.pos + away, self.size - 1))
            to_left = at(jnp.maximum(self.pos - away, 0))
            if right is not None:
                to_right = to_right + right
                to_left = to_left + left
            right = lax.ppermute(to_right.astype(BF), "dp", self.pairs(1)).astype(F32)
            left = lax.ppermute(to_left.astype(BF), "dp", self.pairs(-1)).astype(F32)
        return mine + right + left


def lines_of(count):
    bits = count.bit_length() - 1
    short = 2 ** (bits // 3) if count == 2**bits else 1
    return (
        Line(count, short * short, count // (short * short)),
        Line(count, short, short),
        Line(count, 1, short),
    )


def halves(width):
    return width // 2 // 128 * 128


def gather_weights(lines, own):
    along_z, along_y, along_x = lines
    rows, width = own.shape
    cut = halves(width)
    column = along_z.gather(own)
    first = along_y.gather(along_x.gather(column[..., :cut]))
    second = along_x.gather(along_y.gather(column[..., cut:]))
    first = first.transpose(2, 0, 1, 3, 4).reshape(-1, cut)
    second = second.transpose(2, 1, 0, 3, 4).reshape(-1, width - cut)
    return jnp.concatenate([first, second], axis=1)


def scatter_grads(lines, total):
    along_z, along_y, along_x = lines
    width = total.shape[1]
    cut = halves(width)
    view = total.reshape(along_z.size, along_y.size, along_x.size, -1, width)
    first = along_x.scatter(along_y.scatter(view[..., :cut].transpose(1, 2, 0, 3, 4)))
    second = along_y.scatter(along_x.scatter(view[..., cut:].transpose(2, 1, 0, 3, 4)))
    return along_z.scatter(jnp.concatenate([first, second], axis=-1))


def other_core(value):
    return lax.ppermute(value, "mp", [(0, 1), (1, 0)])


def both_halves(value):
    other = other_core(value)
    low = lax.axis_index("mp") == 0
    return jnp.concatenate([jnp.where(low, value, other), jnp.where(low, other, value)], axis=-1)


def add_cores(value):
    low = value.astype(BF)
    return low.astype(F32) + other_core(low).astype(F32)


def dot(a, b, contract, out=F32):
    return lax.dot_general(a, b, ((contract[:1], contract[1:]), ((), ())), preferred_element_type=F32).astype(out)


def shards(
    tokens,
    segments,
    present,
    chosen,
    attention,
    mixing,
    expand,
    contract,
    prenorm,
    midnorm,
    router,
    cotangent,
    count,
):
    lines = lines_of(count)
    row_count, length, half_width = tokens.shape
    sel_count = chosen.shape[1]
    token_count = row_count * sel_count
    own_rows = mixing.shape[1]
    hidden_here = expand.shape[1]
    heads_here = half_width // HD
    scale = HD ** (-0.5)

    vectors = jnp.stack([prenorm, midnorm, router], axis=1)
    vectors = jnp.pad(vectors, ((0, 0), (0, 125)))
    first_own = jnp.concatenate(
        [attention[0], attention[1], attention[2], mixing.T, vectors], axis=1
    )
    first = gather_weights(lines, first_own)
    full_up = gather_weights(lines, expand)
    full_down = gather_weights(lines, contract.T)
    full_in = first[:, : 3 * half_width]
    full_mix = first[:, 3 * half_width : 4 * half_width]
    gains = first[:, 4 * half_width : 4 * half_width + 3].astype(F32)
    pre_scale, mid_scale, router_vec = gains[:, 0], gains[:, 1], gains[:, 2]

    positions = jnp.arange(length, dtype=jnp.int32)
    hit = chosen[:, :, None] == positions[None, None, :]
    one_hot = hit.astype(BF)
    local_rows = jnp.einsum("bts,bsd->btd", one_hot, tokens, preferred_element_type=F32).astype(BF)
    local_grads = jnp.einsum("bts,bsd->btd", one_hot, cotangent, preferred_element_type=F32).astype(BF)
    seg_sel = jnp.sum(jnp.where(hit, segments[:, None, :], 0), axis=-1)
    keep_sel = jnp.sum(jnp.where(hit, present[:, None, :], 0), axis=-1).astype(F32)

    both = both_halves(jnp.stack([local_rows, local_grads]))
    states_flat = both[0].reshape(token_count, -1)
    states = states_flat.astype(F32)
    upstream = both[1].reshape(token_count, -1).astype(F32)
    keep_flat = keep_sel.reshape(token_count)
    permitted = allowed_pairs(seg_sel, keep_sel)

    normed = normalize(states, pre_scale).astype(BF)
    packed = dot(normed, full_in, (1, 0), BF)
    shaped = packed.reshape(row_count, sel_count, 3, heads_here, HD)
    queries, key_rows, val_rows = (shaped[:, :, 0], shaped[:, :, 1], shaped[:, :, 2])
    scores = jnp.einsum("bqhd,bkhd->bhqk", queries, key_rows, preferred_element_type=F32) * scale
    scores = jnp.where(permitted, scores, -1e30)
    row_max = jnp.max(scores, axis=-1, keepdims=True)
    exponent = jnp.exp(scores - row_max)
    attn_probs = exponent / jnp.sum(exponent, axis=-1, keepdims=True)
    attn_weights = attn_probs.astype(BF)
    context = jnp.einsum("bhqk,bkhd->bqhd", attn_weights, val_rows, preferred_element_type=F32)
    context = context.astype(BF).reshape(token_count, half_width)
    attended = add_cores(dot(context, full_mix, (1, 1)))
    middle = states + attended
    normed_mid = normalize(middle, mid_scale).astype(BF)
    hidden = dot(normed_mid, full_up, (1, 0))
    activated = gelu_tanh(hidden).astype(BF)
    feedfwd = add_cores(dot(activated, full_down, (1, 1)))
    branch = attended + feedfwd
    router_prob = jax.nn.sigmoid(jnp.sum(states * router_vec, axis=-1))
    gate_value = router_prob * keep_flat
    finished = states + gate_value[:, None] * branch

    gate_grad = jnp.sum(upstream * branch, axis=-1)
    logit_grad = gate_grad * keep_flat * router_prob * (1.0 - router_prob)
    router_grad = jnp.sum(logit_grad[:, None] * states, axis=0)
    branch_grad = gate_value[:, None] * upstream
    feed_grad = branch_grad.astype(BF)
    down_out = scatter_grads(lines, dot(feed_grad, activated, (0, 0)))
    act_grad = dot(feed_grad, full_down, (1, 0))
    _, gelu_pull = jax.vjp(gelu_tanh, hidden)
    hidden_grad = gelu_pull(act_grad)[0].astype(BF)
    up_out = scatter_grads(lines, dot(normed_mid, hidden_grad, (0, 0)))
    mid_in_grad = add_cores(dot(hidden_grad, full_up, (1, 1)))
    _, mid_pull = jax.vjp(normalize, middle, mid_scale)
    middle_grad, midnorm_grad = mid_pull(mid_in_grad)
    mixed_grad = (branch_grad + middle_grad).astype(BF)
    mixing_grad = dot(mixed_grad, context, (0, 0))
    context_grad = dot(mixed_grad, full_mix, (1, 0), BF)
    context_grad = context_grad.reshape(row_count, sel_count, heads_here, HD)
    prob_grad = jnp.einsum("bqhd,bkhd->bhqk", context_grad, val_rows, preferred_element_type=F32)
    centre = jnp.sum(attn_probs * prob_grad, axis=-1, keepdims=True)
    score_grad = (attn_probs * (prob_grad - centre)).astype(BF)
    query_grad = jnp.einsum("bhqk,bkhd->bqhd", score_grad, key_rows, preferred_element_type=F32) * scale
    key_grad = jnp.einsum("bhqk,bqhd->bkhd", score_grad, queries, preferred_element_type=F32) * scale
    value_grad = jnp.einsum("bhqk,bqhd->bkhd", attn_weights, context_grad, preferred_element_type=F32)
    packed_grad = jnp.concatenate(
        [v.astype(BF).reshape(token_count, half_width) for v in (query_grad, key_grad, value_grad)],
        axis=1,
    )
    attention_grad = dot(normed, packed_grad, (0, 0))
    pre_in_grad = add_cores(dot(packed_grad, full_in, (1, 1)))
    _, pre_pull = jax.vjp(normalize, states, pre_scale)
    states_grad, prenorm_grad = pre_pull(pre_in_grad)
    total_grad = upstream + logit_grad[:, None] * router_vec + middle_grad + states_grad

    vector_grads = jnp.stack([prenorm_grad, midnorm_grad, router_grad], axis=1)
    vector_grads = jnp.pad(vector_grads, ((0, 0), (0, 125)))
    first_out = scatter_grads(
        lines, jnp.concatenate([attention_grad, mixing_grad, vector_grads], axis=1)
    )

    offset = lax.axis_index("mp") * half_width

    def put(base, values):
        mine = lax.dynamic_slice_in_dim(values, offset, half_width, 1).astype(BF)
        mine = mine.reshape(row_count, sel_count, half_width)
        placed = jnp.einsum("bts,btd->bsd", one_hot, mine, preferred_element_type=F32).astype(BF)
        return jnp.where(jnp.any(hit, axis=1)[:, :, None], placed, base)

    attention_out = first_out[:, : 3 * half_width].reshape(own_rows, 3, half_width).transpose(1, 0, 2)
    vector_out = first_out[:, 4 * half_width : 4 * half_width + 3]
    return (
        put(tokens, finished),
        put(cotangent, total_grad),
        attention_out,
        first_out[:, 3 * half_width : 4 * half_width].T,
        up_out,
        down_out.T,
        vector_out[:, 0],
        vector_out[:, 1],
        vector_out[:, 2],
    )


def solution(mesh):
    in_specs = (
        P("dp", None, "mp"),
        P("dp", None),
        P("dp", None),
        P("dp", None),
        P(None, "dp", "mp"),
        P("mp", "dp"),
        P("dp", "mp"),
        P("mp", "dp"),
        P("dp"),
        P("dp"),
        P("dp"),
        P("dp", None, "mp"),
    )
    out_specs = (
        P("dp", None, "mp"),
        P("dp", None, "mp"),
        P(None, "dp", "mp"),
        P("mp", "dp"),
        P("dp", "mp"),
        P("mp", "dp"),
        P("dp"),
        P("dp"),
        P("dp"),
    )
    count = mesh.shape["dp"]

    def body(*args):
        return shards(*args, count)

    return jax.shard_map(body, mesh=mesh, in_specs=in_specs, out_specs=out_specs, check_vma=False)
```

time: 990 us -> 399 us (0.40)
  waiting for transfers between devices: 417 us -> 94.5 us
  local copies, waits for them, and re-layouts: 277 us -> 50.6 us
  blocking collectives: 165 us -> 0 us
  starting transfers between devices: 0.91 us -> 137 us
  other arithmetic: 30.1 us -> 46.1 us
  between operations: 16.6 us -> 3.31 us
  matrix products: 71.7 us -> 60.1 us
    reduce_scatter x3 -> x0, waiting for transfers between devices: 309 us -> none  [the longest x1 142 us: shards(): lax.psum_scatter(contract_grad, 'dp', scatter_dimension=1, tiled=True)]
    scatter x2 -> x0, local copies, waits for them, and re-layouts: 185 us -> none  [the longest x1 92.7 us: shards(): cotangent.at[row_ids, chosen]]
    ppermute x0 -> x65, starting transfers between devices: none -> 137 us  [the longest x9 42.2 us: gather(): right = lax.ppermute(right, 'dp', self.pairs(1))]
    unnamed x2 -> x0, blocking collectives: 124 us -> none
    ppermute x0 -> x65, waiting for transfers between devices: none -> 94.5 us  [the longest x24 87.2 us: swap(): return lax.ppermute(value, 'dp', self.pairs(1) + self.pairs(-1))]
    all_gather x5 -> x0, waiting for transfers between devices: 77.4 us -> none  [the longest x1 63.2 us: shards(): lax.all_gather(expand, 'dp', axis=0, tiled=True)]
    all_gather x1 -> x0, blocking collectives: 41.8 us -> none  [shards(): lax.all_gather(mixing, 'dp', axis=1, tiled=True)]
    gather x7 -> x0, local copies, waits for them, and re-layouts: 33.2 us -> none  [the longest x1 9.97 us: shards(): local_grads = cotangent[row_ids, chosen]]
  transfers between devices with their start and end apart: 12 -> 65, of which waited for: 7 -> 20; matrix products, arithmetic and copies ran while one was open for 30% -> 33% of each run, Pallas kernels for 0% -> 0%
where the time goes in v1:
time: 399 us; the launch traced here: 391 us
  starting transfers between devices  137 us (34%)
  waiting for transfers between devices  94.5 us (24%)
  matrix products  60.1 us (15%)
  local copies, waits for them, and re-layouts  50.6 us (13%)
  other arithmetic  46.1 us (12%)
    ppermute x24, waiting for transfers between devices, swap(): return lax.ppermute(value, 'dp', self.pairs(1) + self.pairs(-1))  87.2 us
    ppermute x9, starting transfers between devices, gather(): right = lax.ppermute(right, 'dp', self.pairs(1))  42.2 us
    ppermute x9, starting transfers between devices, scatter(): right = lax.ppermute(to_right.astype(BF), 'dp', self.pairs(1)).astype(F32)  40.8 us
    dot_general x12, matrix products, dot(): lax.dot_general(a, b, ((contract[:1], contract[1:]), ((), ())), preferred...  31.5 us
    ppermute x24, starting transfers between devices, swap(): return lax.ppermute(value, 'dp', self.pairs(1) + self.pairs(-1))  29.5 us
    unnamed x171, local copies, waits for them, and re-layouts  17.7 us
    ppermute x9, starting transfers between devices, scatter(): left = lax.ppermute(to_left.astype(BF), 'dp', self.pairs(-1)).astype(F32)  11.8 us
    ppermute x9, starting transfers between devices, gather(): left = lax.ppermute(left, 'dp', self.pairs(-1))  11.6 us
  transfers between devices with their start and end apart: 65, of which 20 were waited for; matrix products, arithmetic and copies ran while one was open for 33% of the time, Pallas kernels for 0%

profile of v1, /device:TPU:0, one launch (start us, length us, event | category | flops | bytes accessed | tf_op | source)
XLA Modules:
  0.0 391.2 jit_solution(4656380684877501805)
XLA Ops:
  0.6 4.9 %collective-permute-start.12 = (bf16[48,1536]{1,0:T(8,128)(2,1)}, bf16[48,1536]{1,0:T(8,128)(2,1)S(1)}, u32[]{:S(2)}, u32[]{:S(2)}) collective-permute-start(bf16[48,1536]{1,0:T(8,128)(2,1)} %param.18), channel_id=1, source_target_pairs={{0,8},{2,10},{4,12},{6,14},{8,16},{10,18},{12,20},{14,22},{16,24},... | collective-permute-start | bytes 442376 | tf_op jit(solution)/shard_map/ppermute | solution.py:54
  12.1 5.2 %collective-permute-start.1 = (bf16[48,1664]{1,0:T(8,128)(2,1)S(1)}, bf16[48,1664]{1,0:T(8,128)(2,1)S(1)}, u32[]{:S(2)}, u32[]{:S(2)}) collective-permute-start(bf16[48,1664]{1,0:T(8,128)(2,1)S(1)} %constant_dynamic-update-slice_fusion), channel_id=1, source_target_pairs={{0,8},{2,10},{4,12},{6,14},{8,16},{10,18},{12,20},{14,22},{16,24},... | collective-permute-start | bytes 479240 | tf_op jit(solution)/shard_map/ppermute | solution.py:54
  18.7 4.6 %select_reduce_fusion.1 = (s32[3,256]{1,0:T(4,128)S(1)}, s32[3,256]{1,0:T(4,128)S(1)}) fusion(s32[3,2048]{1,0:T(4,128)} %param.14, s32[3,256]{1,0:T(4,128)} %param.15, s32[3,2048]{1,0:T(4,128)} %param.13), kind=kLoop, calls=%fused_computation.4 | loop fusion | flops 7862784 | bytes 58368 | tf_op jit(solution)/shard_map/reduce_sum | solution.py:180
  23.3 4.2 %fusion.36 = bf16[1,3,256,384]{3,2,1,0:T(8,128)(2,1)S(1)} fusion(bf16[3,2048,384]{2,1,0:T(8,128)(2,1)} %param.12, s32[3,256]{1,0:T(4,128)} %param.15), kind=kOutput, calls=%fused_computation.130 | convolution fusion | flops 1209827328 | bytes 5311488 | tf_op jit(solution)/shard_map/bts,bsd->btd/dot_general | solution.py:177
  30.4 4.5 %collective-permute-start.13 = (bf16[48,1536]{1,0:T(8,128)(2,1)S(1)}, bf16[48,1536]{1,0:T(8,128)(2,1)S(1)}, u32[]{:S(2)}, u32[]{:S(2)}) collective-permute-start(bf16[48,1536]{1,0:T(8,128)(2,1)S(1)} %collective-permute-done.12), channel_id=1, source_target_pairs={{0,8},{2,10},{4,12},{6,14},{8,16},{10,18},{12,20},{14,22},{16,24},... | collective-permute-start | bytes 442376 | tf_op jit(solution)/shard_map/ppermute | solution.py:54
  36.5 3.9 collective-permute-start.22
  41.7 4.6 %collective-permute-start.14 = (bf16[48,1536]{1,0:T(8,128)(2,1)S(1)}, bf16[48,1536]{1,0:T(8,128)(2,1)S(1)}, u32[]{:S(2)}, u32[]{:S(2)}) collective-permute-start(bf16[48,1536]{1,0:T(8,128)(2,1)S(1)} %collective-permute-done.13), channel_id=1, source_target_pairs={{0,8},{2,10},{4,12},{6,14},{8,16},{10,18},{12,20},{14,22},{16,24},... | collective-permute-start | bytes 442376 | tf_op jit(solution)/shard_map/ppermute | solution.py:54
  48.4 4.6 %collective-permute-start.23 = (bf16[48,1536]{1,0:T(8,128)(2,1)S(1)}, bf16[48,1536]{1,0:T(8,128)(2,1)S(1)}, u32[]{:S(2)}, u32[]{:S(2)}) collective-permute-start(bf16[48,1536]{1,0:T(8,128)(2,1)S(1)} %collective-permute-done.22), channel_id=1, source_target_pairs={{0,8},{2,10},{4,12},{6,14},{8,16},{10,18},{12,20},{14,22},{16,24},... | collective-permute-start | bytes 442376 | tf_op jit(solution)/shard_map/ppermute | solution.py:54
  54.3 4.6 %collective-permute-start.2 = (bf16[48,1664]{1,0:T(8,128)(2,1)S(1)}, bf16[48,1664]{1,0:T(8,128)(2,1)S(1)}, u32[]{:S(2)}, u32[]{:S(2)}) collective-permute-start(bf16[48,1664]{1,0:T(8,128)(2,1)S(1)} %collective-permute-done.1), channel_id=1, source_target_pairs={{0,8},{2,10},{4,12},{6,14},{8,16},{10,18},{12,20},{14,22},{16,24},... | collective-permute-start | bytes 479240 | tf_op jit(solution)/shard_map/ppermute | solution.py:54
  61.7 5.2 %collective-permute-start.24 = (bf16[48,1536]{1,0:T(8,128)(2,1)S(1)}, bf16[48,1536]{1,0:T(8,128)(2,1)S(1)}, u32[]{:S(2)}, u32[]{:S(2)}) collective-permute-start(bf16[48,1536]{1,0:T(8,128)(2,1)S(1)} %collective-permute-done.23), channel_id=1, source_target_pairs={{0,8},{2,10},{4,12},{6,14},{8,16},{10,18},{12,20},{14,22},{16,24},... | collective-permute-start | bytes 442376 | tf_op jit(solution)/shard_map/ppermute | solution.py:54
  68.3 4.8 %collective-permute-start.3 = (bf16[48,1664]{1,0:T(8,128)(2,1)S(1)}, bf16[48,1664]{1,0:T(8,128)(2,1)S(1)}, u32[]{:S(2)}, u32[]{:S(2)}) collective-permute-start(bf16[48,1664]{1,0:T(8,128)(2,1)S(1)} %collective-permute-done.2), channel_id=1, source_target_pairs={{0,8},{2,10},{4,12},{6,14},{8,16},{10,18},{12,20},{14,22},{16,24},... | collective-permute-start | bytes 479240 | tf_op jit(solution)/shard_map/ppermute | solution.py:54
  102.9 8.2 %collective-permute-done.19 = bf16[2,4,48,768]{3,2,1,0:T(8,128)(2,1)S(1)} collective-permute-done((bf16[2,4,48,768]{3,2,1,0:T(8,128)(2,1)S(1)}, bf16[2,4,48,768]{3,2,1,0:T(8,128)(2,1)S(1)}, u32[]{:S(2)}, u32[]{:S(2)}) %collective-permute-start.19) | collective-permute-done | bytes 589856 | tf_op jit(solution)/shard_map/ppermute | solution.py:43
  114.3 9.4 %collective-permute-done.29 = bf16[2,4,48,768]{3,2,1,0:T(8,128)(2,1)S(1)} collective-permute-done((bf16[2,4,48,768]{3,2,1,0:T(8,128)(2,1)S(1)}, bf16[2,4,48,768]{3,2,1,0:T(8,128)(2,1)S(1)}, u32[]{:S(2)}, u32[]{:S(2)}) %collective-permute-start.29) | collective-permute-done | bytes 589856 | tf_op jit(solution)/shard_map/ppermute | solution.py:43
  125.1 9.7 %collective-permute-done.10 = bf16[2,4,48,768]{3,2,1,0:T(8,128)(2,1)S(1)} collective-permute-done((bf16[2,4,48,768]{3,2,1,0:T(8,128)(2,1)S(1)}, bf16[2,4,48,768]{3,2,1,0:T(8,128)(2,1)S(1)}, u32[]{:S(2)}, u32[]{:S(2)}) %collective-permute-start.10) | collective-permute-done | bytes 589856 | tf_op jit(solution)/shard_map/ppermute | solution.py:43
  143.2 6.7 %reshape.257 = bf16[3,256,3,6,64]{4,3,2,1,0:T(8,128)(2,1)} reshape(bf16[768,1152]{1,0:T(8,128)(2,1)} %convolution_convert_fusion) | data formatting | bytes 3538944 | tf_op jit(solution)/shard_map/reshape | solution.py:191
  149.9 4.9 %fusion.166 = (bf16[3,256,1,6,64]{4,3,2,1,0:T(8,128)(2,1)}, bf16[3,256,1,6,64]{4,3,2,1,0:T(8,128)(2,1)}, bf16[3,256,1,6,64]{4,3,2,1,0:T(8,128)(2,1)}) fusion(bf16[3,256,3,6,64]{4,3,2,1,0:T(8,128)(2,1)} %reshape.257), kind=kLoop, calls=%fused_computation.389 | loop fusion | bytes 3538944 | tf_op jit(solution)/shard_map/slice | solution.py:192
  184.3 5.2 %fusion.12 = bf16[768,1536]{1,0:T(8,128)(2,1)S(1)} fusion(f32[768,1536]{1,0:T(8,128)S(1)} %fusion.27, bf16[768,768]{1,0:T(8,128)(2,1)S(1)} %multiply_convert_fusion.4, bf16[768,768]{1,0:T(8,128)(2,1)S(1)} %bitcast.441, bf16[768,768]{1,0:T(8,128)(2,1)S(1)} %bitcast.439), kind=kOutput, calls=%fused_computation.19 | convolution fusion | flops 1840250880 | bytes 10616832 | tf_op jit(solution)/shard_map/dot_general | solution.py:134
  201.1 11.8 %collective-permute-done.55 = bf16[2,4,48,768]{3,2,1,0:T(8,128)(2,1)S(1)} collective-permute-done((bf16[2,4,48,768]{3,2,1,0:T(8,128)(2,1)S(1)}, bf16[2,4,48,768]{3,2,1,0:T(8,128)(2,1)S(1)}, u32[]{:S(2)}, u32[]{:S(2)}) %collective-permute-start.55) | collective-permute-done | bytes 589856 | tf_op jit(solution)/shard_map/ppermute | solution.py:43
  215.4 9.8 %collective-permute-done.45 = bf16[2,4,48,768]{3,2,1,0:T(8,128)(2,1)S(1)} collective-permute-done((bf16[2,4,48,768]{3,2,1,0:T(8,128)(2,1)S(1)}, bf16[2,4,48,768]{3,2,1,0:T(8,128)(2,1)S(1)}, u32[]{:S(2)}, u32[]{:S(2)}) %collective-permute-start.45) | collective-permute-done | bytes 589856 | tf_op jit(solution)/shard_map/ppermute | solution.py:43
  230.2 5.3 %collective-permute-done.56 = bf16[4,48,768]{2,1,0:T(8,128)(2,1)S(1)} collective-permute-done((bf16[4,48,768]{2,1,0:T(8,128)(2,1)S(1)}, bf16[4,48,768]{2,1,0:T(8,128)(2,1)S(1)}, u32[]{:S(2)}, u32[]{:S(2)}) %collective-permute-start.56) | collective-permute-done | bytes 294944 | tf_op jit(solution)/shard_map/ppermute | solution.py:43
  242.3 4.6 %collective-permute-start.49 = (bf16[48,1536]{1,0:T(8,128)(2,1)S(1)}, bf16[48,1536]{1,0:T(8,128)(2,1)S(1)}, u32[]{:S(2)}, u32[]{:S(2)}) collective-permute-start(bf16[48,1536]{1,0:T(8,128)(2,1)S(1)} %get-tuple-element.78), channel_id=1, source_target_pairs={{0,8},{2,10},{4,12},{6,14},{8,16},{10,18},{12,20},{14,22},{16,24},... | collective-permute-start | bytes 442376 | tf_op jit(solution)/shard_map/ppermute | solution.py:77
  249.0 5.2 %collective-permute-start.60 = (bf16[48,1536]{1,0:T(8,128)(2,1)}, bf16[48,1536]{1,0:T(8,128)(2,1)}, u32[]{:S(2)}, u32[]{:S(2)}) collective-permute-start(bf16[48,1536]{1,0:T(8,128)(2,1)} %get-tuple-element.70), channel_id=1, source_target_pairs={{0,8},{2,10},{4,12},{6,14},{8,16},{10,18},{12,20},{14,22},{16,24},... | collective-permute-start | bytes 442376 | tf_op jit(solution)/shard_map/ppermute | solution.py:77
  256.3 5.2 %collective-permute-start.50 = (bf16[48,1536]{1,0:T(8,128)(2,1)}, bf16[48,1536]{1,0:T(8,128)(2,1)}, u32[]{:S(2)}, u32[]{:S(2)}) collective-permute-start(bf16[48,1536]{1,0:T(8,128)(2,1)} %get-tuple-element.76), channel_id=1, source_target_pairs={{0,8},{2,10},{4,12},{6,14},{8,16},{10,18},{12,20},{14,22},{16,24},... | collective-permute-start | bytes 442376 | tf_op jit(solution)/shard_map/ppermute | solution.py:77
  264.2 5.5 %add_convert_fusion = (bf16[768,768]{1,0:T(8,128)(2,1)S(1)}, f32[768,768]{1,0:T(8,128)}, f32[768]{0:T(1024)}, f32[768,768]{1,0:T(8,128)}) fusion(bf16[1,3,256,768]{3,2,1,0:T(8,128)(2,1)S(1)} %pad_maximum_fusion.10, f32[768]{0:T(1024)S(1)} %mul.281, f32[768,768]{1,0:T(8,128)S(1)} %get-tuple-element.47, f32[768]{0:T(1024)S(1)} %multiply_multiply_fusion.3, ...), kind=kLoop, calls=%fused_computation.87 | loop fusion | flops 12385536 | bytes 16530432 | tf_op jit(solution)/shard_map/convert_element_type | solution.py:225
  276.2 4.2 %fusion.38 = bf16[3,256,6,64]{1,3,2,0:T(8,128)(2,1)} fusion(bf16[3,256,6,64]{1,3,2,0:T(8,128)(2,1)S(1)} %copy.96, f32[3,6,256,256]{2,3,1,0:T(8,128)} %copy-done.14, f32[3,6,256]{2,1,0:T(8,128)} %copy-done.54), kind=kOutput, calls=%fused_computation.132 | convolution fusion | flops 153649152 | bytes 5916672 | tf_op jit(solution)/shard_map/bhqk,bqhd->bkhd/dot_general | solution.py:234
  291.6 5.2 %collective-permute-start.61 = (bf16[48,1536]{1,0:T(8,128)(2,1)}, bf16[48,1536]{1,0:T(8,128)(2,1)}, u32[]{:S(2)}, u32[]{:S(2)}) collective-permute-start(bf16[48,1536]{1,0:T(8,128)(2,1)} %get-tuple-element.68), channel_id=1, source_target_pairs={{0,8},{2,10},{4,12},{6,14},{8,16},{10,18},{12,20},{14,22},{16,24},... | collective-permute-start | bytes 442376 | tf_op jit(solution)/shard_map/ppermute | solution.py:77
  308.3 5.2 %collective-permute-start.51 = (bf16[48,1536]{1,0:T(8,128)(2,1)}, bf16[48,1536]{1,0:T(8,128)(2,1)}, u32[]{:S(2)}, u32[]{:S(2)}) collective-permute-start(bf16[48,1536]{1,0:T(8,128)(2,1)} %get-tuple-element.74), channel_id=1, source_target_pairs={{0,8},{2,10},{4,12},{6,14},{8,16},{10,18},{12,20},{14,22},{16,24},... | collective-permute-start | bytes 442376 | tf_op jit(solution)/shard_map/ppermute | solution.py:77
  330.1 11.9 %collective-permute-done.35 = bf16[2,4,48,768]{3,2,1,0:T(8,128)(2,1)S(1)} collective-permute-done((bf16[2,4,48,768]{3,2,1,0:T(8,128)(2,1)S(1)}, bf16[2,4,48,768]{3,2,1,0:T(8,128)(2,1)S(1)}, u32[]{:S(2)}, u32[]{:S(2)}) %collective-permute-start.35) | collective-permute-done | bytes 589856 | tf_op jit(solution)/shard_map/ppermute | solution.py:43
  354.1 4.0 %collective-permute-start.39 = (bf16[48,1664]{1,0:T(8,128)(2,1)S(1)}, bf16[48,1664]{1,0:T(8,128)(2,1)S(1)}, u32[]{:S(2)}, u32[]{:S(2)}) collective-permute-start(bf16[48,1664]{1,0:T(8,128)(2,1)S(1)} %get-tuple-element.66), channel_id=1, source_target_pairs={{0,8},{2,10},{4,12},{6,14},{8,16},{10,18},{12,20},{14,22},{16,24},... | collective-permute-start | bytes 479240 | tf_op jit(solution)/shard_map/ppermute | solution.py:77
  360.9 4.4 %collective-permute-done.42 = bf16[48,1664]{1,0:T(8,128)(2,1)S(1)} collective-permute-done((bf16[48,1664]{1,0:T(8,128)(2,1)S(1)}, bf16[48,1664]{1,0:T(8,128)(2,1)S(1)}, u32[]{:S(2)}, u32[]{:S(2)}) %collective-permute-start.42) | collective-permute-done | bytes 159776 | tf_op jit(solution)/shard_map/ppermute | solution.py:78
  369.9 6.8 %convert_select_fusion.1 = bf16[3,2048,384]{2,1,0:T(8,128)(2,1)} fusion(bf16[3,2048,384]{2,1,0:T(8,128)(2,1)} %param.12, pred[3,2048]{1,0:T(4,128)(4,1)S(1)} %copy-done.61, bf16[3,256,384]{2,1,0:T(8,128)(2,1)S(1)} %bitcast.445, s32[3,256]{1,0:T(4,128)S(1)} %copy-done.59), kind=kOutput, calls=%fused_computation.23 | convolution fusion | flops 1214251008 | bytes 10036224 | tf_op jit(solution)/shard_map/bts,btd->bsd/dot_general | solution.py:256
  376.8 4.6 %collective-permute-start.41 = (bf16[48,1664]{1,0:T(8,128)(2,1)S(1)}, bf16[48,1664]{1,0:T(8,128)(2,1)S(1)}, u32[]{:S(2)}, u32[]{:S(2)}) collective-permute-start(bf16[48,1664]{1,0:T(8,128)(2,1)S(1)} %get-tuple-element.62), channel_id=1, source_target_pairs={{0,8},{2,10},{4,12},{6,14},{8,16},{10,18},{12,20},{14,22},{16,24},... | collective-permute-start | bytes 479240 | tf_op jit(solution)/shard_map/ppermute | solution.py:77
  (430 shorter events, 199.2 us)
Async XLA Ops:
  0.6 29.8 %collective-permute-start.12 = (bf16[48,1536]{1,0:T(8,128)(2,1)}, bf16[48,1536]{1,0:T(8,128)(2,1)S(1)}, u32[]{:S(2)}, u32[]{:S(2)}) collective-permute-start(bf16[48,1536]{1,0:T(8,128)(2,1)} %param.18), channel_id=1, source_target_pairs={{0,8},{2,10},{4,12},{6,14},{8,16},{10,18},{12,20},{14,22},{16,24},... | collective-permute-start | bytes 442376 | tf_op jit(solution)/shard_map/ppermute | solution.py:54
  5.6 34.8 %collective-permute-start.15 = (bf16[48,1536]{1,0:T(8,128)(2,1)}, bf16[48,1536]{1,0:T(8,128)(2,1)S(1)}, u32[]{:S(2)}, u32[]{:S(2)}) collective-permute-start(bf16[48,1536]{1,0:T(8,128)(2,1)} %param.18), channel_id=1, source_target_pairs={{8,0},{10,2},{12,4},{14,6},{16,8},{18,10},{20,12},{22,14},{24,16},... | collective-permute-start | bytes 442376 | tf_op jit(solution)/shard_map/ppermute | solution.py:55
  10.8 37.6 %collective-permute-start.4 = (bf16[48,1664]{1,0:T(8,128)(2,1)S(1)}, bf16[48,1664]{1,0:T(8,128)(2,1)S(1)}, u32[]{:S(2)}, u32[]{:S(2)}) collective-permute-start(bf16[48,1664]{1,0:T(8,128)(2,1)S(1)} %constant_dynamic-update-slice_fusion), channel_id=1, source_target_pairs={{8,0},{10,2},{12,4},{14,6},{16,8},{18,10},{20,12},{22,14},{24,16},... | collective-permute-start | bytes 479240 | tf_op jit(solution)/shard_map/ppermute | solution.py:55
  12.1 40.9 %collective-permute-start.1 = (bf16[48,1664]{1,0:T(8,128)(2,1)S(1)}, bf16[48,1664]{1,0:T(8,128)(2,1)S(1)}, u32[]{:S(2)}, u32[]{:S(2)}) collective-permute-start(bf16[48,1664]{1,0:T(8,128)(2,1)S(1)} %constant_dynamic-update-slice_fusion), channel_id=1, source_target_pairs={{0,8},{2,10},{4,12},{6,14},{8,16},{10,18},{12,20},{14,22},{16,24},... | collective-permute-start | bytes 479240 | tf_op jit(solution)/shard_map/ppermute | solution.py:54
  17.3 19.1 %collective-permute-start.25 = (bf16[48,1536]{1,0:T(8,128)(2,1)}, bf16[48,1536]{1,0:T(8,128)(2,1)S(1)}, u32[]{:S(2)}, u32[]{:S(2)}) collective-permute-start(bf16[48,1536]{1,0:T(8,128)(2,1)} %bitcast.446), channel_id=1, source_target_pairs={{8,0},{10,2},{12,4},{14,6},{16,8},{18,10},{20,12},{22,14},{24,16},... | collective-permute-start | bytes 442376 | tf_op jit(solution)/shard_map/ppermute | solution.py:55
  41.7 17.2 %collective-permute-start.14 = (bf16[48,1536]{1,0:T(8,128)(2,1)S(1)}, bf16[48,1536]{1,0:T(8,128)(2,1)S(1)}, u32[]{:S(2)}, u32[]{:S(2)}) collective-permute-start(bf16[48,1536]{1,0:T(8,128)(2,1)S(1)} %collective-permute-done.13), channel_id=1, source_target_pairs={{0,8},{2,10},{4,12},{6,14},{8,16},{10,18},{12,20},{14,22},{16,24},... | collective-permute-start | bytes 442376 | tf_op jit(solution)/shard_map/ppermute | solution.py:54
  60.3 38.9 %collective-permute-start = (bf16[2,3,256,384]{3,2,1,0:T(8,128)(2,1)S(1)}, bf16[2,3,256,384]{3,2,1,0:T(8,128)(2,1)S(1)}, u32[]{:S(2)}, u32[]{:S(2)}) collective-permute-start(bf16[2,3,256,384]{3,2,1,0:T(8,128)(2,1)S(1)} %pad_maximum_fusion.11), channel_id=1, source_target_pairs={{0,1},{1,0},{2,3},{3,2},{4,5},{5,4},{6,7},{7,6},{8,9},{9,8},{10,11... | collective-permute-start | bytes 3538952 | tf_op jit(solution)/shard_map/ppermute | solution.py:119
  60.4 14.4 %collective-permute-start.27 = (bf16[48,1536]{1,0:T(8,128)(2,1)S(1)}, bf16[48,1536]{1,0:T(8,128)(2,1)S(1)}, u32[]{:S(2)}, u32[]{:S(2)}) collective-permute-start(bf16[48,1536]{1,0:T(8,128)(2,1)S(1)} %collective-permute-done.26), channel_id=1, source_target_pairs={{8,0},{10,2},{12,4},{14,6},{16,8},{18,10},{20,12},{22,14},{24,16},... | collective-permute-start | bytes 442376 | tf_op jit(solution)/shard_map/ppermute | solution.py:55
  89.4 21.7 %collective-permute-start.19 = (bf16[2,4,48,768]{3,2,1,0:T(8,128)(2,1)S(1)}, bf16[2,4,48,768]{3,2,1,0:T(8,128)(2,1)S(1)}, u32[]{:S(2)}, u32[]{:S(2)}) collective-permute-start(bf16[2,4,48,768]{3,2,1,0:T(8,128)(2,1)S(1)} %pad_maximum_fusion.16), channel_id=1, source_target_pairs={{0,4},{2,6},{8,12},{10,14},{16,20},{18,22},{24,28},{26,30},{4,0},{... | collective-permute-start | bytes 1769480 | tf_op jit(solution)/shard_map/ppermute | solution.py:43
  91.1 20.6 %collective-permute-start.21 = (bf16[2,4,48,768]{3,2,1,0:T(8,128)(2,1)S(1)}, bf16[2,4,48,768]{3,2,1,0:T(8,128)(2,1)S(1)}, u32[]{:S(2)}, u32[]{:S(2)}) collective-permute-start(bf16[2,4,48,768]{3,2,1,0:T(8,128)(2,1)S(1)} %pad_maximum_fusion.17), channel_id=1, source_target_pairs={{0,2},{4,6},{8,10},{12,14},{16,18},{20,22},{24,26},{28,30},{2,0},{... | collective-permute-start | bytes 1769480 | tf_op jit(solution)/shard_map/ppermute | solution.py:43
  95.7 28.0 %collective-permute-start.29 = (bf16[2,4,48,768]{3,2,1,0:T(8,128)(2,1)S(1)}, bf16[2,4,48,768]{3,2,1,0:T(8,128)(2,1)S(1)}, u32[]{:S(2)}, u32[]{:S(2)}) collective-permute-start(bf16[2,4,48,768]{3,2,1,0:T(8,128)(2,1)S(1)} %pad_maximum_fusion.18), channel_id=1, source_target_pairs={{0,4},{2,6},{8,12},{10,14},{16,20},{18,22},{24,28},{26,30},{4,0},{... | collective-permute-start | bytes 1769480 | tf_op jit(solution)/shard_map/ppermute | solution.py:43
  98.5 71.3 %collective-permute-start.31 = (bf16[2,4,48,768]{3,2,1,0:T(8,128)(2,1)}, bf16[2,4,48,768]{3,2,1,0:T(8,128)(2,1)}, u32[]{:S(2)}, u32[]{:S(2)}) collective-permute-start(bf16[2,4,48,768]{3,2,1,0:T(8,128)(2,1)} %pad_maximum_fusion.19), channel_id=1, source_target_pairs={{0,2},{4,6},{8,10},{12,14},{16,18},{20,22},{24,26},{28,30},{2,0},{... | collective-permute-start | bytes 1769480 | tf_op jit(solution)/shard_map/ppermute | solution.py:43
  99.3 35.5 %collective-permute-start.10 = (bf16[2,4,48,768]{3,2,1,0:T(8,128)(2,1)S(1)}, bf16[2,4,48,768]{3,2,1,0:T(8,128)(2,1)S(1)}, u32[]{:S(2)}, u32[]{:S(2)}) collective-permute-start(bf16[2,4,48,768]{3,2,1,0:T(8,128)(2,1)S(1)} %pad_maximum_fusion.15), channel_id=1, source_target_pairs={{0,4},{2,6},{8,12},{10,14},{16,20},{18,22},{24,28},{26,30},{4,0},{... | collective-permute-start | bytes 1769480 | tf_op jit(solution)/shard_map/ppermute | solution.py:43
  111.1 23.9 %collective-permute-start.8 = (bf16[2,4,48,896]{3,2,0,1:T(8,128)(2,1)S(1)}, bf16[2,4,48,896]{3,2,0,1:T(8,128)(2,1)S(1)}, u32[]{:S(2)}, u32[]{:S(2)}) collective-permute-start(bf16[2,4,48,896]{3,2,0,1:T(8,128)(2,1)S(1)} %pad_maximum_fusion.14), channel_id=1, source_target_pairs={{0,2},{4,6},{8,10},{12,14},{16,18},{20,22},{24,26},{28,30},{2,0},{... | collective-permute-start | bytes 2064392 | tf_op jit(solution)/shard_map/ppermute | solution.py:43
  196.7 16.2 %collective-permute-start.55 = (bf16[2,4,48,768]{3,2,1,0:T(8,128)(2,1)S(1)}, bf16[2,4,48,768]{3,2,1,0:T(8,128)(2,1)S(1)}, u32[]{:S(2)}, u32[]{:S(2)}) collective-permute-start(bf16[2,4,48,768]{3,2,1,0:T(8,128)(2,1)S(1)} %fusion.55), channel_id=1, source_target_pairs={{0,4},{2,6},{8,12},{10,14},{16,20},{18,22},{24,28},{26,30},{4,0},{... | collective-permute-start | bytes 1769480 | tf_op jit(solution)/shard_map/ppermute | solution.py:43
  198.4 15.5 %collective-permute-start.57 = (bf16[2,4,48,768]{3,2,0,1:T(8,128)(2,1)S(1)}, bf16[2,4,48,768]{3,2,0,1:T(8,128)(2,1)S(1)}, u32[]{:S(2)}, u32[]{:S(2)}) collective-permute-start(bf16[2,4,48,768]{3,2,0,1:T(8,128)(2,1)S(1)} %fusion.51), channel_id=1, source_target_pairs={{0,2},{4,6},{8,10},{12,14},{16,18},{20,22},{24,26},{28,30},{2,0},{... | collective-permute-start | bytes 1769480 | tf_op jit(solution)/shard_map/ppermute | solution.py:43
  199.3 62.2 %collective-permute-start.33 = (bf16[768,768]{1,0:T(8,128)(2,1)S(1)}, bf16[768,768]{1,0:T(8,128)(2,1)S(1)}, u32[]{:S(2)}, u32[]{:S(2)}) collective-permute-start(bf16[768,768]{1,0:T(8,128)(2,1)S(1)} %convolution_convert_fusion.3), channel_id=1, source_target_pairs={{0,1},{1,0},{2,3},{3,2},{4,5},{5,4},{6,7},{7,6},{8,9},{9,8},{10,11... | collective-permute-start | bytes 3538952 | tf_op jit(solution)/shard_map/ppermute | solution.py:119
  199.3 65.0 %collective-permute-start.32 = (bf16[768,768]{1,0:T(8,128)(2,1)S(1)}, bf16[768,768]{1,0:T(8,128)(2,1)S(1)}, u32[]{:S(2)}, u32[]{:S(2)}) collective-permute-start(bf16[768,768]{1,0:T(8,128)(2,1)S(1)} %convolution_convert_fusion.4), channel_id=1, source_target_pairs={{0,1},{1,0},{2,3},{3,2},{4,5},{5,4},{6,7},{7,6},{8,9},{9,8},{10,11... | collective-permute-start | bytes 3538952 | tf_op jit(solution)/shard_map/ppermute | solution.py:119
  200.5 24.7 %collective-permute-start.45 = (bf16[2,4,48,768]{3,2,1,0:T(8,128)(2,1)S(1)}, bf16[2,4,48,768]{3,2,1,0:T(8,128)(2,1)S(1)}, u32[]{:S(2)}, u32[]{:S(2)}) collective-permute-start(bf16[2,4,48,768]{3,2,1,0:T(8,128)(2,1)S(1)} %fusion.53), channel_id=1, source_target_pairs={{0,4},{2,6},{8,12},{10,14},{16,20},{18,22},{24,28},{26,30},{4,0},{... | collective-permute-start | bytes 1769480 | tf_op jit(solution)/shard_map/ppermute | solution.py:43
  212.9 16.3 %collective-permute-start.47 = (bf16[2,4,48,768]{3,2,1,0:T(8,128)(2,1)S(1)}, bf16[2,4,48,768]{3,2,1,0:T(8,128)(2,1)S(1)}, u32[]{:S(2)}, u32[]{:S(2)}) collective-permute-start(bf16[2,4,48,768]{3,2,1,0:T(8,128)(2,1)S(1)} %fusion.54), channel_id=1, source_target_pairs={{0,2},{4,6},{8,10},{12,14},{16,18},{20,22},{24,26},{28,30},{2,0},{... | collective-permute-start | bytes 1769480 | tf_op jit(solution)/shard_map/ppermute | solution.py:43
  213.9 21.6 %collective-permute-start.56 = (bf16[4,48,768]{2,1,0:T(8,128)(2,1)S(1)}, bf16[4,48,768]{2,1,0:T(8,128)(2,1)S(1)}, u32[]{:S(2)}, u32[]{:S(2)}) collective-permute-start(bf16[4,48,768]{2,1,0:T(8,128)(2,1)S(1)} %fusion.94), channel_id=1, source_target_pairs={{0,2},{4,6},{8,10},{12,14},{16,18},{20,22},{24,26},{28,30},{2,0},{... | collective-permute-start | bytes 884744 | tf_op jit(solution)/shard_map/ppermute | solution.py:43
  249.0 40.7 %collective-permute-start.60 = (bf16[48,1536]{1,0:T(8,128)(2,1)}, bf16[48,1536]{1,0:T(8,128)(2,1)}, u32[]{:S(2)}, u32[]{:S(2)}) collective-permute-start(bf16[48,1536]{1,0:T(8,128)(2,1)} %get-tuple-element.70), channel_id=1, source_target_pairs={{0,8},{2,10},{4,12},{6,14},{8,16},{10,18},{12,20},{14,22},{16,24},... | collective-permute-start | bytes 442376 | tf_op jit(solution)/shard_map/ppermute | solution.py:77
  254.2 35.6 %collective-permute-start.63 = (bf16[48,1536]{1,0:T(8,128)(2,1)}, bf16[48,1536]{1,0:T(8,128)(2,1)}, u32[]{:S(2)}, u32[]{:S(2)}) collective-permute-start(bf16[48,1536]{1,0:T(8,128)(2,1)} %get-tuple-element.71), channel_id=1, source_target_pairs={{8,0},{10,2},{12,4},{14,6},{16,8},{18,10},{20,12},{22,14},{24,16},... | collective-permute-start | bytes 442376 | tf_op jit(solution)/shard_map/ppermute | solution.py:78
  256.3 49.8 %collective-permute-start.50 = (bf16[48,1536]{1,0:T(8,128)(2,1)}, bf16[48,1536]{1,0:T(8,128)(2,1)}, u32[]{:S(2)}, u32[]{:S(2)}) collective-permute-start(bf16[48,1536]{1,0:T(8,128)(2,1)} %get-tuple-element.76), channel_id=1, source_target_pairs={{0,8},{2,10},{4,12},{6,14},{8,16},{10,18},{12,20},{14,22},{16,24},... | collective-permute-start | bytes 442376 | tf_op jit(solution)/shard_map/ppermute | solution.py:77
  261.5 44.6 %collective-permute-start.53 = (bf16[48,1536]{1,0:T(8,128)(2,1)}, bf16[48,1536]{1,0:T(8,128)(2,1)}, u32[]{:S(2)}, u32[]{:S(2)}) collective-permute-start(bf16[48,1536]{1,0:T(8,128)(2,1)} %get-tuple-element.77), channel_id=1, source_target_pairs={{8,0},{10,2},{12,4},{14,6},{16,8},{18,10},{20,12},{22,14},{24,16},... | collective-permute-start | bytes 442376 | tf_op jit(solution)/shard_map/ppermute | solution.py:78
  291.6 27.7 %collective-permute-start.61 = (bf16[48,1536]{1,0:T(8,128)(2,1)}, bf16[48,1536]{1,0:T(8,128)(2,1)}, u32[]{:S(2)}, u32[]{:S(2)}) collective-permute-start(bf16[48,1536]{1,0:T(8,128)(2,1)} %get-tuple-element.68), channel_id=1, source_target_pairs={{0,8},{2,10},{4,12},{6,14},{8,16},{10,18},{12,20},{14,22},{16,24},... | collective-permute-start | bytes 442376 | tf_op jit(solution)/shard_map/ppermute | solution.py:77
  296.8 22.5 %collective-permute-start.64 = (bf16[48,1536]{1,0:T(8,128)(2,1)}, bf16[48,1536]{1,0:T(8,128)(2,1)}, u32[]{:S(2)}, u32[]{:S(2)}) collective-permute-start(bf16[48,1536]{1,0:T(8,128)(2,1)} %get-tuple-element.69), channel_id=1, source_target_pairs={{8,0},{10,2},{12,4},{14,6},{16,8},{18,10},{20,12},{22,14},{24,16},... | collective-permute-start | bytes 442376 | tf_op jit(solution)/shard_map/ppermute | solution.py:78
  306.0 15.0 %collective-permute-start.34 = (bf16[768,768]{1,0:T(8,128)(2,1)S(1)}, bf16[768,768]{1,0:T(8,128)(2,1)S(1)}, u32[]{:S(2)}, u32[]{:S(2)}) collective-permute-start(bf16[768,768]{1,0:T(8,128)(2,1)S(1)} %convolution_convert_fusion.1), channel_id=1, source_target_pairs={{0,1},{1,0},{2,3},{3,2},{4,5},{5,4},{6,7},{7,6},{8,9},{9,8},{10,11... | collective-permute-start | bytes 3538952 | tf_op jit(solution)/shard_map/ppermute | solution.py:119
  308.3 20.1 %collective-permute-start.51 = (bf16[48,1536]{1,0:T(8,128)(2,1)}, bf16[48,1536]{1,0:T(8,128)(2,1)}, u32[]{:S(2)}, u32[]{:S(2)}) collective-permute-start(bf16[48,1536]{1,0:T(8,128)(2,1)} %get-tuple-element.74), channel_id=1, source_target_pairs={{0,8},{2,10},{4,12},{6,14},{8,16},{10,18},{12,20},{14,22},{16,24},... | collective-permute-start | bytes 442376 | tf_op jit(solution)/shard_map/ppermute | solution.py:77
  313.5 14.9 %collective-permute-start.54 = (bf16[48,1536]{1,0:T(8,128)(2,1)}, bf16[48,1536]{1,0:T(8,128)(2,1)}, u32[]{:S(2)}, u32[]{:S(2)}) collective-permute-start(bf16[48,1536]{1,0:T(8,128)(2,1)} %get-tuple-element.75), channel_id=1, source_target_pairs={{8,0},{10,2},{12,4},{14,6},{16,8},{18,10},{20,12},{22,14},{24,16},... | collective-permute-start | bytes 442376 | tf_op jit(solution)/shard_map/ppermute | solution.py:78
  326.6 15.4 %collective-permute-start.35 = (bf16[2,4,48,768]{3,2,1,0:T(8,128)(2,1)S(1)}, bf16[2,4,48,768]{3,2,1,0:T(8,128)(2,1)S(1)}, u32[]{:S(2)}, u32[]{:S(2)}) collective-permute-start(bf16[2,4,48,768]{3,2,1,0:T(8,128)(2,1)S(1)} %fusion.52), channel_id=1, source_target_pairs={{0,4},{2,6},{8,12},{10,14},{16,20},{18,22},{24,28},{26,30},{4,0},{... | collective-permute-start | bytes 1769480 | tf_op jit(solution)/shard_map/ppermute | solution.py:43
  327.5 17.8 %collective-permute-start.37 = (bf16[2,4,48,896]{3,2,1,0:T(8,128)(2,1)S(1)}, bf16[2,4,48,896]{3,2,1,0:T(8,128)(2,1)S(1)}, u32[]{:S(2)}, u32[]{:S(2)}) collective-permute-start(bf16[2,4,48,896]{3,2,1,0:T(8,128)(2,1)S(1)} %fusion.50), channel_id=1, source_target_pairs={{0,2},{4,6},{8,10},{12,14},{16,18},{20,22},{24,26},{28,30},{2,0},{... | collective-permute-start | bytes 2064392 | tf_op jit(solution)/shard_map/ppermute | solution.py:43
  (102 other events, 714.7 us)

commit v2 on v1

--- a/solution.py
+++ b/solution.py
@@ -1,6 +1,8 @@
 import jax
 import jax.numpy as jnp
 from jax import lax
+from jax.experimental import pallas as pl
+from jax.experimental.pallas import tpu as pltpu
 from jax.sharding import PartitionSpec as P
 
 HD = 64
@@ -27,92 +29,87 @@
     return (causal[None] & same_doc & open_key)[:, None]
 
 
-class Line:
-    def __init__(self, count, stride, size):
-        self.count, self.stride, self.size = count, stride, size
-        self.pos = (lax.axis_index("dp") // stride) % size
-
-    def pairs(self, step):
-        return [
-            (i, i + step * self.stride)
-            for i in range(self.count)
-            if 0 <= (i // self.stride) % self.size + step < self.size
-        ]
-
-    def swap(self, value):
-        return lax.ppermute(value, "dp", self.pairs(1) + self.pairs(-1))
-
-    def gather(self, own):
-        if self.size == 1:
-            return own[None]
-        if self.size == 2:
-            other = self.swap(own)
-            first = self.pos == 0
-            return jnp.stack([jnp.where(first, own, other), jnp.where(first, other, own)])
-        lower, upper, right, left = [], [], own, own
-        for _ in range(self.size - 1):
-            right = lax.ppermute(right, "dp", self.pairs(1))
-            left = lax.ppermute(left, "dp", self.pairs(-1))
-            lower.insert(0, right)
-            upper.append(left)
-        stack = jnp.stack(lower + [own] + upper)
-        return lax.dynamic_slice_in_dim(stack, self.size - 1 - self.pos, self.size, 0)
-
-    def scatter(self, value):
-        def at(index):
-            return lax.dynamic_index_in_dim(value, index, 0, keepdims=False)
-
-        mine = at(self.pos)
-        if self.size == 1:
-            return mine
-        if self.size == 2:
-            return mine + self.swap(at(1 - self.pos).astype(BF)).astype(F32)
-        right = left = None
-        for away in range(self.size - 1, 0, -1):
-            to_right = at(jnp.minimum(self.pos + away, self.size - 1))
-            to_left = at(jnp.maximum(self.pos - away, 0))
-            if right is not None:
-                to_right = to_right + right
-                to_left = to_left + left
-            right = lax.ppermute(to_right.astype(BF), "dp", self.pairs(1)).astype(F32)
-            left = lax.ppermute(to_left.astype(BF), "dp", self.pairs(-1)).astype(F32)
-        return mine + right + left
-
-
-def lines_of(count):
-    bits = count.bit_length() - 1
-    short = 2 ** (bits // 3) if count == 2**bits else 1
-    return (
-        Line(count, short * short, count // (short * short)),
-        Line(count, short, short),
-        Line(count, 1, short),
-    )
+def untouched(*refs):
+    pass
+
+
+def tie(value, *others):
+    if not others:
+        return value
+    anywhere = pl.BlockSpec(memory_space=pl.ANY)
+    return pl.pallas_call(
+        untouched,
+        out_shape=jax.ShapeDtypeStruct(value.shape, value.dtype),
+        in_specs=[anywhere] * (1 + len(others)),
+        out_specs=anywhere,
+        input_output_aliases={0: 0},
+        compiler_params=pltpu.CompilerParams(vmem_limit_bytes=1 << 20),
+        cost_estimate=pl.CostEstimate(flops=0, bytes_accessed=0, transcendentals=0),
+    )(value, *others)
+
+
+class Cube:
+    def __init__(self, count):
+        self.count, self.bits = count, count.bit_length() - 1
+        self.index = lax.axis_index("dp").astype(jnp.uint32)
+        short = self.bits // 3
+        self.x, self.y = list(range(short)), list(range(short, 2 * short))
+        self.z = list(range(2 * short, self.bits))
+
+    def swap(self, value, bit):
+        return lax.ppermute(value, "dp", [(i, i ^ (1 << bit)) for i in range(self.count)])
+
+    def low(self, bit):
+        return (self.index >> bit) % 2 == 0
+
+    def double(self, value, bit):
+        other, low = self.swap(value, bit), self.low(bit)
+        return jnp.stack([jnp.where(low, value, other), jnp.where(low, other, value)])
+
+    def halve(self, value, axis, bit):
+        own = ((self.index >> bit) % 2).astype(jnp.int32)
+        mine = lax.dynamic_index_in_dim(value, own, axis, keepdims=False)
+        sent = lax.dynamic_index_in_dim(value, 1 - own, axis, keepdims=False)
+        return mine + self.swap(sent.astype(BF), bit).astype(F32)
 
 
 def halves(width):
     return width // 2 // 128 * 128
 
 
-def gather_weights(lines, own):
-    along_z, along_y, along_x = lines
+def gather_weights(cube, own, after=()):
     rows, width = own.shape
     cut = halves(width)
-    column = along_z.gather(own)
-    first = along_y.gather(along_x.gather(column[..., :cut]))
-    second = along_x.gather(along_y.gather(column[..., cut:]))
-    first = first.transpose(2, 0, 1, 3, 4).reshape(-1, cut)
-    second = second.transpose(2, 1, 0, 3, 4).reshape(-1, width - cut)
-    return jnp.concatenate([first, second], axis=1)
-
-
-def scatter_grads(lines, total):
-    along_z, along_y, along_x = lines
+    column = tie(own, *after)
+    for bit in cube.z[::-1]:
+        column = cube.double(column, bit)
+    marks, done = [column], []
+    for part, order in ((column[..., :cut], cube.x + cube.y), (column[..., cut:], cube.y + cube.x)):
+        for bit in order:
+            part = cube.double(part, bit)
+        axes = order[::-1] + cube.z
+        bits = sorted(axes, reverse=True)
+        part = part.transpose([axes.index(b) for b in bits] + [cube.bits, cube.bits + 1])
+        done.append(part.reshape(-1, part.shape[-1]))
+    return jnp.concatenate(done, axis=1), marks
+
+
+def scatter_grads(cube, total):
     width = total.shape[1]
     cut = halves(width)
-    view = total.reshape(along_z.size, along_y.size, along_x.size, -1, width)
-    first = along_x.scatter(along_y.scatter(view[..., :cut].transpose(1, 2, 0, 3, 4)))
-    second = along_y.scatter(along_x.scatter(view[..., cut:].transpose(2, 1, 0, 3, 4)))
-    return along_z.scatter(jnp.concatenate([first, second], axis=-1))
+    parts = []
+    for part, order in ((total[:, :cut], cube.y + cube.x), (total[:, cut:], cube.x + cube.y)):
+        part = part.reshape([2] * cube.bits + [-1, part.shape[1]])
+        axes = list(range(cube.bits))[::-1]
+        for bit in order:
+            part = cube.halve(part, axes.index(bit), bit)
+            axes.remove(bit)
+        parts.append(part)
+    part = jnp.concatenate(parts, axis=-1)
+    for bit in axes[::-1]:
+        part = cube.halve(part, axes.index(bit), bit)
+        axes.remove(bit)
+    return part
 
 
 def other_core(value):
@@ -149,7 +146,7 @@
     cotangent,
     count,
 ):
-    lines = lines_of(count)
+    cube = Cube(count)
     row_count, length, half_width = tokens.shape
     sel_count = chosen.shape[1]
     token_count = row_count * sel_count
@@ -163,9 +160,9 @@
     first_own = jnp.concatenate(
         [attention[0], attention[1], attention[2], mixing.T, vectors], axis=1
     )
-    first = gather_weights(lines, first_own)
-    full_up = gather_weights(lines, expand)
-    full_down = gather_weights(lines, contract.T)
+    first, marks = gather_weights(cube, first_own)
+    full_up, marks = gather_weights(cube, expand, marks)
+    full_down, marks = gather_weights(cube, contract.T, marks)
     full_in = first[:, : 3 * half_width]
     full_mix = first[:, 3 * half_width : 4 * half_width]
     gains = first[:, 4 * half_width : 4 * half_width + 3].astype(F32)
@@ -214,11 +211,11 @@
     router_grad = jnp.sum(logit_grad[:, None] * states, axis=0)
     branch_grad = gate_value[:, None] * upstream
     feed_grad = branch_grad.astype(BF)
-    down_out = scatter_grads(lines, dot(feed_grad, activated, (0, 0)))
+    down_out = scatter_grads(cube, dot(feed_grad, activated, (0, 0)))
     act_grad = dot(feed_grad, full_down, (1, 0))
     _, gelu_pull = jax.vjp(gelu_tanh, hidden)
     hidden_grad = gelu_pull(act_grad)[0].astype(BF)
-    up_out = scatter_grads(lines, dot(normed_mid, hidden_grad, (0, 0)))
+    up_out = scatter_grads(cube, dot(normed_mid, hidden_grad, (0, 0)))
     mid_in_grad = add_cores(dot(hidden_grad, full_up, (1, 1)))
     _, mid_pull = jax.vjp(normalize, middle, mid_scale)
     middle_grad, midnorm_grad = mid_pull(mid_in_grad)
@@ -245,7 +242,7 @@
     vector_grads = jnp.stack([prenorm_grad, midnorm_grad, router_grad], axis=1)
     vector_grads = jnp.pad(vector_grads, ((0, 0), (0, 125)))
     first_out = scatter_grads(
-        lines, jnp.concatenate([attention_grad, mixing_grad, vector_grads], axis=1)
+        cube, jnp.concatenate([attention_grad, mixing_grad, vector_grads], axis=1)
     )
 
     offset = lax.axis_index("mp") * half_width

time: 399 us -> 303 us (0.76)
  starting transfers between devices: 137 us -> 44.7 us
  waiting for transfers between devices: 94.5 us -> 101 us
  matrix products: 60.1 us -> 56.1 us
    ppermute x60 -> x36, starting transfers between devices: 136 us -> 44.1 us  [swap(): lax.ppermute(value, 'dp', [(i, i ^ 1 << bit) for i in range(self.count)])]
    ppermute x60 -> x36, waiting for transfers between devices: 94.5 us -> 101 us  [swap(): lax.ppermute(value, 'dp', [(i, i ^ 1 << bit) for i in range(self.count)])]
    another operation x19 -> x31, other arithmetic: 3.43 us -> 8.8 us  [double(): jnp.stack([jnp.where(low, value, other), jnp.where(low, other, value)])]
    unnamed x171 -> x152, local copies, waits for them, and re-layouts: 17.7 us -> 18.2 us
  transfers between devices with their start and end apart: 65 -> 41, of which waited for: 20 -> 19; matrix products, arithmetic and copies ran while one was open for 33% -> 40% of each run, Pallas kernels for 0% -> 0%
where the time goes in v2:
time: 303 us; the launch traced here: 299 us
  waiting for transfers between devices  101 us (33%)
  matrix products  56.1 us (19%)
  local copies, waits for them, and re-layouts  47.7 us (16%)
  other arithmetic  46.2 us (15%)
  starting transfers between devices  44.7 us (15%)
    ppermute x36, waiting for transfers between devices, swap(): lax.ppermute(value, 'dp', [(i, i ^ 1 << bit) for i in range(self.count)])  101 us
    ppermute x36, starting transfers between devices, swap(): lax.ppermute(value, 'dp', [(i, i ^ 1 << bit) for i in range(self.count)])  44.1 us
    dot_general x12, matrix products, dot(): lax.dot_general(a, b, ((contract[:1], contract[1:]), ((), ())), preferred...  28.9 us
    unnamed x152, local copies, waits for them, and re-layouts  18.2 us
    dot_general x2, matrix products, put(): jnp.einsum('bts,btd->bsd', one_hot, mine, preferred_element_type=F32)  10.6 us
    another operation x31, other arithmetic, double(): jnp.stack([jnp.where(low, value, other), jnp.where(low, other, value)])  8.8 us
    reshape x1, local copies, waits for them, and re-layouts, shards(): shaped = packed.reshape(row_count, sel_count, 3, heads_here, HD)  6.32 us
  transfers between devices with their start and end apart: 41, of which 19 were waited for; matrix products, arithmetic and copies ran while one was open for 40% of the time, Pallas kernels for 0%

profile of v2, /device:TPU:0, one launch (start us, length us, event | category | flops | bytes accessed | tf_op | source)
XLA Modules:
  0.0 298.7 jit_solution(14519884236696352743)
XLA Ops:
  6.4 4.1 %collective-permute-start.1 = (bf16[48,1664]{1,0:T(8,128)(2,1)S(1)}, bf16[48,1664]{1,0:T(8,128)(2,1)S(1)}, u32[]{:S(2)}, u32[]{:S(2)}) collective-permute-start(bf16[48,1664]{1,0:T(8,128)(2,1)S(1)} %constant_dynamic-update-slice_fusion), channel_id=1, source_target_pairs={{0,16},{2,18},{4,20},{6,22},{8,24},{10,26},{12,28},{14,30},{16,0},... | collective-permute-start | bytes 479240 | tf_op jit(solution)/shard_map/ppermute | solution.py:60
  10.5 4.2 %fusion.34 = bf16[1,3,256,384]{3,2,1,0:T(8,128)(2,1)S(1)} fusion(bf16[3,2048,384]{2,1,0:T(8,128)(2,1)} %param.12, s32[3,256]{1,0:T(4,128)} %param.15), kind=kOutput, calls=%fused_computation.99 | convolution fusion | flops 1209827328 | bytes 5311488 | tf_op jit(solution)/shard_map/bts,bsd->btd/dot_general | solution.py:174
  17.8 2.8 select_reduce_fusion.1
  25.5 7.3 %collective-permute-done.2 = bf16[2,48,1664]{2,1,0:T(8,128)(2,1)S(1)} collective-permute-done((bf16[2,48,1664]{2,1,0:T(8,128)(2,1)S(1)}, bf16[2,48,1664]{2,1,0:T(8,128)(2,1)S(1)}, u32[]{:S(2)}, u32[]{:S(2)}) %collective-permute-start.2) | collective-permute-done | bytes 319520 | tf_op jit(solution)/shard_map/ppermute | solution.py:60
  36.8 5.7 %collective-permute-done.8 = bf16[48,1536]{1,0:T(8,128)(2,1)S(1)} collective-permute-done((bf16[48,1536]{1,0:T(8,128)(2,1)S(1)}, bf16[48,1536]{1,0:T(8,128)(2,1)S(1)}, u32[]{:S(2)}, u32[]{:S(2)}) %collective-permute-start.8) | collective-permute-done | bytes 147488 | tf_op jit(solution)/shard_map/ppermute | solution.py:60
  44.5 6.1 %collective-permute-done.9 = bf16[2,48,1536]{2,1,0:T(8,128)(2,1)S(1)} collective-permute-done((bf16[2,48,1536]{2,1,0:T(8,128)(2,1)S(1)}, bf16[2,48,1536]{2,1,0:T(8,128)(2,1)S(1)}, u32[]{:S(2)}, u32[]{:S(2)}) %collective-permute-start.9) | collective-permute-done | bytes 294944 | tf_op jit(solution)/shard_map/ppermute | solution.py:60
  54.4 4.4 %collective-permute-done.14 = bf16[48,1536]{1,0:T(8,128)(2,1)S(1)} collective-permute-done((bf16[48,1536]{1,0:T(8,128)(2,1)S(1)}, bf16[48,1536]{1,0:T(8,128)(2,1)S(1)}, u32[]{:S(2)}, u32[]{:S(2)}) %collective-permute-start.14) | collective-permute-done | bytes 147488 | tf_op jit(solution)/shard_map/ppermute | solution.py:60
  63.1 12.0 %collective-permute-done.10 = bf16[2,2,48,768]{3,2,1,0:T(8,128)(2,1)S(1)} collective-permute-done((bf16[2,2,48,768]{3,2,1,0:T(8,128)(2,1)S(1)}, bf16[2,2,48,768]{3,2,1,0:T(8,128)(2,1)S(1)}, u32[]{:S(2)}, u32[]{:S(2)}) %collective-permute-start.10) | collective-permute-done | bytes 294944 | tf_op jit(solution)/shard_map/ppermute | solution.py:60
  90.1 2.9 convolution_convert_fusion
  93.0 6.3 %reshape.270 = bf16[3,256,3,6,64]{4,3,2,1,0:T(8,128)(2,1)} reshape(bf16[768,1152]{1,0:T(8,128)(2,1)} %convolution_convert_fusion) | data formatting | bytes 3538944 | tf_op jit(solution)/shard_map/reshape | solution.py:188
  99.3 4.9 %fusion.109 = (bf16[3,256,1,6,64]{4,3,2,1,0:T(8,128)(2,1)}, bf16[3,256,1,6,64]{4,3,2,1,0:T(8,128)(2,1)}, bf16[3,256,1,6,64]{4,3,2,1,0:T(8,128)(2,1)}) fusion(bf16[3,256,3,6,64]{4,3,2,1,0:T(8,128)(2,1)} %reshape.270), kind=kLoop, calls=%fused_computation.312 | loop fusion | bytes 3538944 | tf_op jit(solution)/shard_map/slice | solution.py:189
  106.1 2.5 copy.144
  128.2 5.6 %collective-permute-done.17 = bf16[2,2,2,48,768]{4,3,2,1,0:T(8,128)(2,1)S(1)} collective-permute-done((bf16[2,2,2,48,768]{4,3,2,1,0:T(8,128)(2,1)S(1)}, bf16[2,2,2,48,768]{4,3,2,1,0:T(8,128)(2,1)S(1)}, u32[]{:S(2)}, u32[]{:S(2)}) %collective-permute-start.17) | collective-permute-done | bytes 589856 | tf_op jit(solution)/shard_map/ppermute | solution.py:60
  140.9 2.9 convolution_convert_fusion.4
  143.8 5.3 %fusion.12 = bf16[768,1536]{1,0:T(8,128)(2,1)S(1)} fusion(f32[768,1536]{1,0:T(8,128)S(1)} %fusion.26, bf16[768,768]{1,0:T(8,128)(2,1)S(1)} %multiply_convert_fusion.4, bf16[768,768]{1,0:T(8,128)(2,1)S(1)} %bitcast.312, bf16[768,768]{1,0:T(8,128)(2,1)S(1)} %bitcast.310), kind=kOutput, calls=%fused_computation.17 | convolution fusion | flops 1840250880 | bytes 10616832 | tf_op jit(solution)/shard_map/dot_general | solution.py:131
  149.1 2.2 fusion.103
  160.6 11.4 %collective-permute-done.37 = bf16[2,2,2,48,768]{4,3,0,1,2:T(8,128)(2,1)S(1)} collective-permute-done((bf16[2,2,2,48,768]{4,3,0,1,2:T(8,128)(2,1)S(1)}, bf16[2,2,2,48,768]{4,3,0,1,2:T(8,128)(2,1)S(1)}, u32[]{:S(2)}, u32[]{:S(2)}) %collective-permute-start.37) | collective-permute-done | bytes 589856 | tf_op jit(solution)/shard_map/ppermute | solution.py:60
  174.4 7.4 %collective-permute-done.31 = bf16[2,2,2,48,768]{4,3,0,1,2:T(8,128)(2,1)S(1)} collective-permute-done((bf16[2,2,2,48,768]{4,3,0,1,2:T(8,128)(2,1)S(1)}, bf16[2,2,2,48,768]{4,3,0,1,2:T(8,128)(2,1)S(1)}, u32[]{:S(2)}, u32[]{:S(2)}) %collective-permute-start.31) | collective-permute-done | bytes 589856 | tf_op jit(solution)/shard_map/ppermute | solution.py:60
  183.7 3.9 %collective-permute-done.29 = bf16[2,2,2,48,768]{4,3,0,1,2:T(8,128)(2,1)S(1)} collective-permute-done((bf16[2,2,2,48,768]{4,3,0,1,2:T(8,128)(2,1)S(1)}, bf16[2,2,2,48,768]{4,3,0,1,2:T(8,128)(2,1)S(1)}, u32[]{:S(2)}, u32[]{:S(2)}) %collective-permute-start.29) | collective-permute-done | bytes 589856 | tf_op jit(solution)/shard_map/ppermute | solution.py:60
  194.4 3.1 %collective-permute-done.30 = bf16[2,2,48,768]{3,2,0,1:T(8,128)(2,1)S(1)} collective-permute-done((bf16[2,2,48,768]{3,2,0,1:T(8,128)(2,1)S(1)}, bf16[2,2,48,768]{3,2,0,1:T(8,128)(2,1)S(1)}, u32[]{:S(2)}, u32[]{:S(2)}) %collective-permute-start.30) | collective-permute-done | bytes 294944 | tf_op jit(solution)/shard_map/ppermute | solution.py:60
  200.6 3.7 %add_convert_fusion = (bf16[768,768]{1,0:T(8,128)(2,1)}, f32[768,768]{1,0:T(8,128)}, f32[768]{0:T(1024)S(1)}, f32[768,768]{1,0:T(8,128)}) fusion(bf16[1,3,256,768]{3,2,1,0:T(8,128)(2,1)S(1)} %pad_maximum_fusion.10, f32[768]{0:T(1024)S(1)} %mul.281, f32[768,768]{1,0:T(8,128)S(1)} %get-tuple-element.47, f32[768]{0:T(1024)S(1)} %multiply_multiply_fusion.3, ...), kind=kLoop, calls=%fused_computation.45 | loop fusion | flops 12385536 | bytes 16530432 | tf_op jit(solution)/shard_map/convert_element_type | solution.py:222
  206.8 2.2 convolution_convert_fusion.6
  210.8 2.2 copy.110
  213.0 3.3 %fusion.36 = bf16[3,256,6,64]{1,3,2,0:T(8,128)(2,1)S(1)} fusion(bf16[3,256,6,64]{1,3,2,0:T(8,128)(2,1)S(1)} %copy.110, f32[3,6,256,256]{2,3,1,0:T(8,128)} %copy-done.13, f32[3,6,256]{2,1,0:T(8,128)} %copy-done.52), kind=kOutput, calls=%fused_computation.101 | convolution fusion | flops 153649152 | bytes 5916672 | tf_op jit(solution)/shard_map/bhqk,bqhd->bkhd/dot_general | solution.py:231
  216.4 3.3 %multiply_reduce_fusion = (f32[3,6,256]{2,1,0:T(8,128)S(1)}, f32[3,6,256,256]{2,3,1,0:T(8,128)S(1)}) fusion(f32[3,6,256,256]{2,3,1,0:T(8,128)} %copy-done.13, f32[3,6,256]{2,1,0:T(8,128)S(1)} %copy-done.53, bf16[3,256,6,64]{1,3,2,0:T(8,128)(2,1)S(1)} %copy.110, bf16[3,256,1,6,64]{1,4,3,0,2:T(8,128)(2,1)S(1)} %copy-done.37), kind=kOutput, calls=%fused_computation.20 | convolution fusion | flops 154529280 | bytes 10653696 | tf_op jit(solution)/shard_map/bqhd,bkhd->bhqk/dot_general | solution.py:226
  238.1 2.3 collective-permute-start.34
  240.4 8.2 %collective-permute-done.40 = bf16[48,1536]{1,0:T(8,128)(2,1)S(1)} collective-permute-done((bf16[48,1536]{1,0:T(8,128)(2,1)S(1)}, bf16[48,1536]{1,0:T(8,128)(2,1)S(1)}, u32[]{:S(2)}, u32[]{:S(2)}) %collective-permute-start.40) | collective-permute-done | bytes 147488 | tf_op jit(solution)/shard_map/ppermute | solution.py:60
  261.1 11.5 %collective-permute-done.25 = bf16[2,2,2,48,896]{4,3,0,1,2:T(8,128)(2,1)S(1)} collective-permute-done((bf16[2,2,2,48,896]{4,3,0,1,2:T(8,128)(2,1)S(1)}, bf16[2,2,2,48,896]{4,3,0,1,2:T(8,128)(2,1)S(1)}, u32[]{:S(2)}, u32[]{:S(2)}) %collective-permute-start.25) | collective-permute-done | bytes 688160 | tf_op jit(solution)/shard_map/ppermute | solution.py:60
  274.0 7.0 %collective-permute-done.26 = bf16[2,2,48,896]{3,2,0,1:T(8,128)(2,1)S(1)} collective-permute-done((bf16[2,2,48,896]{3,2,0,1:T(8,128)(2,1)S(1)}, bf16[2,2,48,896]{3,2,0,1:T(8,128)(2,1)S(1)}, u32[]{:S(2)}, u32[]{:S(2)}) %collective-permute-start.26) | collective-permute-done | bytes 344096 | tf_op jit(solution)/shard_map/ppermute | solution.py:60
  281.3 6.8 %convert_select_fusion.1 = bf16[3,2048,384]{2,1,0:T(8,128)(2,1)} fusion(bf16[3,2048,384]{2,1,0:T(8,128)(2,1)} %param.12, pred[3,2048]{1,0:T(4,128)(4,1)S(1)} %copy-done.60, bf16[3,256,384]{2,1,0:T(8,128)(2,1)S(1)} %bitcast.319, s32[3,256]{1,0:T(4,128)S(1)} %copy-done.57), kind=kOutput, calls=%fused_computation.21 | convolution fusion | flops 1214251008 | bytes 10036224 | tf_op jit(solution)/shard_map/bts,btd->bsd/dot_general | solution.py:253
  289.9 3.8 %convert_select_fusion = bf16[3,2048,384]{2,1,0:T(8,128)(2,1)} fusion(bf16[3,2048,384]{2,1,0:T(8,128)(2,1)S(1)} %bitcast.326, pred[3,2048]{1,0:T(4,128)(4,1)S(1)} %copy-done.60, bf16[3,256,384]{2,1,0:T(8,128)(2,1)S(1)} %bitcast.318, s32[3,256]{1,0:T(4,128)S(1)} %copy-done.57), kind=kOutput, calls=%fused_computation.18 | convolution fusion | flops 1214251008 | bytes 10036224 | tf_op jit(solution)/shard_map/bts,btd->bsd/dot_general | solution.py:253
  293.8 2.5 collective-permute-done.28
  (371 shorter events, 134.3 us)
Async XLA Ops:
  6.4 16.3 %collective-permute-start.1 = (bf16[48,1664]{1,0:T(8,128)(2,1)S(1)}, bf16[48,1664]{1,0:T(8,128)(2,1)S(1)}, u32[]{:S(2)}, u32[]{:S(2)}) collective-permute-start(bf16[48,1664]{1,0:T(8,128)(2,1)S(1)} %constant_dynamic-update-slice_fusion), channel_id=1, source_target_pairs={{0,16},{2,18},{4,20},{6,22},{8,24},{10,26},{12,28},{14,30},{16,0},... | collective-permute-start | bytes 479240 | tf_op jit(solution)/shard_map/ppermute | solution.py:60
  17.8 42.6 %collective-permute-start = (bf16[2,3,256,384]{3,2,1,0:T(8,128)(2,1)}, bf16[2,3,256,384]{3,2,1,0:T(8,128)(2,1)S(1)}, u32[]{:S(2)}, u32[]{:S(2)}) collective-permute-start(bf16[2,3,256,384]{3,2,1,0:T(8,128)(2,1)} %pad_maximum_fusion.11), channel_id=1, source_target_pairs={{0,1},{1,0},{2,3},{3,2},{4,5},{5,4},{6,7},{7,6},{8,9},{9,8},{10,11... | collective-permute-start | bytes 3538952 | tf_op jit(solution)/shard_map/ppermute | solution.py:116
  22.9 10.0 %collective-permute-start.2 = (bf16[2,48,1664]{2,1,0:T(8,128)(2,1)S(1)}, bf16[2,48,1664]{2,1,0:T(8,128)(2,1)S(1)}, u32[]{:S(2)}, u32[]{:S(2)}) collective-permute-start(bf16[2,48,1664]{2,1,0:T(8,128)(2,1)S(1)} %pad_maximum_fusion.22), channel_id=1, source_target_pairs={{0,8},{2,10},{4,12},{6,14},{8,0},{10,2},{12,4},{14,6},{16,24},{18,... | collective-permute-start | bytes 958472 | tf_op jit(solution)/shard_map/ppermute | solution.py:60
  33.0 9.6 %collective-permute-start.8 = (bf16[48,1536]{1,0:T(8,128)(2,1)S(1)}, bf16[48,1536]{1,0:T(8,128)(2,1)S(1)}, u32[]{:S(2)}, u32[]{:S(2)}) collective-permute-start(bf16[48,1536]{1,0:T(8,128)(2,1)S(1)} %shard_map.187), channel_id=1, source_target_pairs={{0,16},{2,18},{4,20},{6,22},{8,24},{10,26},{12,28},{14,30},{16,0},... | collective-permute-start | bytes 442376 | tf_op jit(solution)/shard_map/ppermute | solution.py:60
  42.8 39.4 %collective-permute-start.6 = (bf16[2,2,2,48,768]{4,3,2,1,0:T(8,128)(2,1)S(1)}, bf16[2,2,2,48,768]{4,3,2,1,0:T(8,128)(2,1)S(1)}, u32[]{:S(2)}, u32[]{:S(2)}) collective-permute-start(bf16[2,2,2,48,768]{4,3,2,1,0:T(8,128)(2,1)S(1)} %pad_maximum_fusion.17), channel_id=1, source_target_pairs={{0,4},{2,6},{4,0},{6,2},{8,12},{10,14},{12,8},{14,10},{16,20},{18,... | collective-permute-start | bytes 1769480 | tf_op jit(solution)/shard_map/ppermute | solution.py:60
  52.2 30.9 %collective-permute-start.4 = (bf16[2,2,2,48,896]{4,3,2,1,0:T(8,128)(2,1)S(1)}, bf16[2,2,2,48,896]{4,3,2,1,0:T(8,128)(2,1)S(1)}, u32[]{:S(2)}, u32[]{:S(2)}) collective-permute-start(bf16[2,2,2,48,896]{4,3,2,1,0:T(8,128)(2,1)S(1)} %pad_maximum_fusion.16), channel_id=1, source_target_pairs={{0,2},{2,0},{4,6},{6,4},{8,10},{10,8},{12,14},{14,12},{16,18},{18,... | collective-permute-start | bytes 2064392 | tf_op jit(solution)/shard_map/ppermute | solution.py:60
  53.8 21.3 %collective-permute-start.10 = (bf16[2,2,48,768]{3,2,1,0:T(8,128)(2,1)S(1)}, bf16[2,2,48,768]{3,2,1,0:T(8,128)(2,1)S(1)}, u32[]{:S(2)}, u32[]{:S(2)}) collective-permute-start(bf16[2,2,48,768]{3,2,1,0:T(8,128)(2,1)S(1)} %get-tuple-element.82), channel_id=1, source_target_pairs={{0,2},{2,0},{4,6},{6,4},{8,10},{10,8},{12,14},{14,12},{16,18},{18,... | collective-permute-start | bytes 884744 | tf_op jit(solution)/shard_map/ppermute | solution.py:60
  58.7 18.9 %collective-permute-start.12 = (bf16[2,2,48,768]{3,2,1,0:T(8,128)(2,1)S(1)}, bf16[2,2,48,768]{3,2,1,0:T(8,128)(2,1)S(1)}, u32[]{:S(2)}, u32[]{:S(2)}) collective-permute-start(bf16[2,2,48,768]{3,2,1,0:T(8,128)(2,1)S(1)} %get-tuple-element.83), channel_id=1, source_target_pairs={{0,4},{2,6},{4,0},{6,2},{8,12},{10,14},{12,8},{14,10},{16,20},{18,... | collective-permute-start | bytes 884744 | tf_op jit(solution)/shard_map/ppermute | solution.py:60
  60.4 20.5 %collective-permute-start.15 = (bf16[2,48,1536]{2,1,0:T(8,128)(2,1)S(1)}, bf16[2,48,1536]{2,1,0:T(8,128)(2,1)S(1)}, u32[]{:S(2)}, u32[]{:S(2)}) collective-permute-start(bf16[2,48,1536]{2,1,0:T(8,128)(2,1)S(1)} %pad_maximum_fusion.25), channel_id=1, source_target_pairs={{0,8},{2,10},{4,12},{6,14},{8,0},{10,2},{12,4},{14,6},{16,24},{18,... | collective-permute-start | bytes 884744 | tf_op jit(solution)/shard_map/ppermute | solution.py:60
  76.2 52.0 %collective-permute-start.11 = (bf16[2,2,2,48,768]{4,3,2,1,0:T(8,128)(2,1)}, bf16[2,2,2,48,768]{4,3,2,1,0:T(8,128)(2,1)}, u32[]{:S(2)}, u32[]{:S(2)}) collective-permute-start(bf16[2,2,2,48,768]{4,3,2,1,0:T(8,128)(2,1)} %pad_maximum_fusion.18), channel_id=1, source_target_pairs={{0,4},{2,6},{4,0},{6,2},{8,12},{10,14},{12,8},{14,10},{16,20},{18,... | collective-permute-start | bytes 1769480 | tf_op jit(solution)/shard_map/ppermute | solution.py:60
  79.3 55.9 %collective-permute-start.13 = (bf16[2,2,2,48,768]{4,3,2,1,0:T(8,128)(2,1)}, bf16[2,2,2,48,768]{4,3,2,1,0:T(8,128)(2,1)}, u32[]{:S(2)}, u32[]{:S(2)}) collective-permute-start(bf16[2,2,2,48,768]{4,3,2,1,0:T(8,128)(2,1)} %pad_maximum_fusion.19), channel_id=1, source_target_pairs={{0,2},{2,0},{4,6},{6,4},{8,10},{10,8},{12,14},{14,12},{16,18},{18,... | collective-permute-start | bytes 1769480 | tf_op jit(solution)/shard_map/ppermute | solution.py:60
  81.7 38.3 %collective-permute-start.16 = (bf16[2,2,48,768]{3,2,1,0:T(8,128)(2,1)}, bf16[2,2,48,768]{3,2,1,0:T(8,128)(2,1)}, u32[]{:S(2)}, u32[]{:S(2)}) collective-permute-start(bf16[2,2,48,768]{3,2,1,0:T(8,128)(2,1)} %get-tuple-element.88), channel_id=1, source_target_pairs={{0,2},{2,0},{4,6},{6,4},{8,10},{10,8},{12,14},{14,12},{16,18},{18,... | collective-permute-start | bytes 884744 | tf_op jit(solution)/shard_map/ppermute | solution.py:60
  82.3 40.6 %collective-permute-start.18 = (bf16[2,2,48,768]{3,2,1,0:T(8,128)(2,1)}, bf16[2,2,48,768]{3,2,1,0:T(8,128)(2,1)}, u32[]{:S(2)}, u32[]{:S(2)}) collective-permute-start(bf16[2,2,48,768]{3,2,1,0:T(8,128)(2,1)} %get-tuple-element.89), channel_id=1, source_target_pairs={{0,4},{2,6},{4,0},{6,2},{8,12},{10,14},{12,8},{14,10},{16,20},{18,... | collective-permute-start | bytes 884744 | tf_op jit(solution)/shard_map/ppermute | solution.py:60
  121.3 12.5 %collective-permute-start.17 = (bf16[2,2,2,48,768]{4,3,2,1,0:T(8,128)(2,1)S(1)}, bf16[2,2,2,48,768]{4,3,2,1,0:T(8,128)(2,1)S(1)}, u32[]{:S(2)}, u32[]{:S(2)}) collective-permute-start(bf16[2,2,2,48,768]{4,3,2,1,0:T(8,128)(2,1)S(1)} %pad_maximum_fusion.20), channel_id=1, source_target_pairs={{0,4},{2,6},{4,0},{6,2},{8,12},{10,14},{12,8},{14,10},{16,20},{18,... | collective-permute-start | bytes 1769480 | tf_op jit(solution)/shard_map/ppermute | solution.py:60
  124.0 12.2 %collective-permute-start.19 = (bf16[2,2,2,48,768]{4,3,2,1,0:T(8,128)(2,1)S(1)}, bf16[2,2,2,48,768]{4,3,2,1,0:T(8,128)(2,1)S(1)}, u32[]{:S(2)}, u32[]{:S(2)}) collective-permute-start(bf16[2,2,2,48,768]{4,3,2,1,0:T(8,128)(2,1)S(1)} %pad_maximum_fusion.21), channel_id=1, source_target_pairs={{0,2},{2,0},{4,6},{6,4},{8,10},{10,8},{12,14},{14,12},{16,18},{18,... | collective-permute-start | bytes 1769480 | tf_op jit(solution)/shard_map/ppermute | solution.py:60
  128.2 10.0 %collective-permute-start.7 = (bf16[768,768]{1,0:T(8,128)(2,1)S(1)}, bf16[768,768]{1,0:T(8,128)(2,1)S(1)}, u32[]{:S(2)}, u32[]{:S(2)}) collective-permute-start(bf16[768,768]{1,0:T(8,128)(2,1)S(1)} %convolution_convert_fusion.2), channel_id=1, source_target_pairs={{0,1},{1,0},{2,3},{3,2},{4,5},{5,4},{6,7},{7,6},{8,9},{9,8},{10,11... | collective-permute-start | bytes 3538952 | tf_op jit(solution)/shard_map/ppermute | solution.py:116
  155.9 16.1 %collective-permute-start.37 = (bf16[2,2,2,48,768]{4,3,0,1,2:T(8,128)(2,1)S(1)}, bf16[2,2,2,48,768]{4,3,0,1,2:T(8,128)(2,1)S(1)}, u32[]{:S(2)}, u32[]{:S(2)}) collective-permute-start(bf16[2,2,2,48,768]{4,3,0,1,2:T(8,128)(2,1)S(1)} %fusion.54), channel_id=1, source_target_pairs={{0,2},{2,0},{4,6},{6,4},{8,10},{10,8},{12,14},{14,12},{16,18},{18,... | collective-permute-start | bytes 1769480 | tf_op jit(solution)/shard_map/ppermute | solution.py:60
  157.5 16.3 %collective-permute-start.35 = (bf16[2,2,2,48,768]{4,3,0,1,2:T(8,128)(2,1)S(1)}, bf16[2,2,2,48,768]{4,3,0,1,2:T(8,128)(2,1)S(1)}, u32[]{:S(2)}, u32[]{:S(2)}) collective-permute-start(bf16[2,2,2,48,768]{4,3,0,1,2:T(8,128)(2,1)S(1)} %fusion.53), channel_id=1, source_target_pairs={{0,4},{2,6},{4,0},{6,2},{8,12},{10,14},{12,8},{14,10},{16,20},{18,... | collective-permute-start | bytes 1769480 | tf_op jit(solution)/shard_map/ppermute | solution.py:60
  159.0 40.2 %collective-permute-start.21 = (bf16[768,768]{1,0:T(8,128)(2,1)S(1)}, bf16[768,768]{1,0:T(8,128)(2,1)S(1)}, u32[]{:S(2)}, u32[]{:S(2)}) collective-permute-start(bf16[768,768]{1,0:T(8,128)(2,1)S(1)} %convolution_convert_fusion.3), channel_id=1, source_target_pairs={{0,1},{1,0},{2,3},{3,2},{4,5},{5,4},{6,7},{7,6},{8,9},{9,8},{10,11... | collective-permute-start | bytes 3538952 | tf_op jit(solution)/shard_map/ppermute | solution.py:116
  159.0 41.7 %collective-permute-start.20 = (bf16[768,768]{1,0:T(8,128)(2,1)S(1)}, bf16[768,768]{1,0:T(8,128)(2,1)S(1)}, u32[]{:S(2)}, u32[]{:S(2)}) collective-permute-start(bf16[768,768]{1,0:T(8,128)(2,1)S(1)} %convolution_convert_fusion.4), channel_id=1, source_target_pairs={{0,1},{1,0},{2,3},{3,2},{4,5},{5,4},{6,7},{7,6},{8,9},{9,8},{10,11... | collective-permute-start | bytes 3538952 | tf_op jit(solution)/shard_map/ppermute | solution.py:116
  159.9 21.9 %collective-permute-start.31 = (bf16[2,2,2,48,768]{4,3,0,1,2:T(8,128)(2,1)S(1)}, bf16[2,2,2,48,768]{4,3,0,1,2:T(8,128)(2,1)S(1)}, u32[]{:S(2)}, u32[]{:S(2)}) collective-permute-start(bf16[2,2,2,48,768]{4,3,0,1,2:T(8,128)(2,1)S(1)} %fusion.52), channel_id=1, source_target_pairs={{0,2},{2,0},{4,6},{6,4},{8,10},{10,8},{12,14},{14,12},{16,18},{18,... | collective-permute-start | bytes 1769480 | tf_op jit(solution)/shard_map/ppermute | solution.py:60
  171.9 15.7 %collective-permute-start.29 = (bf16[2,2,2,48,768]{4,3,0,1,2:T(8,128)(2,1)S(1)}, bf16[2,2,2,48,768]{4,3,0,1,2:T(8,128)(2,1)S(1)}, u32[]{:S(2)}, u32[]{:S(2)}) collective-permute-start(bf16[2,2,2,48,768]{4,3,0,1,2:T(8,128)(2,1)S(1)} %fusion.51), channel_id=1, source_target_pairs={{0,4},{2,6},{4,0},{6,2},{8,12},{10,14},{12,8},{14,10},{16,20},{18,... | collective-permute-start | bytes 1769480 | tf_op jit(solution)/shard_map/ppermute | solution.py:60
  173.8 17.0 %collective-permute-start.38 = (bf16[2,2,48,768]{3,2,0,1:T(8,128)(2,1)S(1)}, bf16[2,2,48,768]{3,2,0,1:T(8,128)(2,1)S(1)}, u32[]{:S(2)}, u32[]{:S(2)}) collective-permute-start(bf16[2,2,48,768]{3,2,0,1:T(8,128)(2,1)S(1)} %fusion.82), channel_id=1, source_target_pairs={{0,4},{2,6},{4,0},{6,2},{8,12},{10,14},{12,8},{14,10},{16,20},{18,... | collective-permute-start | bytes 884744 | tf_op jit(solution)/shard_map/ppermute | solution.py:60
  181.8 9.6 %collective-permute-start.36 = (bf16[2,2,48,768]{3,2,0,1:T(8,128)(2,1)S(1)}, bf16[2,2,48,768]{3,2,0,1:T(8,128)(2,1)S(1)}, u32[]{:S(2)}, u32[]{:S(2)}) collective-permute-start(bf16[2,2,48,768]{3,2,0,1:T(8,128)(2,1)S(1)} %fusion.81), channel_id=1, source_target_pairs={{0,2},{2,0},{4,6},{6,4},{8,10},{10,8},{12,14},{14,12},{16,18},{18,... | collective-permute-start | bytes 884744 | tf_op jit(solution)/shard_map/ppermute | solution.py:60
  192.3 42.2 %collective-permute-start.39 = (bf16[2,48,1536]{2,1,0:T(8,128)(2,1)}, bf16[2,48,1536]{2,1,0:T(8,128)(2,1)}, u32[]{:S(2)}, u32[]{:S(2)}) collective-permute-start(bf16[2,48,1536]{2,1,0:T(8,128)(2,1)} %fusion.85), channel_id=1, source_target_pairs={{0,8},{2,10},{4,12},{6,14},{8,0},{10,2},{12,4},{14,6},{16,24},{18,... | collective-permute-start | bytes 884744 | tf_op jit(solution)/shard_map/ppermute | solution.py:60
  198.4 37.9 %collective-permute-start.33 = (bf16[2,48,1536]{2,1,0:T(8,128)(2,1)}, bf16[2,48,1536]{2,1,0:T(8,128)(2,1)}, u32[]{:S(2)}, u32[]{:S(2)}) collective-permute-start(bf16[2,48,1536]{2,1,0:T(8,128)(2,1)} %fusion.84), channel_id=1, source_target_pairs={{0,8},{2,10},{4,12},{6,14},{8,0},{10,2},{12,4},{14,6},{16,24},{18,... | collective-permute-start | bytes 884744 | tf_op jit(solution)/shard_map/ppermute | solution.py:60
  229.5 21.3 %collective-permute-start.22 = (bf16[768,768]{1,0:T(8,128)(2,1)S(1)}, bf16[768,768]{1,0:T(8,128)(2,1)S(1)}, u32[]{:S(2)}, u32[]{:S(2)}) collective-permute-start(bf16[768,768]{1,0:T(8,128)(2,1)S(1)} %convolution_convert_fusion.1), channel_id=1, source_target_pairs={{0,1},{1,0},{2,3},{3,2},{4,5},{5,4},{6,7},{7,6},{8,9},{9,8},{10,11... | collective-permute-start | bytes 3538952 | tf_op jit(solution)/shard_map/ppermute | solution.py:116
  231.0 18.4 %collective-permute-start.23 = (bf16[2,2,2,48,768]{4,3,0,1,2:T(8,128)(2,1)S(1)}, bf16[2,2,2,48,768]{4,3,0,1,2:T(8,128)(2,1)S(1)}, u32[]{:S(2)}, u32[]{:S(2)}) collective-permute-start(bf16[2,2,2,48,768]{4,3,0,1,2:T(8,128)(2,1)S(1)} %fusion.50), channel_id=1, source_target_pairs={{0,4},{2,6},{4,0},{6,2},{8,12},{10,14},{12,8},{14,10},{16,20},{18,... | collective-permute-start | bytes 1769480 | tf_op jit(solution)/shard_map/ppermute | solution.py:60
  235.6 13.0 %collective-permute-start.40 = (bf16[48,1536]{1,0:T(8,128)(2,1)S(1)}, bf16[48,1536]{1,0:T(8,128)(2,1)S(1)}, u32[]{:S(2)}, u32[]{:S(2)}) collective-permute-start(bf16[48,1536]{1,0:T(8,128)(2,1)S(1)} %fusion.92), channel_id=1, source_target_pairs={{0,16},{2,18},{4,20},{6,22},{8,24},{10,26},{12,28},{14,30},{16,0},... | collective-permute-start | bytes 442376 | tf_op jit(solution)/shard_map/ppermute | solution.py:60
  238.1 18.5 %collective-permute-start.34 = (bf16[48,1536]{1,0:T(8,128)(2,1)}, bf16[48,1536]{1,0:T(8,128)(2,1)}, u32[]{:S(2)}, u32[]{:S(2)}) collective-permute-start(bf16[48,1536]{1,0:T(8,128)(2,1)} %fusion.91), channel_id=1, source_target_pairs={{0,16},{2,18},{4,20},{6,22},{8,24},{10,26},{12,28},{14,30},{16,0},... | collective-permute-start | bytes 442376 | tf_op jit(solution)/shard_map/ppermute | solution.py:60
  250.3 9.5 %collective-permute-start.24 = (bf16[2,2,48,768]{3,2,0,1:T(8,128)(2,1)}, bf16[2,2,48,768]{3,2,0,1:T(8,128)(2,1)}, u32[]{:S(2)}, u32[]{:S(2)}) collective-permute-start(bf16[2,2,48,768]{3,2,0,1:T(8,128)(2,1)} %fusion.78), channel_id=1, source_target_pairs={{0,2},{2,0},{4,6},{6,4},{8,10},{10,8},{12,14},{14,12},{16,18},{18,... | collective-permute-start | bytes 884744 | tf_op jit(solution)/shard_map/ppermute | solution.py:60
  255.1 17.5 %collective-permute-start.25 = (bf16[2,2,2,48,896]{4,3,0,1,2:T(8,128)(2,1)S(1)}, bf16[2,2,2,48,896]{4,3,0,1,2:T(8,128)(2,1)S(1)}, u32[]{:S(2)}, u32[]{:S(2)}) collective-permute-start(bf16[2,2,2,48,896]{4,3,0,1,2:T(8,128)(2,1)S(1)} %fusion.44), channel_id=1, source_target_pairs={{0,2},{2,0},{4,6},{6,4},{8,10},{10,8},{12,14},{14,12},{16,18},{18,... | collective-permute-start | bytes 2064392 | tf_op jit(solution)/shard_map/ppermute | solution.py:60
  (77 other events, 440.2 us)

commit v3 on v2

v3 whole, which is shorter than its diff:
```python
import functools
import math

import jax
import jax.numpy as jnp
from jax import lax
from jax.experimental import pallas as pl
from jax.experimental.pallas import tpu as pltpu
from jax.sharding import PartitionSpec as P

HD = 64
EPSILON = 1e-06
BF = jnp.bfloat16
F32 = jnp.float32
VMEM_SPARE = 6 << 20


def mm(a, b):
    return jnp.dot(a, b, preferred_element_type=F32)


def mm_nt(a, b):
    return lax.dot_general(a, b, (((1,), (1,)), ((), ())), preferred_element_type=F32)


def mm_tn(a, b):
    return lax.dot_general(a, b, (((0,), (0,)), ((), ())), preferred_element_type=F32)


def inverse_rms(values):
    return lax.rsqrt(jnp.mean(values * values, axis=-1, keepdims=True) + EPSILON)


def call(kernel, outs, args, after=(), flops=0, name=None):
    moved = sum(v.size * v.dtype.itemsize for v in (*args, *outs))

    def body(*refs):
        kernel(*refs[: len(args)], *refs[len(args) + len(after) :])

    return pl.pallas_call(
        body,
        out_shape=outs,
        in_specs=[pl.BlockSpec(memory_space=pltpu.VMEM)] * len(args)
        + [pl.BlockSpec(memory_space=pl.ANY)] * len(after),
        out_specs=[pl.BlockSpec(memory_space=pltpu.VMEM)] * len(outs),
        compiler_params=pltpu.CompilerParams(vmem_limit_bytes=moved + VMEM_SPARE),
        cost_estimate=pl.CostEstimate(flops=flops, bytes_accessed=moved, transcendentals=0),
        name=name,
    )(*args, *after)


def shape(dims, dtype=BF):
    return jax.ShapeDtypeStruct(tuple(dims), dtype)


def first_head(width=2 * HD):
    return lax.broadcasted_iota(jnp.int32, (1, width), 1) < HD


def attention_forward(rows, sel, states_ref, weights_ref, bias_ref, normed_ref, packed_ref, probs_ref, context_ref, gains_ref):
    width = states_ref.shape[1]
    half = context_ref.shape[1]
    gains_ref[...] = weights_ref[:, 3 * half :].astype(F32).T[:8]
    gain = gains_ref[0:1, :]
    scale = HD ** (-0.5)

    @pl.loop(0, rows)
    def _(row):
        here = pl.ds(pl.multiple_of(row * sel, sel), sel)
        states = states_ref[here, :].astype(F32)
        normed = (states * inverse_rms(states) * gain).astype(BF)
        normed_ref[here, :] = normed
        packed_ref[here, :] = mm(normed, weights_ref[:, : 3 * half]).astype(BF)
        bias = bias_ref[row]
        first = first_head()
        for pair in range(half // (2 * HD)):
            at = pair * 2 * HD
            queries = packed_ref[here, at : at + 2 * HD]
            keys = packed_ref[here, half + at : half + at + 2 * HD]
            vals = packed_ref[here, 2 * half + at : 2 * half + at + 2 * HD]
            found = []
            for head in range(2):
                mine = first if head == 0 else ~first
                scores = mm_nt(jnp.where(mine, queries, jnp.zeros_like(queries)), keys) * scale + bias
                exponent = jnp.exp(scores - jnp.max(scores, axis=-1, keepdims=True))
                probs = exponent / jnp.sum(exponent, axis=-1, keepdims=True)
                probs_ref[row, 2 * pair + head] = probs
                found.append(mm(probs.astype(BF), vals))
            context_ref[here, at : at + 2 * HD] = jnp.where(first, found[0], found[1]).astype(BF)


def mix_forward(context_ref, mix_ref, out_ref):
    out_ref[...] = mm_nt(context_ref[...], mix_ref[...]).astype(BF)


def up_forward(
    rows, sel, states_ref, upstream_ref, own_ref, other_ref, up_ref, gains_ref, keep_ref,
    normed_ref, activated_ref, slope_ref, feed_grad_ref, grad_ref,
):
    mid_gain, router = gains_ref[1:2, :], gains_ref[2:3, :]
    c, a = (2.0 / math.pi) ** 0.5, 0.044715

    @pl.loop(0, rows)
    def _(row):
        here = pl.ds(pl.multiple_of(row * sel, sel), sel)
        states = states_ref[here, :].astype(F32)
        prob = jax.nn.sigmoid(jnp.sum(states * router, axis=-1, keepdims=True))
        gate = prob * keep_ref[here, :]
        feed_grad_ref[here, :] = (gate * upstream_ref[here, :].astype(F32)).astype(BF)
        middle = states + (own_ref[here, :].astype(F32) + other_ref[here, :].astype(F32))
        normed = (middle * inverse_rms(middle) * mid_gain).astype(BF)
        normed_ref[here, :] = normed
        chunk = 512
        for at in range(0, up_ref.shape[1], chunk):
            hidden = mm(normed, up_ref[:, at : at + chunk])
            square = hidden * hidden
            bent = jnp.tanh(c * hidden * (1.0 + a * square))
            activated_ref[here, at : at + chunk] = (0.5 * hidden * (1.0 + bent)).astype(BF)
            slope = 0.5 * (1.0 + bent) + 0.5 * c * hidden * (1.0 - bent * bent) * (1.0 + 3.0 * a * square)
            slope_ref[here, at : at + chunk] = slope.astype(BF)

    tall = 256
    for at in range(0, grad_ref.shape[0], tall):
        grad_ref[at : at + tall, :] = mm_tn(feed_grad_ref[:, at : at + tall], activated_ref[...]).astype(BF)


def down_backward(rows, sel, feed_grad_ref, down_ref, slope_ref, up_ref, hidden_grad_ref, out_ref):
    @pl.loop(0, rows)
    def _(row):
        here = pl.ds(pl.multiple_of(row * sel, sel), sel)
        feed_grad = feed_grad_ref[here, :]
        chunk = 512
        for at in range(0, down_ref.shape[1], chunk):
            act_grad = mm(feed_grad, down_ref[:, at : at + chunk])
            hidden_grad_ref[here, at : at + chunk] = (
                act_grad * slope_ref[here, at : at + chunk].astype(F32)
            ).astype(BF)
        out_ref[here, :] = mm_nt(hidden_grad_ref[here, :], up_ref[...]).astype(BF)


def down_forward(normed_ref, hidden_grad_ref, activated_ref, down_ref, grad_ref, out_ref):
    tall = 256
    for at in range(0, grad_ref.shape[0], tall):
        grad_ref[at : at + tall, :] = mm_tn(normed_ref[:, at : at + tall], hidden_grad_ref[...]).astype(BF)
    for at in range(0, out_ref.shape[0], tall):
        out_ref[at : at + tall, :] = mm_nt(activated_ref[at : at + tall, :], down_ref[...]).astype(BF)


def norm_backward(values, grads, gain):
    rho = inverse_rms(values)
    unit = values * rho
    scaled = grads * gain
    back = rho * (scaled - unit * jnp.mean(scaled * unit, axis=-1, keepdims=True))
    return back, jnp.sum(grads * unit, axis=0, keepdims=True)


def attention_backward(
    rows, sel, states_ref, own_ref, other_ref, mid_own_ref, mid_other_ref, upstream_ref, keep_ref, gains_ref,
    mix_ref, weights_ref, packed_ref, probs_ref,
    mixed_ref, packed_grad_ref, out_ref, middle_grad_ref, gain_grad_ref,
):
    mid_gain, router = gains_ref[1:2, :], gains_ref[2:3, :]
    half = mix_ref.shape[1]
    scale = HD ** (-0.5)
    gain_grad_ref[...] = jnp.zeros_like(gain_grad_ref)

    @pl.loop(0, rows)
    def _(row):
        here = pl.ds(pl.multiple_of(row * sel, sel), sel)
        states = states_ref[here, :].astype(F32)
        middle = states + (own_ref[here, :].astype(F32) + other_ref[here, :].astype(F32))
        mid_in = mid_own_ref[here, :].astype(F32) + mid_other_ref[here, :].astype(F32)
        middle_grad, gain_grad = norm_backward(middle, mid_in, mid_gain)
        gain_grad_ref[0:1, :] += gain_grad
        middle_grad_ref[here, :] = middle_grad
        gate = jax.nn.sigmoid(jnp.sum(states * router, axis=-1, keepdims=True)) * keep_ref[here, :]
        mixed = (gate * upstream_ref[here, :].astype(F32) + middle_grad).astype(BF)
        mixed_ref[here, :] = mixed
        context_grad = mm(mixed, mix_ref[...]).astype(BF)
        first = first_head()
        for pair in range(half // (2 * HD)):
            at = pair * 2 * HD
            queries = packed_ref[here, at : at + 2 * HD]
            keys = packed_ref[here, half + at : half + at + 2 * HD]
            vals = packed_ref[here, 2 * half + at : 2 * half + at + 2 * HD]
            grads = context_grad[:, at : at + 2 * HD]
            by_query, by_key, by_value = [], [], []
            for head in range(2):
                mine = first if head == 0 else ~first
                probs = probs_ref[row, 2 * pair + head]
                prob_grad = mm_nt(jnp.where(mine, grads, jnp.zeros_like(grads)), vals)
                centre = jnp.sum(probs * prob_grad, axis=-1, keepdims=True)
                score_grad = (probs * (prob_grad - centre)).astype(BF)
                by_query.append(mm(score_grad, keys))
                by_key.append(mm_tn(score_grad, queries))
                by_value.append(mm_tn(probs.astype(BF), grads))
            packed_grad_ref[here, at : at + 2 * HD] = (
                jnp.where(first, by_query[0], by_query[1]) * scale
            ).astype(BF)
            packed_grad_ref[here, half + at : half + at + 2 * HD] = (
                jnp.where(first, by_key[0], by_key[1]) * scale
            ).astype(BF)
            packed_grad_ref[here, 2 * half + at : 2 * half + at + 2 * HD] = jnp.where(
                first, by_value[0], by_value[1]
            ).astype(BF)
        out_ref[here, :] = mm_nt(packed_grad_ref[here, :], weights_ref[:, : 3 * half]).astype(BF)


def projection_grads(normed_ref, packed_grad_ref, mixed_ref, context_ref, grad_ref):
    tall = 256
    wide = packed_grad_ref.shape[1]
    for at in range(0, grad_ref.shape[0], tall):
        grad_ref[at : at + tall, :wide] = mm_tn(normed_ref[:, at : at + tall], packed_grad_ref[...]).astype(BF)
        grad_ref[at : at + tall, wide:] = mm_tn(mixed_ref[:, at : at + tall], context_ref[...]).astype(BF)


def final_forward(
    rows, sel, states_ref, upstream_ref, own_ref, other_ref, feed_own_ref, feed_other_ref, gains_ref, keep_ref,
    finished_ref, logit_grad_ref, router_grad_ref,
):
    router = gains_ref[2:3, :]
    router_grad_ref[...] = jnp.zeros_like(router_grad_ref)

    @pl.loop(0, rows)
    def _(row):
        here = pl.ds(pl.multiple_of(row * sel, sel), sel)
        states = states_ref[here, :].astype(F32)
        attended = own_ref[here, :].astype(F32) + other_ref[here, :].astype(F32)
        branch = attended + (feed_own_ref[here, :].astype(F32) + feed_other_ref[here, :].astype(F32))
        prob = jax.nn.sigmoid(jnp.sum(states * router, axis=-1, keepdims=True))
        keep = keep_ref[here, :]
        finished_ref[here, :] = (states + prob * keep * branch).astype(BF)
        gate_grad = jnp.sum(upstream_ref[here, :].astype(F32) * branch, axis=-1, keepdims=True)
        logit_grad = gate_grad * keep * prob * (1.0 - prob)
        logit_grad_ref[here, :] = logit_grad
        router_grad_ref[0:1, :] += jnp.sum(logit_grad * states, axis=0, keepdims=True)


def final_backward(
    rows, sel, states_ref, upstream_ref, middle_grad_ref, pre_own_ref, pre_other_ref, logit_grad_ref, gains_ref,
    total_ref, gain_grad_ref,
):
    pre_gain, router = gains_ref[0:1, :], gains_ref[2:3, :]
    gain_grad_ref[...] = jnp.zeros_like(gain_grad_ref)

    @pl.loop(0, rows)
    def _(row):
        here = pl.ds(pl.multiple_of(row * sel, sel), sel)
        states = states_ref[here, :].astype(F32)
        pre_in = pre_own_ref[here, :].astype(F32) + pre_other_ref[here, :].astype(F32)
        back, gain_grad = norm_backward(states, pre_in, pre_gain)
        gain_grad_ref[0:1, :] += gain_grad
        total = upstream_ref[here, :].astype(F32) + logit_grad_ref[here, :] * router
        total_ref[here, :] = (total + middle_grad_ref[here, :] + back).astype(BF)


def untouched(*refs):
    pass


def tie(value, *others):
    if not others:
        return value
    anywhere = pl.BlockSpec(memory_space=pl.ANY)
    return pl.pallas_call(
        untouched,
        out_shape=jax.ShapeDtypeStruct(value.shape, value.dtype),
        in_specs=[anywhere] * (1 + len(others)),
        out_specs=anywhere,
        input_output_aliases={0: 0},
        compiler_params=pltpu.CompilerParams(vmem_limit_bytes=1 << 20),
        cost_estimate=pl.CostEstimate(flops=0, bytes_accessed=0, transcendentals=0),
    )(value, *others)


class Cube:
    def __init__(self, count):
        self.count, self.bits = count, count.bit_length() - 1
        self.index = lax.axis_index("dp").astype(jnp.uint32)
        short = self.bits // 3
        self.x, self.y = list(range(short)), list(range(short, 2 * short))
        self.z = list(range(2 * short, self.bits))

    def swap(self, value, bit):
        return lax.ppermute(value, "dp", [(i, i ^ (1 << bit)) for i in range(self.count)])

    def low(self, bit):
        return (self.index >> bit) % 2 == 0

    def double(self, value, bit, after=()):
        other, low = tie(self.swap(value, bit), *after), self.low(bit)
        return jnp.stack([jnp.where(low, value, other), jnp.where(low, other, value)])

    def halve(self, value, axis, bit, after=()):
        own = ((self.index >> bit) % 2).astype(jnp.int32)
        mine = lax.dynamic_index_in_dim(value, own, axis, keepdims=False)
        sent = lax.dynamic_index_in_dim(value, 1 - own, axis, keepdims=False)
        return mine.astype(F32) + tie(self.swap(sent.astype(BF), bit), *after).astype(F32)


def halves(width):
    return width // 2 // 128 * 128


def gather_z(cube, own, after=()):
    column = tie(own, *after)
    for bit in cube.z[::-1]:
        column = cube.double(column, bit)
    return column


def gather_first(cube, column):
    cut = halves(column.shape[-1])
    parts = []
    for part, order in ((column[..., :cut], cube.x), (column[..., cut:], cube.y)):
        for bit in order:
            part = cube.double(part, bit)
        parts.append(part)
    return parts


def gather_second(cube, parts, after=()):
    done = []
    for part, before, order in zip(parts, (cube.x, cube.y), (cube.y, cube.x)):
        for bit in order:
            part = cube.double(part, bit, after)
        axes = order[::-1] + before[::-1] + cube.z
        bits = sorted(axes, reverse=True)
        part = part.transpose([axes.index(b) for b in bits] + [cube.bits, cube.bits + 1])
        done.append(part.reshape(-1, part.shape[-1]))
    return jnp.concatenate(done, axis=1)


def reduce_first(cube, total, after=()):
    cut = halves(total.shape[1])
    pieces = [(total[:, :cut], cube.y), (total[:, cut:], cube.x)] if cut else [(total, cube.y)]
    parts = []
    for part, order in pieces:
        part = part.reshape([2] * cube.bits + [-1, part.shape[1]])
        axes = list(range(cube.bits))[::-1]
        for bit in order:
            part = cube.halve(part, axes.index(bit), bit, after)
            axes.remove(bit)
        parts.append(part)
    return parts


def reduce_second(cube, parts, after=()):
    done = []
    for part, order, gone in zip(parts, (cube.x, cube.y), (cube.y, cube.x)):
        axes = [b for b in range(cube.bits)[::-1] if b not in gone]
        for bit in order:
            part = cube.halve(part, axes.index(bit), bit, after)
            axes.remove(bit)
        done.append(part)
    return jnp.concatenate(done, axis=-1)


def reduce_z(cube, part, after=()):
    axes = cube.z[::-1]
    for bit in cube.z:
        part = cube.halve(part, axes.index(bit), bit, after.pop(0) if after else ())
        axes.remove(bit)
    return part


def other_core(value):
    return lax.ppermute(value, "mp", [(0, 1), (1, 0)])


def both_halves(value):
    other = other_core(value)
    low = lax.axis_index("mp") == 0
    return jnp.concatenate([jnp.where(low, value, other), jnp.where(low, other, value)], axis=-1)


def shards(
    tokens,
    segments,
    present,
    chosen,
    attention,
    mixing,
    expand,
    contract,
    prenorm,
    midnorm,
    router,
    cotangent,
    count,
):
    cube = Cube(count)
    row_count, length, half_width = tokens.shape
    sel_count = chosen.shape[1]
    token_count = row_count * sel_count
    own_rows = mixing.shape[1]
    width = 2 * half_width
    hidden_here = expand.shape[1]
    heads_here = half_width // HD
    by_row = (row_count, sel_count)

    vectors = jnp.pad(jnp.stack([prenorm, midnorm, router], axis=1), ((0, 0), (0, 125)))
    first_own = jnp.concatenate([attention[0], attention[1], attention[2], vectors], axis=1)
    second_own = jnp.concatenate([mixing.T, expand], axis=1)
    first_z = gather_z(cube, first_own)
    second_z = gather_z(cube, second_own, [first_z])
    down_z = gather_z(cube, contract.T, [second_z])
    first = gather_second(cube, gather_first(cube, first_z))
    second_parts = gather_first(cube, second_z)
    second = gather_second(cube, second_parts)
    mix, up = second[:, :half_width], second[:, half_width:]
    down_parts = gather_first(cube, down_z)

    positions = jnp.arange(length, dtype=jnp.int32)
    hit = chosen[:, :, None] == positions[None, None, :]
    one_hot = hit.astype(BF)
    local_rows = jnp.einsum("bts,bsd->btd", one_hot, tokens, preferred_element_type=F32).astype(BF)
    local_grads = jnp.einsum("bts,bsd->btd", one_hot, cotangent, preferred_element_type=F32).astype(BF)
    seg_sel = jnp.sum(jnp.where(hit, segments[:, None, :], 0), axis=-1)
    keep_sel = jnp.sum(jnp.where(hit, present[:, None, :], 0), axis=-1).astype(F32)
    taken = jnp.any(hit, axis=1)[:, :, None]

    both = both_halves(jnp.stack([local_rows, local_grads]))
    states = both[0].reshape(token_count, width)
    upstream = both[1].reshape(token_count, width)
    keep = keep_sel.reshape(token_count, 1)
    slots = jnp.arange(sel_count)
    diagonal = slots[None, :] == slots[:, None]
    causal = slots[None, :] <= slots[:, None]
    same_doc = seg_sel[:, :, None] == seg_sel[:, None, :]
    open_key = (keep_sel[:, None, :] > 0) | diagonal[None]
    bias = jnp.where(causal[None] & same_doc & open_key, 0.0, -1e30).astype(F32)

    wide = shape((token_count, width))
    tall = shape((token_count, hidden_here))
    vector = shape((8, width), F32)
    normed, packed, probs, context, gains = call(
        functools.partial(attention_forward, *by_row),
        (
            wide,
            shape((token_count, 3 * half_width)),
            shape((row_count, heads_here, sel_count, sel_count), F32),
            shape((token_count, half_width)),
            vector,
        ),
        (states, first, bias),
        after=second_parts,
        flops=token_count * width * half_width * 6,
        name="attention_forward",
    )
    (att_own,) = call(
        mix_forward, (wide,), (context, mix), flops=2 * token_count * width * half_width, name="mix_forward"
    )
    att_other = other_core(att_own)
    normed_mid, activated, slope, feed_grad, down_grad = call(
        functools.partial(up_forward, *by_row),
        (wide, tall, tall, wide, shape((width, hidden_here))),
        (states, upstream, att_own, att_other, up, gains, keep),
        flops=4 * token_count * width * hidden_here,
        name="up_forward",
    )
    down = gather_second(cube, down_parts, [activated])

    hidden_grad, mid_own = call(
        functools.partial(down_backward, *by_row),
        (tall, wide),
        (feed_grad, down, slope, up),
        flops=4 * token_count * width * hidden_here,
        name="down_backward",
    )
    up_grad, feed_own = call(
        down_forward,
        (shape((width, hidden_here)), wide),
        (normed_mid, hidden_grad, activated, down),
        flops=4 * token_count * width * hidden_here,
        name="down_forward",
    )
    feed_other = other_core(feed_own)
    mid_other = tie(other_core(mid_own), feed_own)
    down_grads = reduce_first(cube, down_grad, [feed_own])

    mixed, packed_grad, pre_own, middle_grad, mid_gain_grad = call(
        functools.partial(attention_backward, *by_row),
        (
            wide,
            shape((token_count, 3 * half_width)),
            wide,
            shape((token_count, width), F32),
            vector,
        ),
        (states, att_own, att_other, mid_own, mid_other, upstream, keep, gains, mix, first, packed, probs),
        flops=10 * token_count * width * half_width,
        name="attention_backward",
    )
    down_part = reduce_second(cube, down_grads, [packed_grad])
    up_grads = reduce_first(cube, up_grad, [packed_grad])
    (first_grad,) = call(
        projection_grads,
        (shape((width, 4 * half_width)),),
        (normed, packed_grad, mixed, context),
        flops=8 * token_count * width * half_width,
        name="projection_grads",
    )
    pre_other = tie(other_core(pre_own), first_grad)
    finished, logit_grad, router_grad = call(
        functools.partial(final_forward, *by_row),
        (wide, shape((token_count, 1), F32), vector),
        (states, upstream, att_own, att_other, feed_own, feed_other, gains, keep),
        name="final_forward",
    )
    total_grad, pre_gain_grad = call(
        functools.partial(final_backward, *by_row),
        (wide, vector),
        (states, upstream, middle_grad, pre_own, pre_other, logit_grad, gains),
        name="final_backward",
    )
    up_part = reduce_second(cube, up_grads, [total_grad])
    vector_grads = jnp.concatenate([pre_gain_grad[:1], mid_gain_grad[:1], router_grad[:1]])
    vector_grads = jnp.pad(vector_grads.T, ((0, 0), (0, 125)))
    vector_half = reduce_first(cube, vector_grads)
    down_out = reduce_z(cube, down_part, [[total_grad], vector_half])
    first_grads = reduce_first(cube, first_grad, vector_half)
    vector_part = reduce_second(cube, vector_half)
    first_part = reduce_second(cube, first_grads, [vector_part])
    up_out = reduce_z(cube, up_part, [[vector_part], []])
    first_out = reduce_z(cube, jnp.concatenate([first_part, vector_part], axis=-1))

    offset = lax.axis_index("mp") * half_width

    def put(base, values):
        mine = lax.dynamic_slice_in_dim(values, offset, half_width, 1)
        mine = mine.reshape(row_count, sel_count, half_width)
        placed = jnp.einsum("bts,btd->bsd", one_hot, mine, preferred_element_type=F32).astype(BF)
        return jnp.where(taken, placed, base)

    attention_out = first_out[:, : 3 * half_width].reshape(own_rows, 3, half_width).transpose(1, 0, 2)
    vector_out = first_out[:, 4 * half_width : 4 * half_width + 3]
    return (
        put(tokens, tie(finished, *vector_half)),
        put(cotangent, total_grad),
        attention_out,
        first_out[:, 3 * half_width : 4 * half_width].T,
        up_out,
        down_out.T,
        vector_out[:, 0],
        vector_out[:, 1],
        vector_out[:, 2],
    )


def solution(mesh):
    in_specs = (
        P("dp", None, "mp"),
        P("dp", None),
        P("dp", None),
        P("dp", None),
        P(None, "dp", "mp"),
        P("mp", "dp"),
        P("dp", "mp"),
        P("mp", "dp"),
        P("dp"),
        P("dp"),
        P("dp"),
        P("dp", None, "mp"),
    )
    out_specs = (
        P("dp", None, "mp"),
        P("dp", None, "mp"),
        P(None, "dp", "mp"),
        P("mp", "dp"),
        P("dp", "mp"),
        P("mp", "dp"),
        P("dp"),
        P("dp"),
        P("dp"),
    )
    count = mesh.shape["dp"]

    def body(*args):
        return shards(*args, count)

    return jax.shard_map(body, mesh=mesh, in_specs=in_specs, out_specs=out_specs, check_vma=False)
```

time: 303 us -> 214 us (0.71); the launches traced: 299 us -> 214 us
  Pallas kernels: 0.01 us -> 40.8 us
  matrix products: 56.1 us -> 19.4 us
  local copies, waits for them, and re-layouts: 47.7 us -> 17.2 us
  other arithmetic: 46.2 us -> 17 us
  waiting for transfers between devices: 101 us -> 71.8 us
    pallas_call x0 -> x9, Pallas kernels: none -> 40.7 us  [call(): pl.pallas_call(body, out_shape=outs, in_specs=[pl.BlockSpec(memory_space=...]
    dot_general x18 -> x0, matrix products: 39.5 us -> none  [the longest x12 28.9 us: dot(): lax.dot_general(a, b, ((contract[:1], contract[1:]), ((), ())), preferred...]
    ppermute x36 -> x38, waiting for transfers between devices: 101 us -> 71.8 us  [swap(): lax.ppermute(value, 'dp', [(i, i ^ 1 << bit) for i in range(self.count)])]
    unnamed x152 -> x41, local copies, waits for them, and re-layouts: 18.2 us -> 7.27 us
    convert_element_type x12 -> x2, other arithmetic: 11 us -> 0.08 us  [halve(): sent.astype(BF)]
    reshape x3 -> x0, local copies, waits for them, and re-layouts: 10.3 us -> none  [the longest x1 6.32 us: shards(): shaped = packed.reshape(row_count, sel_count, 3, heads_here, HD)]
    another operation x31 -> x33, other arithmetic: 8.8 us -> 2.06 us  [double(): jnp.stack([jnp.where(low, value, other), jnp.where(low, other, value)])]
    slice x5 -> x7, local copies, waits for them, and re-layouts: 6.9 us -> 0.53 us  [the longest x2 0.31 us: reduce_first(): total[:, cut:]]
  transfers between devices with their start and end apart: 41 -> 43, of which waited for: 19 -> 16; matrix products, arithmetic and copies ran while one was open for 40% -> 20% of each run, Pallas kernels for 0% -> 19%
where the time goes in v3:
time: 214 us
  waiting for transfers between devices  71.8 us (34%)
  starting transfers between devices  45.6 us (21%)
  Pallas kernels  40.8 us (19%)
  matrix products  19.4 us (9%)
  local copies, waits for them, and re-layouts  17.2 us (8%)
  other arithmetic  17 us (8%)
    ppermute x38, waiting for transfers between devices, swap(): lax.ppermute(value, 'dp', [(i, i ^ 1 << bit) for i in range(self.count)])  71.8 us
    ppermute x38, starting transfers between devices, swap(): lax.ppermute(value, 'dp', [(i, i ^ 1 << bit) for i in range(self.count)])  45.1 us
    pallas_call x9, Pallas kernels, call(): pl.pallas_call(body, out_shape=outs, in_specs=[pl.BlockSpec(memory_space=...  40.7 us
    dot_general x2, matrix products, put(): jnp.einsum('bts,btd->bsd', one_hot, mine, preferred_element_type=F32)  13.4 us
    unnamed x41, local copies, waits for them, and re-layouts  7.27 us
  transfers between devices with their start and end apart: 43, of which 16 were waited for; matrix products, arithmetic and copies ran while one was open for 20% of the time, Pallas kernels for 19%

profile of v3, /device:TPU:0, one launch (start us, length us, event | category | flops | bytes accessed | tf_op | source)
XLA Modules:
  0.0 213.7 jit_solution(16943384158848895049)
XLA Ops:
  3.2 4.1 %collective-permute-start.1 = (bf16[48,1280]{1,0:T(8,128)(2,1)S(1)}, bf16[48,1280]{1,0:T(8,128)(2,1)S(1)}, u32[]{:S(2)}, u32[]{:S(2)}) collective-permute-start(bf16[48,1280]{1,0:T(8,128)(2,1)S(1)} %fusion.43), channel_id=1, source_target_pairs={{0,16},{2,18},{4,20},{6,22},{8,24},{10,26},{12,28},{14,30},{16,0},... | collective-permute-start | bytes 368648 | tf_op jit(solution)/shard_map/ppermute | solution.py:285
  7.3 4.2 %fusion.11 = bf16[1,3,256,384]{3,2,1,0:T(8,128)(2,1)S(1)} fusion(bf16[3,2048,384]{2,1,0:T(8,128)(2,1)} %param.23, s32[3,256]{1,0:T(4,128)} %param.15), kind=kOutput, calls=%fused_computation.32 | convolution fusion | flops 1209827328 | bytes 5311488 | tf_op jit(solution)/shard_map/bts,bsd->btd/dot_general | solution.py:418
  11.6 1.8 fusion.12
  14.6 2.5 %select_reduce_fusion = (s32[3,256]{1,0:T(4,128)S(1)}, s32[3,256]{1,0:T(4,128)S(1)}) fusion(s32[3,2048]{1,0:T(4,128)S(1)} %copy-done.12, s32[3,256]{1,0:T(4,128)S(1)} %copy-done.14, s32[3,2048]{1,0:T(4,128)S(1)} %copy-done.13), kind=kLoop, calls=%fused_computation | loop fusion | flops 7862784 | bytes 58368 | tf_op jit(solution)/shard_map/reduce_sum | solution.py:420
  17.4 1.6 collective-permute-start.2
  19.3 6.3 %collective-permute-done.2 = bf16[2,48,1280]{2,1,0:T(8,128)(2,1)S(1)} collective-permute-done((bf16[2,48,1280]{2,1,0:T(8,128)(2,1)S(1)}, bf16[2,48,1280]{2,1,0:T(8,128)(2,1)S(1)}, u32[]{:S(2)}, u32[]{:S(2)}) %collective-permute-start.2) | collective-permute-done | bytes 245792 | tf_op jit(solution)/shard_map/ppermute | solution.py:285
  27.9 1.7 collective-permute-start.3
  31.2 5.5 %collective-permute-done.7 = bf16[48,1920]{1,0:T(8,128)(2,1)S(1)} collective-permute-done((bf16[48,1920]{1,0:T(8,128)(2,1)S(1)}, bf16[48,1920]{1,0:T(8,128)(2,1)S(1)}, u32[]{:S(2)}, u32[]{:S(2)}) %collective-permute-start.7) | collective-permute-done | bytes 184352 | tf_op jit(solution)/shard_map/ppermute | solution.py:285
  40.3 6.0 %collective-permute-done.8 = bf16[2,48,1920]{2,1,0:T(8,128)(2,1)S(1)} collective-permute-done((bf16[2,48,1920]{2,1,0:T(8,128)(2,1)S(1)}, bf16[2,48,1920]{2,1,0:T(8,128)(2,1)S(1)}, u32[]{:S(2)}, u32[]{:S(2)}) %collective-permute-start.8) | collective-permute-done | bytes 368672 | tf_op jit(solution)/shard_map/ppermute | solution.py:285
  49.5 5.1 %collective-permute-done.14 = bf16[48,1536]{1,0:T(8,128)(2,1)S(1)} collective-permute-done((bf16[48,1536]{1,0:T(8,128)(2,1)S(1)}, bf16[48,1536]{1,0:T(8,128)(2,1)S(1)}, u32[]{:S(2)}, u32[]{:S(2)}) %collective-permute-start.14) | collective-permute-done | bytes 147488 | tf_op jit(solution)/shard_map/ppermute | solution.py:285
  59.4 4.2 %collective-permute-done.9 = bf16[2,2,48,896]{3,2,1,0:T(8,128)(2,1)S(1)} collective-permute-done((bf16[2,2,48,896]{3,2,1,0:T(8,128)(2,1)S(1)}, bf16[2,2,48,896]{3,2,1,0:T(8,128)(2,1)S(1)}, u32[]{:S(2)}, u32[]{:S(2)}) %collective-permute-start.9) | collective-permute-done | bytes 344096 | tf_op jit(solution)/shard_map/ppermute | solution.py:285
  67.8 5.5 %attention_forward.1 = (bf16[768,768]{1,0:T(8,128)(2,1)S(1)}, bf16[768,1152]{1,0:T(8,128)(2,1)S(1)}, f32[3,6,256,256]{3,2,1,0:T(8,128)S(1)}, bf16[768,384]{1,0:T(8,128)(2,1)S(1)}, f32[8,768]{1,0:T(8,128)S(1)}) custom-call(bf16[768,768]{1,0:T(8,128)(2,1)S(1)} %bitcast.240, bf16[768,1280]{1,0:T(8,128)(2,1)S(1)} %pad_maximum_fusion.2.refs_1_.refs_9_, ...), custom_call_target="tpu_custom_call" | custom-call | flops 1358954496 | bytes 12214272 | tf_op jit(solution)/shard_map/attention_forward/pallas_call | solution.py:40
  75.5 6.8 %collective-permute-done.11 = bf16[2,2,2,48,896]{4,3,2,1,0:T(8,128)(2,1)S(1)} collective-permute-done((bf16[2,2,2,48,896]{4,3,2,1,0:T(8,128)(2,1)S(1)}, bf16[2,2,2,48,896]{4,3,2,1,0:T(8,128)(2,1)S(1)}, u32[]{:S(2)}, u32[]{:S(2)}) %collective-permute-start.11) | collective-permute-done | bytes 688160 | tf_op jit(solution)/shard_map/ppermute | solution.py:285
  87.3 2.7 %collective-permute-done.13 = bf16[2,2,2,48,1024]{4,3,2,1,0:T(8,128)(2,1)S(1)} collective-permute-done((bf16[2,2,2,48,1024]{4,3,2,1,0:T(8,128)(2,1)S(1)}, bf16[2,2,2,48,1024]{4,3,2,1,0:T(8,128)(2,1)S(1)}, u32[]{:S(2)}, u32[]{:S(2)}) %collective-permute-start.13) | collective-permute-done | bytes 786464 | tf_op jit(solution)/shard_map/ppermute | solution.py:285
  90.6 7.7 %up_forward.1 = (bf16[768,768]{1,0:T(8,128)(2,1)S(1)}, bf16[768,1536]{1,0:T(8,128)(2,1)S(1)}, bf16[768,1536]{1,0:T(8,128)(2,1)S(1)}, bf16[768,768]{1,0:T(8,128)(2,1)S(1)}, bf16[768,1536]{1,0:T(8,128)(2,1)S(1)}) custom-call(bf16[768,768]{1,0:T(8,128)(2,1)S(1)} %bitcast.241, bf16[768,768]{1,0:T(8,128)(2,1)S(1)} %bitcast.245, ...), custom_call_target="tpu_custom_call" | custom-call | flops 3623878656 | bytes 16542720 | tf_op jit(solution)/shard_map/up_forward/pallas_call | solution.py:40
  100.1 1.7 collective-permute-done.19.refs_0_
  105.6 4.6 %down_backward.1 = (bf16[768,1536]{1,0:T(8,128)(2,1)S(1)}, bf16[768,768]{1,0:T(8,128)(2,1)S(1)}) custom-call(bf16[768,768]{1,0:T(8,128)(2,1)S(1)} %get-tuple-element.36.refs_0_, bf16[768,1536]{1,0:T(8,128)(2,1)S(1)} %pad_maximum_fusion.1.refs_1_.refs_3_, bf16[768,1536]{1,0:T(8,128)(2,1)S(1)} %copy-done.1, bf16[768,1536]{1,0:T(8,128)(2,1)S(1)} %pad_maximum_fusion.refs_4_.refs_3_), custom_call_target="tpu_custom_call" | custom-call | flops 3623878656 | bytes 11796480 | tf_op jit(solution)/shard_map/down_backward/pallas_call | solution.py:40
  110.9 3.9 %down_forward.1 = (bf16[768,1536]{1,0:T(8,128)(2,1)S(1)}, bf16[768,768]{1,0:T(8,128)(2,1)S(1)}) custom-call(bf16[768,768]{1,0:T(8,128)(2,1)S(1)} %get-tuple-element.35.refs_0_, bf16[768,1536]{1,0:T(8,128)(2,1)S(1)} %get-tuple-element.39.refs_1_, bf16[768,1536]{1,0:T(8,128)(2,1)S(1)} %get-tuple-element.37.refs_1_.refs_2_, ...), custom_call_target="tpu_custom_call" | custom-call | flops 3623878656 | bytes 11796480 | tf_op jit(solution)/shard_map/down_forward/pallas_call | solution.py:40
  117.8 8.8 %collective-permute-done.37.refs_0_ = bf16[2,2,2,48,768]{4,3,2,1,0:T(8,128)(2,1)S(1)} collective-permute-done((bf16[2,2,2,48,768]{4,3,2,1,0:T(8,128)(2,1)S(1)}, bf16[2,2,2,48,768]{4,3,2,1,0:T(8,128)(2,1)S(1)}, u32[]{:S(2)}, u32[]{:S(2)}) %collective-permute-start.37) | collective-permute-done | bytes 589856 | tf_op jit(solution)/shard_map/ppermute | solution.py:285
  127.9 12.2 %attention_backward.1 = (bf16[768,768]{1,0:T(8,128)(2,1)S(1)}, bf16[768,1152]{1,0:T(8,128)(2,1)S(1)}, bf16[768,768]{1,0:T(8,128)(2,1)S(1)}, f32[768,768]{1,0:T(8,128)S(1)}, f32[8,768]{1,0:T(8,128)S(1)}) custom-call(bf16[768,768]{1,0:T(8,128)(2,1)S(1)} %bitcast.242, bf16[768,768]{1,0:T(8,128)(2,1)S(1)} %mix_forward.1.refs_2_.refs_1_, ...), custom_call_target="tpu_custom_call" | custom-call | flops 2264924160 | bytes 22662144 | tf_op jit(solution)/shard_map/attention_backward/pallas_call | solution.py:40
  140.1 5.0 %collective-permute-done.40.refs_0_ = bf16[2,2,48,768]{3,2,1,0:T(8,128)(2,1)S(1)} collective-permute-done((bf16[2,2,48,768]{3,2,1,0:T(8,128)(2,1)S(1)}, bf16[2,2,48,768]{3,2,1,0:T(8,128)(2,1)S(1)}, u32[]{:S(2)}, u32[]{:S(2)}) %collective-permute-start.40) | collective-permute-done | bytes 294944 | tf_op jit(solution)/shard_map/ppermute | solution.py:285
  145.3 2.6 %collective-permute-start.41 = (bf16[2,48,1536]{2,1,0:T(8,128)(2,1)S(1)}, bf16[2,48,1536]{2,1,0:T(8,128)(2,1)S(1)}, u32[]{:S(2)}, u32[]{:S(2)}) collective-permute-start(bf16[2,48,1536]{2,1,0:T(8,128)(2,1)S(1)} %fusion.35), channel_id=1, source_target_pairs={{0,8},{2,10},{4,12},{6,14},{8,0},{10,2},{12,4},{14,6},{16,24},{18,... | collective-permute-start | bytes 884744 | tf_op jit(solution)/shard_map/ppermute | solution.py:285
  148.9 1.9 final_forward.1
  153.0 2.4 %projection_grads.1.refs_1_ = bf16[768,1536]{1,0:T(8,128)(2,1)S(1)} custom-call(bf16[768,768]{1,0:T(8,128)(2,1)S(1)} %get-tuple-element.47.refs_0_, bf16[768,1152]{1,0:T(8,128)(2,1)S(1)} %get-tuple-element.48.refs_1_, bf16[768,768]{1,0:T(8,128)(2,1)S(1)} %get-tuple-element.49.refs_2_, bf16[768,384]{1,0:T(8,128)(2,1)S(1)} %get-tuple-element.33.refs_0_.refs_3_), custom_call_target="tpu_custom_call" | custom-call | flops 1811939328 | bytes 7077888 | tf_op jit(solution)/shard_map/projection_grads/pallas_call | solution.py:40
  160.8 1.8 final_backward.1
  163.4 3.4 %collective-permute-start.42 = (bf16[48,1536]{1,0:T(8,128)(2,1)}, bf16[48,1536]{1,0:T(8,128)(2,1)}, u32[]{:S(2)}, u32[]{:S(2)}) collective-permute-start(bf16[48,1536]{1,0:T(8,128)(2,1)} %fusion.42), channel_id=1, source_target_pairs={{0,16},{2,18},{4,20},{6,22},{8,24},{10,26},{12,28},{14,30},{16,0},... | collective-permute-start | bytes 442376 | tf_op jit(solution)/shard_map/ppermute | solution.py:285
  174.1 6.7 %convert_select_fusion = bf16[3,2048,384]{2,1,0:T(8,128)(2,1)} fusion(bf16[3,2048,384]{2,1,0:T(8,128)(2,1)} %param.23, pred[3,2048]{1,0:T(4,128)(4,1)S(1)} %copy-done.15, bf16[3,256,384]{2,1,0:T(8,128)(2,1)S(1)} %bitcast.270, s32[3,256]{1,0:T(4,128)S(1)} %copy-done.14), kind=kOutput, calls=%fused_computation.8 | convolution fusion | flops 1214251008 | bytes 10036224 | tf_op jit(solution)/shard_map/bts,btd->bsd/dot_general | solution.py:533
  184.4 6.7 %convert_select_fusion.1 = bf16[3,2048,384]{2,1,0:T(8,128)(2,1)} fusion(bf16[3,2048,384]{2,1,0:T(8,128)(2,1)} %param.12, pred[3,2048]{1,0:T(4,128)(4,1)S(1)} %copy-done.15, bf16[3,256,384]{2,1,0:T(8,128)(2,1)S(1)} %bitcast.269, s32[3,256]{1,0:T(4,128)S(1)} %copy-done.14), kind=kOutput, calls=%fused_computation.9 | convolution fusion | flops 1214251008 | bytes 10036224 | tf_op jit(solution)/shard_map/bts,btd->bsd/dot_general | solution.py:533
  191.1 1.7 fusion.36
  193.1 1.6 collective-permute-start.29
  195.0 9.2 %collective-permute-done.29 = bf16[2,48,1664]{2,1,0:T(8,128)(2,1)S(1)} collective-permute-done((bf16[2,48,1664]{2,1,0:T(8,128)(2,1)S(1)}, bf16[2,48,1664]{2,1,0:T(8,128)(2,1)S(1)}, u32[]{:S(2)}, u32[]{:S(2)}) %collective-permute-start.29) | collective-permute-done | bytes 319520 | tf_op jit(solution)/shard_map/ppermute | solution.py:285
  205.1 6.4 %collective-permute-done.30 = bf16[48,1664]{1,0:T(8,128)(2,1)S(1)} collective-permute-done((bf16[48,1664]{1,0:T(8,128)(2,1)S(1)}, bf16[48,1664]{1,0:T(8,128)(2,1)S(1)}, u32[]{:S(2)}, u32[]{:S(2)}) %collective-permute-start.30) | collective-permute-done | bytes 159776 | tf_op jit(solution)/shard_map/ppermute | solution.py:285
  (249 shorter events, 65.6 us)
Async XLA Ops:
  3.2 14.0 %collective-permute-start.1 = (bf16[48,1280]{1,0:T(8,128)(2,1)S(1)}, bf16[48,1280]{1,0:T(8,128)(2,1)S(1)}, u32[]{:S(2)}, u32[]{:S(2)}) collective-permute-start(bf16[48,1280]{1,0:T(8,128)(2,1)S(1)} %fusion.43), channel_id=1, source_target_pairs={{0,16},{2,18},{4,20},{6,22},{8,24},{10,26},{12,28},{14,30},{16,0},... | collective-permute-start | bytes 368648 | tf_op jit(solution)/shard_map/ppermute | solution.py:285
  14.6 43.1 %collective-permute-start = (bf16[2,3,256,384]{3,2,1,0:T(8,128)(2,1)}, bf16[2,3,256,384]{3,2,1,0:T(8,128)(2,1)}, u32[]{:S(2)}, u32[]{:S(2)}) collective-permute-start(bf16[2,3,256,384]{3,2,1,0:T(8,128)(2,1)} %pad_maximum_fusion.5), channel_id=1, source_target_pairs={{0,1},{1,0},{2,3},{3,2},{4,5},{5,4},{6,7},{7,6},{8,9},{9,8},{10,11... | collective-permute-start | bytes 3538952 | tf_op jit(solution)/shard_map/ppermute | solution.py:368
  25.7 11.0 %collective-permute-start.7 = (bf16[48,1920]{1,0:T(8,128)(2,1)S(1)}, bf16[48,1920]{1,0:T(8,128)(2,1)S(1)}, u32[]{:S(2)}, u32[]{:S(2)}) collective-permute-start(bf16[48,1920]{1,0:T(8,128)(2,1)S(1)} %shard_map.187), channel_id=1, source_target_pairs={{0,16},{2,18},{4,20},{6,22},{8,24},{10,26},{12,28},{14,30},{16,0},... | collective-permute-start | bytes 552968 | tf_op jit(solution)/shard_map/ppermute | solution.py:285
  37.0 19.1 %collective-permute-start.4 = (bf16[2,2,2,48,640]{4,3,2,1,0:T(8,128)(2,1)S(1)}, bf16[2,2,2,48,640]{4,3,2,1,0:T(8,128)(2,1)S(1)}, u32[]{:S(2)}, u32[]{:S(2)}) collective-permute-start(bf16[2,2,2,48,640]{4,3,2,1,0:T(8,128)(2,1)S(1)} %pad_maximum_fusion.12), channel_id=1, source_target_pairs={{0,4},{2,6},{4,0},{6,2},{8,12},{10,14},{12,8},{14,10},{16,20},{18,... | collective-permute-start | bytes 1474568 | tf_op jit(solution)/shard_map/ppermute | solution.py:285
  38.7 18.5 %collective-permute-start.6 = (bf16[2,2,2,48,640]{4,3,2,1,0:T(8,128)(2,1)S(1)}, bf16[2,2,2,48,640]{4,3,2,1,0:T(8,128)(2,1)S(1)}, u32[]{:S(2)}, u32[]{:S(2)}) collective-permute-start(bf16[2,2,2,48,640]{4,3,2,1,0:T(8,128)(2,1)S(1)} %pad_maximum_fusion.13), channel_id=1, source_target_pairs={{0,2},{2,0},{4,6},{6,4},{8,10},{10,8},{12,14},{14,12},{16,18},{18,... | collective-permute-start | bytes 1474568 | tf_op jit(solution)/shard_map/ppermute | solution.py:285
  48.0 19.0 %collective-permute-start.10 = (bf16[2,2,48,1024]{3,2,1,0:T(8,128)(2,1)S(1)}, bf16[2,2,48,1024]{3,2,1,0:T(8,128)(2,1)S(1)}, u32[]{:S(2)}, u32[]{:S(2)}) collective-permute-start(bf16[2,2,48,1024]{3,2,1,0:T(8,128)(2,1)S(1)} %fusion.24), channel_id=1, source_target_pairs={{0,4},{2,6},{4,0},{6,2},{8,12},{10,14},{12,8},{14,10},{16,20},{18,... | collective-permute-start | bytes 1179656 | tf_op jit(solution)/shard_map/ppermute | solution.py:285
  63.9 18.4 %collective-permute-start.11 = (bf16[2,2,2,48,896]{4,3,2,1,0:T(8,128)(2,1)S(1)}, bf16[2,2,2,48,896]{4,3,2,1,0:T(8,128)(2,1)S(1)}, u32[]{:S(2)}, u32[]{:S(2)}) collective-permute-start(bf16[2,2,2,48,896]{4,3,2,1,0:T(8,128)(2,1)S(1)} %pad_maximum_fusion.8.refs_3_), channel_id=1, source_target_pairs={{0,4},{2,6},{4,0},{6,2},{8,12},{10,14},{12,8},{14,10},{16,20},{18,... | collective-permute-start | bytes 2064392 | tf_op jit(solution)/shard_map/ppermute | solution.py:285
  65.4 10.0 %collective-permute-start.16 = (bf16[2,2,48,768]{3,2,1,0:T(8,128)(2,1)S(1)}, bf16[2,2,48,768]{3,2,1,0:T(8,128)(2,1)S(1)}, u32[]{:S(2)}, u32[]{:S(2)}) collective-permute-start(bf16[2,2,48,768]{3,2,1,0:T(8,128)(2,1)S(1)} %get-tuple-element.122), channel_id=1, source_target_pairs={{0,2},{2,0},{4,6},{6,4},{8,10},{10,8},{12,14},{14,12},{16,18},{18,... | collective-permute-start | bytes 884744 | tf_op jit(solution)/shard_map/ppermute | solution.py:285
  67.2 22.9 %collective-permute-start.13 = (bf16[2,2,2,48,1024]{4,3,2,1,0:T(8,128)(2,1)S(1)}, bf16[2,2,2,48,1024]{4,3,2,1,0:T(8,128)(2,1)S(1)}, u32[]{:S(2)}, u32[]{:S(2)}) collective-permute-start(bf16[2,2,2,48,1024]{4,3,2,1,0:T(8,128)(2,1)S(1)} %pad_maximum_fusion.7.refs_4_), channel_id=1, source_target_pairs={{0,2},{2,0},{4,6},{6,4},{8,10},{10,8},{12,14},{14,12},{16,18},{18,... | collective-permute-start | bytes 2359304 | tf_op jit(solution)/shard_map/ppermute | solution.py:285
  73.2 12.5 %collective-permute-start.18 = (bf16[2,2,48,768]{3,2,1,0:T(8,128)(2,1)S(1)}, bf16[2,2,48,768]{3,2,1,0:T(8,128)(2,1)S(1)}, u32[]{:S(2)}, u32[]{:S(2)}) collective-permute-start(bf16[2,2,48,768]{3,2,1,0:T(8,128)(2,1)S(1)} %get-tuple-element.123), channel_id=1, source_target_pairs={{0,4},{2,6},{4,0},{6,2},{8,12},{10,14},{12,8},{14,10},{16,20},{18,... | collective-permute-start | bytes 884744 | tf_op jit(solution)/shard_map/ppermute | solution.py:285
  83.7 15.8 %collective-permute-start.17 = (bf16[2,2,2,48,768]{4,3,2,1,0:T(8,128)(2,1)S(1)}, bf16[2,2,2,48,768]{4,3,2,1,0:T(8,128)(2,1)S(1)}, u32[]{:S(2)}, u32[]{:S(2)}) collective-permute-start(bf16[2,2,2,48,768]{4,3,2,1,0:T(8,128)(2,1)S(1)} %pad_maximum_fusion.10), channel_id=1, source_target_pairs={{0,4},{2,6},{4,0},{6,2},{8,12},{10,14},{12,8},{14,10},{16,20},{18,... | collective-permute-start | bytes 1769480 | tf_op jit(solution)/shard_map/ppermute | solution.py:285
  85.9 15.9 %collective-permute-start.19 = (bf16[2,2,2,48,768]{4,3,2,1,0:T(8,128)(2,1)S(1)}, bf16[2,2,2,48,768]{4,3,2,1,0:T(8,128)(2,1)S(1)}, u32[]{:S(2)}, u32[]{:S(2)}) collective-permute-start(bf16[2,2,2,48,768]{4,3,2,1,0:T(8,128)(2,1)S(1)} %pad_maximum_fusion.11), channel_id=1, source_target_pairs={{0,2},{2,0},{4,6},{6,4},{8,10},{10,8},{12,14},{14,12},{16,18},{18,... | collective-permute-start | bytes 1769480 | tf_op jit(solution)/shard_map/ppermute | solution.py:285
  102.3 14.5 %collective-permute-start.39 = (bf16[2,2,2,48,768]{4,3,2,1,0:T(8,128)(2,1)S(1)}, bf16[2,2,2,48,768]{4,3,2,1,0:T(8,128)(2,1)S(1)}, u32[]{:S(2)}, u32[]{:S(2)}) collective-permute-start(bf16[2,2,2,48,768]{4,3,2,1,0:T(8,128)(2,1)S(1)} %get-tuple-element.94), channel_id=1, source_target_pairs={{0,2},{2,0},{4,6},{6,4},{8,10},{10,8},{12,14},{14,12},{16,18},{18,... | collective-permute-start | bytes 1769480 | tf_op jit(solution)/shard_map/ppermute | solution.py:285
  110.2 17.0 %collective-permute-start.21 = (bf16[768,768]{1,0:T(8,128)(2,1)S(1)}, bf16[768,768]{1,0:T(8,128)(2,1)S(1)}, u32[]{:S(2)}, u32[]{:S(2)}) collective-permute-start(bf16[768,768]{1,0:T(8,128)(2,1)S(1)} %get-tuple-element.42.refs_3_), channel_id=1, source_target_pairs={{0,1},{1,0},{2,3},{3,2},{4,5},{5,4},{6,7},{7,6},{8,9},{9,8},{10,11... | collective-permute-start | bytes 3538952 | tf_op jit(solution)/shard_map/ppermute | solution.py:368
  110.4 16.2 %collective-permute-start.37 = (bf16[2,2,2,48,768]{4,3,2,1,0:T(8,128)(2,1)S(1)}, bf16[2,2,2,48,768]{4,3,2,1,0:T(8,128)(2,1)S(1)}, u32[]{:S(2)}, u32[]{:S(2)}) collective-permute-start(bf16[2,2,2,48,768]{4,3,2,1,0:T(8,128)(2,1)S(1)} %get-tuple-element.96), channel_id=1, source_target_pairs={{0,4},{2,6},{4,0},{6,2},{8,12},{10,14},{12,8},{14,10},{16,20},{18,... | collective-permute-start | bytes 1769480 | tf_op jit(solution)/shard_map/ppermute | solution.py:285
  114.8 34.1 %collective-permute-start.20 = (bf16[768,768]{1,0:T(8,128)(2,1)S(1)}, bf16[768,768]{1,0:T(8,128)(2,1)S(1)}, u32[]{:S(2)}, u32[]{:S(2)}) collective-permute-start(bf16[768,768]{1,0:T(8,128)(2,1)S(1)} %get-tuple-element.40.refs_4_.refs_1_), channel_id=1, source_target_pairs={{0,1},{1,0},{2,3},{3,2},{4,5},{5,4},{6,7},{7,6},{8,9},{9,8},{10,11... | collective-permute-start | bytes 3538952 | tf_op jit(solution)/shard_map/ppermute | solution.py:368
  115.3 32.6 %collective-permute-start.33 = (bf16[2,2,2,48,768]{4,3,2,1,0:T(8,128)(2,1)S(1)}, bf16[2,2,2,48,768]{4,3,2,1,0:T(8,128)(2,1)S(1)}, u32[]{:S(2)}, u32[]{:S(2)}) collective-permute-start(bf16[2,2,2,48,768]{4,3,2,1,0:T(8,128)(2,1)S(1)} %get-tuple-element.98), channel_id=1, source_target_pairs={{0,2},{2,0},{4,6},{6,4},{8,10},{10,8},{12,14},{14,12},{16,18},{18,... | collective-permute-start | bytes 1769480 | tf_op jit(solution)/shard_map/ppermute | solution.py:285
  116.9 34.6 %collective-permute-start.31 = (bf16[2,2,2,48,768]{4,3,2,1,0:T(8,128)(2,1)S(1)}, bf16[2,2,2,48,768]{4,3,2,1,0:T(8,128)(2,1)S(1)}, u32[]{:S(2)}, u32[]{:S(2)}) collective-permute-start(bf16[2,2,2,48,768]{4,3,2,1,0:T(8,128)(2,1)S(1)} %get-tuple-element.100), channel_id=1, source_target_pairs={{0,4},{2,6},{4,0},{6,2},{8,12},{10,14},{12,8},{14,10},{16,20},{18,... | collective-permute-start | bytes 1769480 | tf_op jit(solution)/shard_map/ppermute | solution.py:285
  126.6 18.6 %collective-permute-start.40 = (bf16[2,2,48,768]{3,2,1,0:T(8,128)(2,1)S(1)}, bf16[2,2,48,768]{3,2,1,0:T(8,128)(2,1)S(1)}, u32[]{:S(2)}, u32[]{:S(2)}) collective-permute-start(bf16[2,2,48,768]{3,2,1,0:T(8,128)(2,1)S(1)} %fusion.32), channel_id=1, source_target_pairs={{0,4},{2,6},{4,0},{6,2},{8,12},{10,14},{12,8},{14,10},{16,20},{18,... | collective-permute-start | bytes 884744 | tf_op jit(solution)/shard_map/ppermute | solution.py:285
  127.3 17.9 %collective-permute-start.38 = (bf16[2,2,48,768]{3,2,1,0:T(8,128)(2,1)S(1)}, bf16[2,2,48,768]{3,2,1,0:T(8,128)(2,1)S(1)}, u32[]{:S(2)}, u32[]{:S(2)}) collective-permute-start(bf16[2,2,48,768]{3,2,1,0:T(8,128)(2,1)S(1)} %fusion.31), channel_id=1, source_target_pairs={{0,2},{2,0},{4,6},{6,4},{8,10},{10,8},{12,14},{14,12},{16,18},{18,... | collective-permute-start | bytes 884744 | tf_op jit(solution)/shard_map/ppermute | solution.py:285
  145.3 17.3 %collective-permute-start.41 = (bf16[2,48,1536]{2,1,0:T(8,128)(2,1)S(1)}, bf16[2,48,1536]{2,1,0:T(8,128)(2,1)S(1)}, u32[]{:S(2)}, u32[]{:S(2)}) collective-permute-start(bf16[2,48,1536]{2,1,0:T(8,128)(2,1)S(1)} %fusion.35), channel_id=1, source_target_pairs={{0,8},{2,10},{4,12},{6,14},{8,0},{10,2},{12,4},{14,6},{16,24},{18,... | collective-permute-start | bytes 884744 | tf_op jit(solution)/shard_map/ppermute | solution.py:285
  147.9 11.4 %collective-permute-start.22 = (bf16[768,768]{1,0:T(8,128)(2,1)S(1)}, bf16[768,768]{1,0:T(8,128)(2,1)S(1)}, u32[]{:S(2)}, u32[]{:S(2)}) collective-permute-start(bf16[768,768]{1,0:T(8,128)(2,1)S(1)} %get-tuple-element.46.refs_3_), channel_id=1, source_target_pairs={{0,1},{1,0},{2,3},{3,2},{4,5},{5,4},{6,7},{7,6},{8,9},{9,8},{10,11... | collective-permute-start | bytes 3538952 | tf_op jit(solution)/shard_map/ppermute | solution.py:368
  150.9 18.0 %collective-permute-start.34 = (bf16[2,2,48,768]{3,2,1,0:T(8,128)(2,1)}, bf16[2,2,48,768]{3,2,1,0:T(8,128)(2,1)}, u32[]{:S(2)}, u32[]{:S(2)}) collective-permute-start(bf16[2,2,48,768]{3,2,1,0:T(8,128)(2,1)} %fusion.30), channel_id=1, source_target_pairs={{0,4},{2,6},{4,0},{6,2},{8,12},{10,14},{12,8},{14,10},{16,20},{18,... | collective-permute-start | bytes 884744 | tf_op jit(solution)/shard_map/ppermute | solution.py:285
  152.4 18.7 %collective-permute-start.32 = (bf16[2,2,48,768]{3,2,1,0:T(8,128)(2,1)}, bf16[2,2,48,768]{3,2,1,0:T(8,128)(2,1)}, u32[]{:S(2)}, u32[]{:S(2)}) collective-permute-start(bf16[2,2,48,768]{3,2,1,0:T(8,128)(2,1)} %fusion.29), channel_id=1, source_target_pairs={{0,2},{2,0},{4,6},{6,4},{8,10},{10,8},{12,14},{14,12},{16,18},{18,... | collective-permute-start | bytes 884744 | tf_op jit(solution)/shard_map/ppermute | solution.py:285
  156.7 24.7 %collective-permute-start.24 = (bf16[2,2,2,48,768]{4,3,2,1,0:T(8,128)(2,1)}, bf16[2,2,2,48,768]{4,3,2,1,0:T(8,128)(2,1)S(1)}, u32[]{:S(2)}, u32[]{:S(2)}) collective-permute-start(bf16[2,2,2,48,768]{4,3,2,1,0:T(8,128)(2,1)} %get-tuple-element.102), channel_id=1, source_target_pairs={{0,4},{2,6},{4,0},{6,2},{8,12},{10,14},{12,8},{14,10},{16,20},{18,... | collective-permute-start | bytes 1769480 | tf_op jit(solution)/shard_map/ppermute | solution.py:285
  159.3 23.9 %collective-permute-start.27 = (bf16[2,2,2,48,768]{4,3,2,1,0:T(8,128)(2,1)}, bf16[2,2,2,48,768]{4,3,2,1,0:T(8,128)(2,1)S(1)}, u32[]{:S(2)}, u32[]{:S(2)}) collective-permute-start(bf16[2,2,2,48,768]{4,3,2,1,0:T(8,128)(2,1)} %get-tuple-element.104), channel_id=1, source_target_pairs={{0,2},{2,0},{4,6},{6,4},{8,10},{10,8},{12,14},{14,12},{16,18},{18,... | collective-permute-start | bytes 1769480 | tf_op jit(solution)/shard_map/ppermute | solution.py:285
  163.4 27.6 %collective-permute-start.42 = (bf16[48,1536]{1,0:T(8,128)(2,1)}, bf16[48,1536]{1,0:T(8,128)(2,1)}, u32[]{:S(2)}, u32[]{:S(2)}) collective-permute-start(bf16[48,1536]{1,0:T(8,128)(2,1)} %fusion.42), channel_id=1, source_target_pairs={{0,16},{2,18},{4,20},{6,22},{8,24},{10,26},{12,28},{14,30},{16,0},... | collective-permute-start | bytes 442376 | tf_op jit(solution)/shard_map/ppermute | solution.py:285
  168.9 11.9 %collective-permute-start.23 = (bf16[2,2,2,48,128]{4,3,2,1,0:T(8,128)(2,1)S(1)}, bf16[2,2,2,48,128]{4,3,2,1,0:T(8,128)(2,1)S(1)}, u32[]{:S(2)}, u32[]{:S(2)}) collective-permute-start(bf16[2,2,2,48,128]{4,3,2,1,0:T(8,128)(2,1)S(1)} %fusion.44), channel_id=1, source_target_pairs={{0,4},{2,6},{4,0},{6,2},{8,12},{10,14},{12,8},{14,10},{16,20},{18,... | collective-permute-start | bytes 294920 | tf_op jit(solution)/shard_map/ppermute | solution.py:285
  173.5 19.3 %collective-permute-start.35 = (bf16[2,48,1536]{2,1,0:T(8,128)(2,1)S(1)}, bf16[2,48,1536]{2,1,0:T(8,128)(2,1)S(1)}, u32[]{:S(2)}, u32[]{:S(2)}) collective-permute-start(bf16[2,48,1536]{2,1,0:T(8,128)(2,1)S(1)} %fusion.34), channel_id=1, source_target_pairs={{0,8},{2,10},{4,12},{6,14},{8,0},{10,2},{12,4},{14,6},{16,24},{18,... | collective-permute-start | bytes 884744 | tf_op jit(solution)/shard_map/ppermute | solution.py:285
  180.8 11.9 %collective-permute-start.26 = (bf16[2,2,48,128]{3,2,1,0:T(8,128)(2,1)S(1)}, bf16[2,2,48,128]{3,2,1,0:T(8,128)(2,1)S(1)}, u32[]{:S(2)}, u32[]{:S(2)}) collective-permute-start(bf16[2,2,48,128]{3,2,1,0:T(8,128)(2,1)S(1)} %fusion.45), channel_id=1, source_target_pairs={{0,2},{2,0},{4,6},{6,4},{8,10},{10,8},{12,14},{14,12},{16,18},{18,... | collective-permute-start | bytes 147464 | tf_op jit(solution)/shard_map/ppermute | solution.py:285
  182.0 10.8 %collective-permute-start.25 = (bf16[2,2,48,768]{3,2,1,0:T(8,128)(2,1)S(1)}, bf16[2,2,48,768]{3,2,1,0:T(8,128)(2,1)S(1)}, u32[]{:S(2)}, u32[]{:S(2)}) collective-permute-start(bf16[2,2,48,768]{3,2,1,0:T(8,128)(2,1)S(1)} %fusion.27), channel_id=1, source_target_pairs={{0,2},{2,0},{4,6},{6,4},{8,10},{10,8},{12,14},{14,12},{16,18},{18,... | collective-permute-start | bytes 884744 | tf_op jit(solution)/shard_map/ppermute | solution.py:285
  193.1 11.1 %collective-permute-start.29 = (bf16[2,48,1664]{2,1,0:T(8,128)(2,1)S(1)}, bf16[2,48,1664]{2,1,0:T(8,128)(2,1)S(1)}, u32[]{:S(2)}, u32[]{:S(2)}) collective-permute-start(bf16[2,48,1664]{2,1,0:T(8,128)(2,1)S(1)} %fusion.26), channel_id=1, source_target_pairs={{0,8},{2,10},{4,12},{6,14},{8,0},{10,2},{12,4},{14,6},{16,24},{18,... | collective-permute-start | bytes 958472 | tf_op jit(solution)/shard_map/ppermute | solution.py:285
  (29 other events, 156.3 us)

commit v4 on v3

--- a/solution.py
+++ b/solution.py
@@ -12,7 +12,7 @@
 EPSILON = 1e-06
 BF = jnp.bfloat16
 F32 = jnp.float32
-VMEM_SPARE = 6 << 20
+VMEM_SPARE = 10 << 20
 
 
 def mm(a, b):
@@ -31,22 +31,26 @@
     return lax.rsqrt(jnp.mean(values * values, axis=-1, keepdims=True) + EPSILON)
 
 
-def call(kernel, outs, args, after=(), flops=0, name=None):
+def call(kernel, outs, args, after=(), bits=None, scratch=(), flops=0, name=None):
     moved = sum(v.size * v.dtype.itemsize for v in (*args, *outs))
+    scalars = [] if bits is None else [bits]
+    count = len(scalars) + len(args)
 
     def body(*refs):
-        kernel(*refs[: len(args)], *refs[len(args) + len(after) :])
+        kernel(*refs[:count], *refs[count + len(after) :])
 
     return pl.pallas_call(
         body,
         out_shape=outs,
-        in_specs=[pl.BlockSpec(memory_space=pltpu.VMEM)] * len(args)
+        in_specs=[pl.BlockSpec(memory_space=pltpu.SMEM)] * len(scalars)
+        + [pl.BlockSpec(memory_space=pltpu.VMEM)] * len(args)
         + [pl.BlockSpec(memory_space=pl.ANY)] * len(after),
         out_specs=[pl.BlockSpec(memory_space=pltpu.VMEM)] * len(outs),
-        compiler_params=pltpu.CompilerParams(vmem_limit_bytes=moved + VMEM_SPARE),
+        scratch_shapes=scratch,
+        compiler_params=pltpu.CompilerParams(vmem_limit_bytes=VMEM_SPARE),
         cost_estimate=pl.CostEstimate(flops=flops, bytes_accessed=moved, transcendentals=0),
         name=name,
-    )(*args, *after)
+    )(*scalars, *args, *after)
 
 
 def shape(dims, dtype=BF):
@@ -60,7 +64,7 @@
 def attention_forward(rows, sel, states_ref, weights_ref, bias_ref, normed_ref, packed_ref, probs_ref, context_ref, gains_ref):
     width = states_ref.shape[1]
     half = context_ref.shape[1]
-    gains_ref[...] = weights_ref[:, 3 * half :].astype(F32).T[:8]
+    gains_ref[...] = weights_ref[:, 4 * half :].astype(F32).T[:8]
     gain = gains_ref[0:1, :]
     scale = HD ** (-0.5)
 
@@ -238,10 +242,12 @@
 
 def final_backward(
     rows, sel, states_ref, upstream_ref, middle_grad_ref, pre_own_ref, pre_other_ref, logit_grad_ref, gains_ref,
-    total_ref, gain_grad_ref,
+    mid_gain_grad_ref, router_grad_ref, total_ref, vectors_ref, lines_ref,
 ):
     pre_gain, router = gains_ref[0:1, :], gains_ref[2:3, :]
-    gain_grad_ref[...] = jnp.zeros_like(gain_grad_ref)
+    lines_ref[...] = jnp.zeros_like(lines_ref)
+    lines_ref[1:2, :] = mid_gain_grad_ref[0:1, :]
+    lines_ref[2:3, :] = router_grad_ref[0:1, :]
 
     @pl.loop(0, rows)
     def _(row):
@@ -249,9 +255,120 @@
         states = states_ref[here, :].astype(F32)
         pre_in = pre_own_ref[here, :].astype(F32) + pre_other_ref[here, :].astype(F32)
         back, gain_grad = norm_backward(states, pre_in, pre_gain)
-        gain_grad_ref[0:1, :] += gain_grad
+        lines_ref[0:1, :] += gain_grad
         total = upstream_ref[here, :].astype(F32) + logit_grad_ref[here, :] * router
         total_ref[here, :] = (total + middle_grad_ref[here, :] + back).astype(BF)
+
+    vectors_ref[...] = lines_ref[...].T.astype(BF)
+
+
+def upright(row):
+    return jnp.broadcast_to(row, (8, row.shape[1])).T[:, :1]
+
+
+def select_rows(tokens_ref, cotangent_ref, chosen_ref, segments_ref, present_ref, picked_ref, bias_ref, keep_ref):
+    sel, length = picked_ref.shape[2], tokens_ref.shape[1]
+    row = pl.ds(pl.program_id(0), 1)
+    chosen = upright(chosen_ref[row, :].astype(F32)).astype(jnp.int32)
+    hit = chosen == lax.broadcasted_iota(jnp.int32, (sel, length), 1)
+    one_hot = jnp.where(hit, 1.0, 0.0).astype(BF)
+    picked_ref[0, 0] = mm(one_hot, tokens_ref[0]).astype(BF)
+    picked_ref[1, 0] = mm(one_hot, cotangent_ref[0]).astype(BF)
+    both = jnp.concatenate(
+        [segments_ref[row, :].astype(F32), present_ref[row, :].astype(F32), jnp.zeros((6, length), F32)], axis=0
+    ).astype(BF)
+    along = mm_nt(both, one_hot)
+    down = along.T
+    slot = lax.broadcasted_iota(jnp.int32, (sel, sel), 0)
+    seen = lax.broadcasted_iota(jnp.int32, (sel, sel), 1)
+    open_key = (along[1:2, :] > 0.5) | (slot == seen)
+    permitted = (seen <= slot) & (down[:, 0:1] == along[0:1, :]) & open_key
+    bias_ref[0] = jnp.where(permitted, 0.0, -1e30)
+    keep_ref[...] = down[:, 1:2]
+
+
+def select(tokens, cotangent, chosen, segments, present):
+    rows, length, half = tokens.shape
+    sel = chosen.shape[1]
+    by_row = pl.BlockSpec((1, length, half), lambda row: (row, 0, 0))
+    all_of = lambda v: pl.BlockSpec(v.shape, lambda row: (0, 0))
+    return pl.pallas_call(
+        select_rows,
+        grid=(rows,),
+        out_shape=(shape((2, rows, sel, half)), shape((rows, sel, sel), F32), shape((rows * sel, 1), F32)),
+        in_specs=[by_row, by_row, all_of(chosen), all_of(segments), all_of(present)],
+        out_specs=[
+            pl.BlockSpec((2, 1, sel, half), lambda row: (0, row, 0, 0)),
+            pl.BlockSpec((1, sel, sel), lambda row: (row, 0, 0)),
+            pl.BlockSpec((sel, 1), lambda row: (row, 0)),
+        ],
+        compiler_params=pltpu.CompilerParams(vmem_limit_bytes=60 << 20),
+        cost_estimate=pl.CostEstimate(
+            flops=4 * rows * sel * length * half, bytes_accessed=4 * tokens.size, transcendentals=0
+        ),
+        name="select_rows",
+    )(tokens, cotangent, chosen, segments, present)
+
+
+def put_rows(bits_ref, chosen_ref, values_ref, base_ref, out_ref):
+    long, half = out_ref.shape[1:]
+    sel = values_ref.shape[0]
+    first = pl.program_id(1) * long
+    chosen = chosen_ref[pl.ds(pl.program_id(0), 1), :]
+    hit = first + lax.broadcasted_iota(jnp.int32, (long, sel), 0) == chosen
+    one_hot = jnp.where(hit, 1.0, 0.0).astype(BF)
+    offset = pl.multiple_of(bits_ref[-1 + bits_ref.shape[0]] * half, half)
+    values = values_ref[:, pl.ds(offset, half)]
+    placed = mm(one_hot, jnp.concatenate([values, jnp.ones((sel, 128), BF)], axis=1))
+    taken = placed[:, half:] > 0.5
+    for at in range(0, half, 128):
+        here = slice(at, at + 128)
+        out_ref[0, :, here] = jnp.where(taken, placed[:, here].astype(BF), base_ref[0, :, here])
+
+
+def put(base, chosen, values, bits, after=()):
+    rows, length, half = base.shape
+    sel = chosen.shape[1]
+    long = length // 2
+
+    def body(*refs):
+        put_rows(*refs[:4], refs[-1])
+
+    return pl.pallas_call(
+        body,
+        grid=(rows, length // long),
+        out_shape=shape(base.shape),
+        in_specs=[
+            pl.BlockSpec(memory_space=pltpu.SMEM),
+            pl.BlockSpec(chosen.shape, lambda row, part: (0, 0)),
+            pl.BlockSpec((sel, values.shape[1]), lambda row, part: (row, 0)),
+            pl.BlockSpec((1, long, half), lambda row, part: (row, part, 0)),
+        ]
+        + [pl.BlockSpec(memory_space=pl.ANY)] * len(after),
+        out_specs=pl.BlockSpec((1, long, half), lambda row, part: (row, part, 0)),
+        compiler_params=pltpu.CompilerParams(vmem_limit_bytes=24 << 20),
+        cost_estimate=pl.CostEstimate(
+            flops=2 * rows * sel * length * half, bytes_accessed=4 * base.size, transcendentals=0
+        ),
+        name="put_rows",
+    )(bits, chosen, values, base, *after)
+
+
+def first_columns(attention_ref, mixing_ref, vectors_ref, out_ref):
+    half = attention_ref.shape[2]
+    for k in range(3):
+        out_ref[:, k * half : (k + 1) * half] = attention_ref[k]
+    out_ref[:, 3 * half : 4 * half] = mixing_ref[...]
+    out_ref[:, 4 * half :] = vectors_ref[...]
+
+
+def second_columns(cuts, expand_ref, contract_ref, out_ref):
+    at = 0
+    for start, end in cuts:
+        out_ref[:, at : at + end - start] = expand_ref[:, start:end]
+        at += end - start
+        out_ref[:, at : at + end - start] = contract_ref[:, start:end]
+        at += end - start
 
 
 def untouched(*refs):
@@ -275,93 +392,170 @@
 
 class Cube:
     def __init__(self, count):
-        self.count, self.bits = count, count.bit_length() - 1
-        self.index = lax.axis_index("dp").astype(jnp.uint32)
-        short = self.bits // 3
+        self.count, self.depth = count, count.bit_length() - 1
+        index = lax.axis_index("dp").astype(jnp.int32)
+        self.bits = jnp.append(
+            (index >> jnp.arange(self.depth)) & 1, lax.axis_index("mp").astype(jnp.int32)
+        )
+        short = self.depth // 3
         self.x, self.y = list(range(short)), list(range(short, 2 * short))
-        self.z = list(range(2 * short, self.bits))
+        self.z = list(range(2 * short, self.depth))
+        self.far = self.z[1:]
+        near = [self.x, self.y, self.z[:1]]
+        self.orders = [sum(near[k:] + near[:k], []) for k in range(3)]
 
     def swap(self, value, bit):
         return lax.ppermute(value, "dp", [(i, i ^ (1 << bit)) for i in range(self.count)])
 
-    def low(self, bit):
-        return (self.index >> bit) % 2 == 0
-
-    def double(self, value, bit, after=()):
-        other, low = tie(self.swap(value, bit), *after), self.low(bit)
-        return jnp.stack([jnp.where(low, value, other), jnp.where(low, other, value)])
-
-    def halve(self, value, axis, bit, after=()):
-        own = ((self.index >> bit) % 2).astype(jnp.int32)
-        mine = lax.dynamic_index_in_dim(value, own, axis, keepdims=False)
-        sent = lax.dynamic_index_in_dim(value, 1 - own, axis, keepdims=False)
-        return mine.astype(F32) + tie(self.swap(sent.astype(BF), bit), *after).astype(F32)
-
-
-def halves(width):
-    return width // 2 // 128 * 128
-
-
-def gather_z(cube, own, after=()):
-    column = tie(own, *after)
-    for bit in cube.z[::-1]:
-        column = cube.double(column, bit)
-    return column
-
-
-def gather_first(cube, column):
-    cut = halves(column.shape[-1])
-    parts = []
-    for part, order in ((column[..., :cut], cube.x), (column[..., cut:], cube.y)):
-        for bit in order:
-            part = cube.double(part, bit)
-        parts.append(part)
-    return parts
-
-
-def gather_second(cube, parts, after=()):
+
+class Part:
+    def __init__(self, value, bits, sent=None, start=0, width=None):
+        self.value, self.bits, self.sent = value, list(bits), sent
+        self.start, self.width = start, width or value.shape[2]
+
+    def columns(self, start, end):
+        return Part(self.value, self.bits, self.sent, self.start + start, end - start)
+
+
+def thirds(width):
+    ends = [(k * width // 3 + 64) // 128 * 128 for k in range(4)]
+    return list(zip(ends, ends[1:]))
+
+
+def start_exchange(cube, part, bit):
+    part.sent = cube.swap(part.value, bit)
+    return part
+
+
+def stack_parts(plan, bits_ref, *refs):
+    ins, outs = refs[: 2 * len(plan)], refs[2 * len(plan) :]
+    for k, (bit, blocks) in enumerate(plan):
+        mine = bits_ref[bit]
+        for block in range(blocks):
+            outs[k][mine, block] = ins[2 * k][block]
+            outs[k][1 - mine, block] = ins[2 * k + 1][block]
+
+
+def stack(cube, parts, bits, after=()):
+    outs, args, plan = [], [], []
+    for part, bit in zip(parts, bits):
+        outs.append(shape((2,) + part.value.shape))
+        args += [part.value, part.sent]
+        plan.append((bit, part.value.shape[0]))
+    found = call(functools.partial(stack_parts, plan), outs, args, after, cube.bits, name="stack_parts")
+    return [
+        Part(v.reshape((-1,) + v.shape[2:]), [bit] + part.bits) for v, part, bit in zip(found, parts, bits)
+    ]
+
+
+def split_columns(plan, own_ref, *out_refs):
+    for ref, (start, end) in zip(out_refs, plan):
+        ref[...] = own_ref[:, :, start:end]
+
+
+def whole_rows(plan, bits_ref, *refs):
+    ins, out_ref = refs[:-1], refs[-1]
+    column = 0
+    for k, (bit, places, start, width) in enumerate(plan):
+        mine = bits_ref[bit]
+        for block, place in enumerate(places):
+            here = slice(column, column + width)
+            out_ref[place + (mine << bit), :, here] = ins[2 * k][block, :, start : start + width]
+            out_ref[place + ((1 - mine) << bit), :, here] = ins[2 * k + 1][block, :, start : start + width]
+        column += width
+
+
+def whole(cube, parts, bits, after=()):
+    args, plan, width = [], [], 0
+    for part, bit in zip(parts, bits):
+        places = []
+        for block in range(part.value.shape[0]):
+            digits = [(block >> k) & 1 for k in range(len(part.bits))][::-1]
+            places.append(sum(digit << b for digit, b in zip(digits, part.bits)))
+        args += [part.value, part.sent]
+        plan.append((bit, places, part.start, part.width))
+        width += part.width
+    rows = parts[0].value.shape[1]
+    (found,) = call(
+        functools.partial(whole_rows, plan),
+        (shape((cube.count, rows, width)),),
+        args,
+        after,
+        cube.bits,
+        name="whole_rows",
+    )
+    return found.reshape(-1, width)
+
+
+def fold_parts(plan, bits_ref, *refs):
+    refs = list(refs)
+    taken = [[(refs.pop(0), refs.pop(0) if sent else None) for sent, _, _ in sources] for _, _, sources in plan]
+    for (bit, (high, low), sources), ins in zip(plan, taken):
+        sent_ref, kept_ref = refs.pop(0), refs.pop(0)
+        mine = bits_ref[bit]
+        column = 0
+        for (_, start, width), (value_ref, other_ref) in zip(sources, ins):
+            there = slice(start, start + width)
+            here = slice(column, column + width)
+            for a in range(high):
+                for b in range(low):
+                    for index, out_ref in ((1 - mine, sent_ref), (mine, kept_ref)):
+                        found = value_ref[a, index, b, :, there].astype(F32)
+                        if other_ref is not None:
+                            found += other_ref[a, index, b, :, there].astype(F32)
+                        out_ref[a * low + b, :, here] = found.astype(out_ref.dtype)
+            column += width
+
+
+def fold(cube, groups, bits, after=()):
+    args, outs, plan = [], [], []
+    for sources, bit in zip(groups, bits):
+        at = sources[0].bits.index(bit)
+        high, low = 1 << at, 1 << (len(sources[0].bits) - at - 1)
+        listed = []
+        for part in sources:
+            for value in (part.value, part.sent):
+                if value is not None:
+                    args.append(value.reshape((high, 2, low) + value.shape[1:]))
+            listed.append((part.sent is not None, part.start, part.width))
+        plan.append((bit, (high, low), listed))
+        dims = (high * low, sources[0].value.shape[1], sum(p.width for p in sources))
+        outs += [shape(dims), shape(dims, F32)]
+    found = call(functools.partial(fold_parts, plan), outs, args, after, cube.bits, name="fold_parts")
     done = []
-    for part, before, order in zip(parts, (cube.x, cube.y), (cube.y, cube.x)):
-        for bit in order:
-            part = cube.double(part, bit, after)
-        axes = order[::-1] + before[::-1] + cube.z
-        bits = sorted(axes, reverse=True)
-        part = part.transpose([axes.index(b) for b in bits] + [cube.bits, cube.bits + 1])
-        done.append(part.reshape(-1, part.shape[-1]))
-    return jnp.concatenate(done, axis=1)
-
-
-def reduce_first(cube, total, after=()):
-    cut = halves(total.shape[1])
-    pieces = [(total[:, :cut], cube.y), (total[:, cut:], cube.x)] if cut else [(total, cube.y)]
-    parts = []
-    for part, order in pieces:
-        part = part.reshape([2] * cube.bits + [-1, part.shape[1]])
-        axes = list(range(cube.bits))[::-1]
-        for bit in order:
-            part = cube.halve(part, axes.index(bit), bit, after)
-            axes.remove(bit)
-        parts.append(part)
-    return parts
-
-
-def reduce_second(cube, parts, after=()):
-    done = []
-    for part, order, gone in zip(parts, (cube.x, cube.y), (cube.y, cube.x)):
-        axes = [b for b in range(cube.bits)[::-1] if b not in gone]
-        for bit in order:
-            part = cube.halve(part, axes.index(bit), bit, after)
-            axes.remove(bit)
-        done.append(part)
-    return jnp.concatenate(done, axis=-1)
-
-
-def reduce_z(cube, part, after=()):
-    axes = cube.z[::-1]
-    for bit in cube.z:
-        part = cube.halve(part, axes.index(bit), bit, after.pop(0) if after else ())
-        axes.remove(bit)
-    return part
+    for k, (sources, bit) in enumerate(zip(groups, bits)):
+        left = [b for b in sources[0].bits if b != bit]
+        done.append(Part(found[2 * k + 1], left, cube.swap(found[2 * k], bit)))
+    return done
+
+
+def cut(cube, total):
+    blocks = total.reshape(cube.count, -1, total.shape[1])
+    bits = list(range(cube.depth))[::-1]
+    return [Part(blocks, bits, None, start, end - start) for start, end in thirds(total.shape[1]) if end > start]
+
+
+def arrived(parts):
+    return [p.sent for p in parts]
+
+
+def sum_first(value_ref, sent_ref, attention_ref, mixing_ref, vectors_ref):
+    half = attention_ref.shape[2]
+    total = value_ref[0] + sent_ref[0].astype(F32)
+    for k in range(3):
+        attention_ref[k] = total[:, k * half : (k + 1) * half]
+    mixing_ref[...] = total[:, 3 * half : 4 * half]
+    vectors_ref[...] = total[:, 4 * half :].T
+
+
+def sum_second(cuts, value_ref, sent_ref, expand_ref, contract_ref):
+    at = 0
+    for start, end in cuts:
+        for side in range(2):
+            width = end - start
+            total = value_ref[0, :, at : at + width] + sent_ref[0, :, at : at + width].astype(F32)
+            (expand_ref if side else contract_ref)[:, start:end] = total
+            at += width
 
 
 def other_core(value):
@@ -400,36 +594,69 @@
     by_row = (row_count, sel_count)
 
     vectors = jnp.pad(jnp.stack([prenorm, midnorm, router], axis=1), ((0, 0), (0, 125)))
-    first_own = jnp.concatenate([attention[0], attention[1], attention[2], vectors], axis=1)
-    second_own = jnp.concatenate([mixing.T, expand], axis=1)
-    first_z = gather_z(cube, first_own)
-    second_z = gather_z(cube, second_own, [first_z])
-    down_z = gather_z(cube, contract.T, [second_z])
-    first = gather_second(cube, gather_first(cube, first_z))
-    second_parts = gather_first(cube, second_z)
-    second = gather_second(cube, second_parts)
-    mix, up = second[:, :half_width], second[:, half_width:]
-    down_parts = gather_first(cube, down_z)
-
-    positions = jnp.arange(length, dtype=jnp.int32)
-    hit = chosen[:, :, None] == positions[None, None, :]
-    one_hot = hit.astype(BF)
-    local_rows = jnp.einsum("bts,bsd->btd", one_hot, tokens, preferred_element_type=F32).astype(BF)
-    local_grads = jnp.einsum("bts,bsd->btd", one_hot, cotangent, preferred_element_type=F32).astype(BF)
-    seg_sel = jnp.sum(jnp.where(hit, segments[:, None, :], 0), axis=-1)
-    keep_sel = jnp.sum(jnp.where(hit, present[:, None, :], 0), axis=-1).astype(F32)
-    taken = jnp.any(hit, axis=1)[:, :, None]
-
-    both = both_halves(jnp.stack([local_rows, local_grads]))
+    cuts = thirds(hidden_here)
+    (first_own,) = call(
+        first_columns, (shape((own_rows, 4 * half_width + 128)),), (attention, mixing.T, vectors), name="first_columns"
+    )
+    first_far = start_exchange(cube, Part(first_own[None], []), cube.far[-1])
+    (second_own,) = call(
+        functools.partial(second_columns, cuts),
+        (shape((own_rows, 2 * hidden_here)),),
+        (expand, contract.T),
+        name="second_columns",
+    )
+    picked, bias, keep = select(tokens, cotangent, chosen, segments, present)
+
+    def spread(far, after, begin=()):
+        for bit in cube.far[-2::-1]:
+            far = start_exchange(cube, stack(cube, [far], [far_bit(far)], after)[0], bit)
+        column = stack(cube, [far], [far_bit(far)], after)[0]
+        ends = thirds(column.width)
+        found = call(
+            functools.partial(split_columns, ends),
+            [shape(column.value.shape[:2] + (end - start,)) for start, end in ends],
+            [column.value],
+            begin,
+            name="split_columns",
+        )
+        return [Part(v, column.bits) for v in found]
+
+    def far_bit(part):
+        return cube.far[-1 - len(part.bits)]
+
+    def step_bits(step):
+        return [order[step] for order in cube.orders]
+
+    def send(parts, step):
+        return [start_exchange(cube, p, bit) for p, bit in zip(parts, step_bits(step))]
+
+    steps = len(cube.orders[0])
+    first_parts = spread(first_far, [picked])
+    both = both_halves(tie(picked, first_parts[0].value))
     states = both[0].reshape(token_count, width)
     upstream = both[1].reshape(token_count, width)
-    keep = keep_sel.reshape(token_count, 1)
-    slots = jnp.arange(sel_count)
-    diagonal = slots[None, :] == slots[:, None]
-    causal = slots[None, :] <= slots[:, None]
-    same_doc = seg_sel[:, :, None] == seg_sel[:, None, :]
-    open_key = (keep_sel[:, None, :] > 0) | diagonal[None]
-    bias = jnp.where(causal[None] & same_doc & open_key, 0.0, -1e30).astype(F32)
+    first_parts = send(first_parts, 0)
+    second_far = start_exchange(cube, Part(tie(second_own, *arrived([first_far]))[None], []), cube.far[-1])
+    for step in range(1, steps):
+        after = arrived([second_far]) if step == steps - 1 else []
+        first_parts = send(stack(cube, first_parts, step_bits(step - 1), after), step)
+    first_last = [p.value for p in first_parts]
+    first = whole(cube, first_parts, step_bits(steps - 1))
+    mix = first[:, 3 * half_width : 4 * half_width]
+    second_parts = send(spread(second_far, [], first_last[:1]), 0)
+    second_begun = []
+    for step in range(1, steps - 1):
+        second_parts = stack(cube, second_parts, step_bits(step - 1), [first] if step == 1 else [])
+        second_begun = second_begun or [p.value for p in second_parts]
+        second_parts = send(second_parts, step)
+    second_parts = stack(cube, second_parts, step_bits(steps - 2))
+    each = hidden_here // 3
+    up_parts, down_parts = [], []
+    for p in second_parts:
+        up_parts.append(Part(p.value[..., :each], p.bits))
+        down_parts.append(Part(p.value[..., each:], p.bits))
+    up = whole(cube, send(up_parts, steps - 1), step_bits(steps - 1))
+    down_parts = send(down_parts, steps - 1)
 
     wide = shape((token_count, width))
     tall = shape((token_count, hidden_here))
@@ -444,7 +671,7 @@
             vector,
         ),
         (states, first, bias),
-        after=second_parts,
+        after=second_begun,
         flops=token_count * width * half_width * 6,
         name="attention_forward",
     )
@@ -459,7 +686,7 @@
         flops=4 * token_count * width * hidden_here,
         name="up_forward",
     )
-    down = gather_second(cube, down_parts, [activated])
+    down = whole(cube, down_parts, step_bits(steps - 1), [activated])
 
     hidden_grad, mid_own = call(
         functools.partial(down_backward, *by_row),
@@ -477,7 +704,15 @@
     )
     feed_other = other_core(feed_own)
     mid_other = tie(other_core(mid_own), feed_own)
-    down_grads = reduce_first(cube, down_grad, [feed_own])
+
+    def back_bits(step):
+        return [order[-1 - step] for order in cube.orders]
+
+    def alone(parts):
+        return [[p] for p in parts]
+
+    both_grads = [list(pair) for pair in zip(cut(cube, down_grad), cut(cube, up_grad))]
+    both_grads = fold(cube, both_grads, back_bits(0))
 
     mixed, packed_grad, pre_own, middle_grad, mid_gain_grad = call(
         functools.partial(attention_backward, *by_row),
@@ -489,62 +724,74 @@
             vector,
         ),
         (states, att_own, att_other, mid_own, mid_other, upstream, keep, gains, mix, first, packed, probs),
+        after=[both_grads[0].value],
         flops=10 * token_count * width * half_width,
         name="attention_backward",
     )
-    down_part = reduce_second(cube, down_grads, [packed_grad])
-    up_grads = reduce_first(cube, up_grad, [packed_grad])
+    finished, logit_grad, router_grad = call(
+        functools.partial(final_forward, *by_row),
+        (wide, shape((token_count, 1), F32), vector),
+        (states, upstream, att_own, att_other, feed_own, feed_other, gains, keep),
+        after=[packed_grad],
+        name="final_forward",
+    )
     (first_grad,) = call(
         projection_grads,
         (shape((width, 4 * half_width)),),
         (normed, packed_grad, mixed, context),
+        after=[finished],
         flops=8 * token_count * width * half_width,
         name="projection_grads",
     )
-    pre_other = tie(other_core(pre_own), first_grad)
-    finished, logit_grad, router_grad = call(
-        functools.partial(final_forward, *by_row),
-        (wide, shape((token_count, 1), F32), vector),
-        (states, upstream, att_own, att_other, feed_own, feed_other, gains, keep),
-        name="final_forward",
-    )
-    total_grad, pre_gain_grad = call(
+    both_grads = fold(cube, alone(both_grads), back_bits(1), [first_grad])
+    pre_other = other_core(tie(pre_own, both_grads[0].value))
+    total_grad, vector_grads = call(
         functools.partial(final_backward, *by_row),
-        (wide, vector),
-        (states, upstream, middle_grad, pre_own, pre_other, logit_grad, gains),
+        (wide, shape((width, 128))),
+        (states, upstream, middle_grad, pre_own, pre_other, logit_grad, gains, mid_gain_grad, router_grad),
+        scratch=[pltpu.VMEM((128, width), F32)],
         name="final_backward",
     )
-    up_part = reduce_second(cube, up_grads, [total_grad])
-    vector_grads = jnp.concatenate([pre_gain_grad[:1], mid_gain_grad[:1], router_grad[:1]])
-    vector_grads = jnp.pad(vector_grads.T, ((0, 0), (0, 125)))
-    vector_half = reduce_first(cube, vector_grads)
-    down_out = reduce_z(cube, down_part, [[total_grad], vector_half])
-    first_grads = reduce_first(cube, first_grad, vector_half)
-    vector_part = reduce_second(cube, vector_half)
-    first_part = reduce_second(cube, first_grads, [vector_part])
-    up_out = reduce_z(cube, up_part, [[vector_part], []])
-    first_out = reduce_z(cube, jnp.concatenate([first_part, vector_part], axis=-1))
-
-    offset = lax.axis_index("mp") * half_width
-
-    def put(base, values):
-        mine = lax.dynamic_slice_in_dim(values, offset, half_width, 1)
-        mine = mine.reshape(row_count, sel_count, half_width)
-        placed = jnp.einsum("bts,btd->bsd", one_hot, mine, preferred_element_type=F32).astype(BF)
-        return jnp.where(taken, placed, base)
-
-    attention_out = first_out[:, : 3 * half_width].reshape(own_rows, 3, half_width).transpose(1, 0, 2)
-    vector_out = first_out[:, 4 * half_width : 4 * half_width + 3]
+    first_grads = alone(cut(cube, first_grad))
+    first_grads[-1] += cut(cube, vector_grads)
+    first_grads = fold(cube, first_grads, back_bits(0))
+    result = put(tokens, chosen, finished, cube.bits, [first_grads[0].value])
+    tokens_grad = put(cotangent, chosen, total_grad, cube.bits, [result])
+    for step in range(2, steps):
+        both_grads = fold(cube, alone(both_grads), back_bits(step), [first_grad] if step == 2 else [])
+    for step in range(1, steps):
+        first_grads = fold(cube, alone(first_grads), back_bits(step), [result] if step == 1 else [])
+    both_grads, first_grads = [both_grads], [first_grads]
+    for bit in cube.far:
+        both_grads = [fold(cube, both_grads, [bit])]
+        first_grads = [fold(cube, first_grads, [bit])]
+    (both_grad,), (first_grad,) = both_grads[0], first_grads[0]
+    up_out, down_out = call(
+        functools.partial(sum_second, cuts),
+        (shape((own_rows, hidden_here), F32),) * 2,
+        (both_grad.value, both_grad.sent),
+        name="sum_second",
+    )
+    attention_out, mixing_out, vector_out = call(
+        sum_first,
+        (
+            shape((3, own_rows, half_width), F32),
+            shape((own_rows, half_width), F32),
+            shape((128, own_rows), F32),
+        ),
+        (first_grad.value, first_grad.sent),
+        name="sum_first",
+    )
     return (
-        put(tokens, tie(finished, *vector_half)),
-        put(cotangent, total_grad),
+        result,
+        tokens_grad,
         attention_out,
-        first_out[:, 3 * half_width : 4 * half_width].T,
+        mixing_out.T,
         up_out,
         down_out.T,
-        vector_out[:, 0],
-        vector_out[:, 1],
-        vector_out[:, 2],
+        vector_out[0],
+        vector_out[1],
+        vector_out[2],
     )
 
 

time: 214 us -> 187 us (0.87)
  Pallas kernels: 40.8 us -> 74.1 us
  matrix products: 19.4 us -> 0 us
  waiting for transfers between devices: 71.8 us -> 53.7 us
  other arithmetic: 17 us -> 2.47 us
  local copies, waits for them, and re-layouts: 17.2 us -> 9.64 us
    dot_general x4 -> x0, matrix products: 19.4 us -> none  [the longest x2 13.4 us: put(): jnp.einsum('bts,btd->bsd', one_hot, mine, preferred_element_type=F32)]
    pallas_call x0 -> x3, Pallas kernels: none -> 18.7 us  [the longest x2 10 us: put(): pl.pallas_call(body, grid=(rows, length // long), out_shape=shape(base.sh...]
    ppermute x38 -> x43, waiting for transfers between devices: 71.8 us -> 53.6 us  [swap(): lax.ppermute(value, 'dp', [(i, i ^ 1 << bit) for i in range(self.count)])]
    pallas_call x9 -> x32, Pallas kernels: 40.7 us -> 55.4 us  [call(): pl.pallas_call(body, out_shape=outs, in_specs=[pl.BlockSpec(memory_space=...]
    add x19 -> x0, other arithmetic: 3.99 us -> none  [halve(): mine.astype(F32) + tie(self.swap(sent.astype(BF), bit), *after).astype(F32)]
    another operation x34 -> x0, other arithmetic: 3.21 us -> none  [the longest x33 2.06 us: double(): jnp.stack([jnp.where(low, value, other), jnp.where(low, other, value)])]
    squeeze x7 -> x1, local copies, waits for them, and re-layouts: 3.41 us -> 0.52 us  [shards(): vector_out[2]]
    convert_element_type x12 -> x0, local copies, waits for them, and re-layouts: 2.71 us -> none  [halve(): sent.astype(BF)]
  transfers between devices with their start and end apart: 43 -> 48, of which waited for: 16 -> 23; matrix products, arithmetic and copies ran while one was open for 20% -> 1% of each run, Pallas kernels for 19% -> 36%
where the time goes in v4:
time: 187 us; the launch traced here: 186 us
  Pallas kernels  74.1 us (40%)
  waiting for transfers between devices  53.7 us (29%)
  starting transfers between devices  45.4 us (24%)
  local copies, waits for them, and re-layouts  9.64 us (5%)
  other arithmetic  2.47 us (1%)
    pallas_call x32, Pallas kernels, call(): pl.pallas_call(body, out_shape=outs, in_specs=[pl.BlockSpec(memory_space=...  55.4 us
    ppermute x43, waiting for transfers between devices, swap(): lax.ppermute(value, 'dp', [(i, i ^ 1 << bit) for i in range(self.count)])  53.6 us
    ppermute x43, starting transfers between devices, swap(): lax.ppermute(value, 'dp', [(i, i ^ 1 << bit) for i in range(self.count)])  44.6 us
    pallas_call x2, Pallas kernels, put(): pl.pallas_call(body, grid=(rows, length // long), out_shape=shape(base.sh...  10 us
    unnamed x35, local copies, waits for them, and re-layouts  8.71 us
    pallas_call x1, Pallas kernels, select(): pl.pallas_call(select_rows, grid=(rows,), out_shape=(shape((2, rows, sel,...  8.65 us
  transfers between devices with their start and end apart: 48, of which 23 were waited for; matrix products, arithmetic and copies ran while one was open for 1% of the time, Pallas kernels for 36%

profile of v4, /device:TPU:0, one launch (start us, length us, event | category | flops | bytes accessed | tf_op | source)
XLA Modules:
  0.0 186.3 jit_solution(15609302739085885722)
XLA Ops:
  3.1 4.1 %collective-permute-start = (bf16[1,48,1664]{2,1,0:T(8,128)(2,1)S(1)}, bf16[1,48,1664]{2,1,0:T(8,128)(2,1)S(1)}, u32[]{:S(2)}, u32[]{:S(2)}) collective-permute-start(bf16[1,48,1664]{2,1,0:T(8,128)(2,1)S(1)} %bitcast.142), channel_id=1, source_target_pairs={{0,16},{2,18},{4,20},{6,22},{8,24},{10,26},{12,28},{14,30},{16,0},... | collective-permute-start | bytes 479240 | tf_op jit(solution)/shard_map/ppermute | solution.py:408
  7.2 8.7 %select_rows.1 = (bf16[2,3,256,384]{3,2,1,0:T(8,128)(2,1)}, f32[3,256,256]{2,1,0:T(8,128)}, f32[768,1]{1,0:T(8,128)}) custom-call(bf16[3,2048,384]{2,1,0:T(8,128)(2,1)} %refs_3_.2, bf16[3,2048,384]{2,1,0:T(8,128)(2,1)} %refs_3_.3, s32[3,256]{1,0:T(4,128)} %refs_1_.3, s32[3,2048]{1,0:T(4,128)} %segments_ref.1, s32[3,2048]{1,0:T(4,128)} %present_ref.1), custom_call_target="tpu_custom_call" | custom-call | flops 2415919104 | bytes 9437184 | tf_op jit(solution)/shard_map/select_rows/pallas_call | solution.py:295
  18.5 1.6 collective-permute-start.3
  20.1 1.5 collective-permute-start.2
  21.6 1.6 collective-permute-start.4
  26.9 2.5 %collective-permute-start.6 = (bf16[4,48,640]{2,1,0:T(8,128)(2,1)S(1)}, bf16[4,48,640]{2,1,0:T(8,128)(2,1)S(1)}, u32[]{:S(2)}, u32[]{:S(2)}) collective-permute-start(bf16[4,48,640]{2,1,0:T(8,128)(2,1)S(1)} %bitcast.161), channel_id=1, source_target_pairs={{0,8},{2,10},{4,12},{6,14},{8,0},{10,2},{12,4},{14,6},{16,24},{18,... | collective-permute-start | bytes 737288 | tf_op jit(solution)/shard_map/ppermute | solution.py:408
  30.5 8.6 %collective-permute-done.8.refs_7_.refs_2_ = bf16[1,48,3072]{2,1,0:T(8,128)(2,1)S(1)} collective-permute-done((bf16[1,48,3072]{2,1,0:T(8,128)(2,1)S(1)}, bf16[1,48,3072]{2,1,0:T(8,128)(2,1)S(1)}, u32[]{:S(2)}, u32[]{:S(2)}) %collective-permute-start.8) | collective-permute-done | bytes 294944 | tf_op jit(solution)/shard_map/ppermute | solution.py:408
  44.2 6.1 %collective-permute-done.11.refs_6_ = bf16[8,48,512]{2,1,0:T(8,128)(2,1)S(1)} collective-permute-done((bf16[8,48,512]{2,1,0:T(8,128)(2,1)S(1)}, bf16[8,48,512]{2,1,0:T(8,128)(2,1)S(1)}, u32[]{:S(2)}, u32[]{:S(2)}) %collective-permute-start.11) | collective-permute-done | bytes 393248 | tf_op jit(solution)/shard_map/ppermute | solution.py:408
  51.5 3.1 %collective-permute-done.10.refs_4_ = bf16[8,48,640]{2,1,0:T(8,128)(2,1)S(1)} collective-permute-done((bf16[8,48,640]{2,1,0:T(8,128)(2,1)S(1)}, bf16[8,48,640]{2,1,0:T(8,128)(2,1)S(1)}, u32[]{:S(2)}, u32[]{:S(2)}) %collective-permute-start.10) | collective-permute-done | bytes 491552 | tf_op jit(solution)/shard_map/ppermute | solution.py:408
  58.9 1.6 collective-permute-start.16
  62.1 1.5 broadcast_select_fusion
  64.8 5.4 %attention_forward.1 = (bf16[768,768]{1,0:T(8,128)(2,1)S(1)}, bf16[768,1152]{1,0:T(8,128)(2,1)S(1)}, f32[3,6,256,256]{3,2,1,0:T(8,128)S(1)}, bf16[768,384]{1,0:T(8,128)(2,1)S(1)}, f32[8,768]{1,0:T(8,128)S(1)}) custom-call(bf16[768,768]{1,0:T(8,128)(2,1)S(1)} %bitcast.88, bf16[768,1664]{1,0:T(8,128)(2,1)S(1)} %bitcast.86, f32[3,256,256]{2,1,0:T(8,128)S(1)} %copy-done.5, ...), custom_call_target="tpu_custom_call" | custom-call | flops 1358954496 | bytes 12804096 | tf_op jit(solution)/shard_map/attention_forward/pallas_call | solution.py:42
  72.9 1.6 collective-permute-start.20
  76.3 7.6 %collective-permute-done.19.refs_2_ = bf16[8,48,512]{2,1,0:T(8,128)(2,1)S(1)} collective-permute-done((bf16[8,48,512]{2,1,0:T(8,128)(2,1)S(1)}, bf16[8,48,512]{2,1,0:T(8,128)(2,1)S(1)}, u32[]{:S(2)}, u32[]{:S(2)}) %collective-permute-start.19) | collective-permute-done | bytes 393248 | tf_op jit(solution)/shard_map/ppermute | solution.py:408
  83.9 1.5 collective-permute-start.23
  86.6 7.4 %up_forward.1 = (bf16[768,768]{1,0:T(8,128)(2,1)S(1)}, bf16[768,1536]{1,0:T(8,128)(2,1)S(1)}, bf16[768,1536]{1,0:T(8,128)(2,1)S(1)}, bf16[768,768]{1,0:T(8,128)(2,1)S(1)}, bf16[768,1536]{1,0:T(8,128)(2,1)S(1)}) custom-call(bf16[768,768]{1,0:T(8,128)(2,1)S(1)} %bitcast.89, bf16[768,768]{1,0:T(8,128)(2,1)S(1)} %bitcast.101, ...), custom_call_target="tpu_custom_call" | custom-call | flops 3623878656 | bytes 16542720 | tf_op jit(solution)/shard_map/up_forward/pallas_call | solution.py:42
  96.1 4.7 %down_backward.1 = (bf16[768,1536]{1,0:T(8,128)(2,1)S(1)}, bf16[768,768]{1,0:T(8,128)(2,1)S(1)}) custom-call(bf16[768,768]{1,0:T(8,128)(2,1)S(1)} %get-tuple-element.123.refs_0_, bf16[768,1536]{1,0:T(8,128)(2,1)S(1)} %bitcast.112, bf16[768,1536]{1,0:T(8,128)(2,1)S(1)} %get-tuple-element.125.refs_2_, bf16[768,1536]{1,0:T(8,128)(2,1)S(1)} %bitcast.115), custom_call_target="tpu_custom_call" | custom-call | flops 3623878656 | bytes 11796480 | tf_op jit(solution)/shard_map/down_backward/pallas_call | solution.py:42
  100.9 3.8 %down_forward.1 = (bf16[768,1536]{1,0:T(8,128)(2,1)S(1)}, bf16[768,768]{1,0:T(8,128)(2,1)S(1)}) custom-call(bf16[768,768]{1,0:T(8,128)(2,1)S(1)} %get-tuple-element.122.refs_0_, bf16[768,1536]{1,0:T(8,128)(2,1)S(1)} %get-tuple-element.126.refs_1_, bf16[768,1536]{1,0:T(8,128)(2,1)S(1)} %get-tuple-element.124.refs_7_.refs_2_, bf16[768,1536]{1,0:T(8,128)(2,1)S(1)} %bitcast.113), custom_call_target="tpu_custom_call" | custom-call | flops 3623878656 | bytes 11796480 | tf_op jit(solution)/shard_map/down_forward/pallas_call | solution.py:42
  108.8 11.9 %attention_backward.1 = (bf16[768,768]{1,0:T(8,128)(2,1)S(1)}, bf16[768,1152]{1,0:T(8,128)(2,1)S(1)}, bf16[768,768]{1,0:T(8,128)(2,1)S(1)}, f32[768,768]{1,0:T(8,128)S(1)}, f32[8,768]{1,0:T(8,128)S(1)}) custom-call(bf16[768,768]{1,0:T(8,128)(2,1)S(1)} %bitcast.90, bf16[768,768]{1,0:T(8,128)(2,1)S(1)} %mix_forward.1.refs_2_.refs_1_, ...), custom_call_target="tpu_custom_call" | custom-call | flops 2264924160 | bytes 23251968 | tf_op jit(solution)/shard_map/attention_backward/pallas_call | solution.py:42
  120.8 1.7 final_forward.1
  122.5 2.4 %projection_grads.1.refs_7_ = bf16[768,1536]{1,0:T(8,128)(2,1)S(1)} custom-call(bf16[768,768]{1,0:T(8,128)(2,1)S(1)} %get-tuple-element.136.refs_0_, bf16[768,1152]{1,0:T(8,128)(2,1)S(1)} %get-tuple-element.134.refs_8_.refs_1_, bf16[768,768]{1,0:T(8,128)(2,1)S(1)} %get-tuple-element.137.refs_2_, bf16[768,384]{1,0:T(8,128)(2,1)S(1)} %get-tuple-element.116.refs_0_.refs_3_, ...), custom_call_target="tpu_custom_call" | custom-call | flops 1811939328 | bytes 7077888 | tf_op jit(solution)/shard_map/projection_grads/pallas_call | solution.py:42
  131.1 2.0 %final_backward.1 = (bf16[768,768]{1,0:T(8,128)(2,1)S(1)}, bf16[768,128]{1,0:T(8,128)(2,1)S(1)}) custom-call(bf16[768,768]{1,0:T(8,128)(2,1)S(1)} %bitcast.92, bf16[768,768]{1,0:T(8,128)(2,1)S(1)} %bitcast.104, f32[768,768]{1,0:T(8,128)S(1)} %get-tuple-element.138.refs_2_, bf16[768,768]{1,0:T(8,128)(2,1)S(1)} %get-tuple-element.139.refs_3_, ...), custom_call_target="tpu_custom_call" | custom-call | bytes 8530944 | tf_op jit(solution)/shard_map/final_backward/pallas_call | solution.py:42
  136.3 4.0 %collective-permute-done.41 = bf16[4,48,1024]{2,1,0:T(8,128)(2,1)S(1)} collective-permute-done((bf16[4,48,1024]{2,1,0:T(8,128)(2,1)S(1)}, bf16[4,48,1024]{2,1,0:T(8,128)(2,1)S(1)}, u32[]{:S(2)}, u32[]{:S(2)}) %collective-permute-start.41) | collective-permute-done | bytes 393248 | tf_op jit(solution)/shard_map/ppermute | solution.py:408
  144.3 4.2 %collective-permute-done.31 = bf16[8,48,512]{2,1,0:T(8,128)(2,1)S(1)} collective-permute-done((bf16[8,48,512]{2,1,0:T(8,128)(2,1)S(1)}, bf16[8,48,512]{2,1,0:T(8,128)(2,1)S(1)}, u32[]{:S(2)}, u32[]{:S(2)}) %collective-permute-start.31) | collective-permute-done | bytes 393248 | tf_op jit(solution)/shard_map/ppermute | solution.py:408
  149.3 5.0 %put_rows.2.refs_4_.refs_7_ = bf16[3,2048,384]{2,1,0:T(8,128)(2,1)} custom-call(s32[5]{0:T(128)S(1)} %pad_add_fusion.refs_0_, s32[3,256]{1,0:T(4,128)S(1)} %copy-done.11, bf16[768,768]{1,0:T(8,128)(2,1)S(1)} %get-tuple-element.135.refs_4_.refs_2_, bf16[3,2048,384]{2,1,0:T(8,128)(2,1)S(1)} %bitcast.106, f32[8,48,512]{2,1,0:T(8,128)S(1)} %get-tuple-element.150.refs_4_), custom_call_target="tpu_custom_call" | custom-call | flops 1207959552 | bytes 9437184 | tf_op jit(solution)/shard_map/put_rows/pallas_call | solution.py:337
  154.4 2.3 %copy-done = bf16[3,2048,384]{2,1,0:T(8,128)(2,1)S(1)} copy-done((bf16[3,2048,384]{2,1,0:T(8,128)(2,1)S(1)}, bf16[3,2048,384]{2,1,0:T(8,128)(2,1)}, u32[]{:S(2)}) %copy-start) | copy-done | bytes 4718616
  158.9 1.5 collective-permute-start.34
  162.4 2.2 %collective-permute-done.34 = bf16[4,48,512]{2,1,0:T(8,128)(2,1)S(1)} collective-permute-done((bf16[4,48,512]{2,1,0:T(8,128)(2,1)S(1)}, bf16[4,48,512]{2,1,0:T(8,128)(2,1)S(1)}, u32[]{:S(2)}, u32[]{:S(2)}) %collective-permute-start.34) | collective-permute-done | bytes 196640 | tf_op jit(solution)/shard_map/ppermute | solution.py:408
  164.5 4.7 %collective-permute-done.35 = bf16[4,48,512]{2,1,0:T(8,128)(2,1)S(1)} collective-permute-done((bf16[4,48,512]{2,1,0:T(8,128)(2,1)S(1)}, bf16[4,48,512]{2,1,0:T(8,128)(2,1)S(1)}, u32[]{:S(2)}, u32[]{:S(2)}) %collective-permute-start.35) | collective-permute-done | bytes 196640 | tf_op jit(solution)/shard_map/ppermute | solution.py:408
  171.3 3.4 %collective-permute-done.37 = bf16[2,48,512]{2,1,0:T(8,128)(2,1)S(1)} collective-permute-done((bf16[2,48,512]{2,1,0:T(8,128)(2,1)S(1)}, bf16[2,48,512]{2,1,0:T(8,128)(2,1)S(1)}, u32[]{:S(2)}, u32[]{:S(2)}) %collective-permute-start.37) | collective-permute-done | bytes 98336 | tf_op jit(solution)/shard_map/ppermute | solution.py:408
  175.4 2.1 %collective-permute-done.39 = bf16[2,48,640]{2,1,0:T(8,128)(2,1)S(1)} collective-permute-done((bf16[2,48,640]{2,1,0:T(8,128)(2,1)S(1)}, bf16[2,48,640]{2,1,0:T(8,128)(2,1)S(1)}, u32[]{:S(2)}, u32[]{:S(2)}) %collective-permute-start.39) | collective-permute-done | bytes 122912 | tf_op jit(solution)/shard_map/ppermute | solution.py:408
  179.9 5.0 %put_rows.3 = bf16[3,2048,384]{2,1,0:T(8,128)(2,1)} custom-call(s32[5]{0:T(128)S(1)} %pad_add_fusion.refs_0_, s32[3,256]{1,0:T(4,128)S(1)} %copy-done.11, bf16[768,768]{1,0:T(8,128)(2,1)S(1)} %get-tuple-element.151.refs_2_, bf16[3,2048,384]{2,1,0:T(8,128)(2,1)S(1)} %bitcast.100, bf16[3,2048,384]{2,1,0:T(8,128)(2,1)S(1)} %copy-done.1), custom_call_target="tpu_custom_call" | custom-call | flops 1207959552 | bytes 9437184 | tf_op jit(solution)/shard_map/put_rows/pallas_call | solution.py:337
  (152 shorter events, 60.0 us)
Async XLA Ops:
  3.1 12.8 %collective-permute-start = (bf16[1,48,1664]{2,1,0:T(8,128)(2,1)S(1)}, bf16[1,48,1664]{2,1,0:T(8,128)(2,1)S(1)}, u32[]{:S(2)}, u32[]{:S(2)}) collective-permute-start(bf16[1,48,1664]{2,1,0:T(8,128)(2,1)S(1)} %bitcast.142), channel_id=1, source_target_pairs={{0,16},{2,18},{4,20},{6,22},{8,24},{10,26},{12,28},{14,30},{16,0},... | collective-permute-start | bytes 479240 | tf_op jit(solution)/shard_map/ppermute | solution.py:408
  18.5 43.6 %collective-permute-start.1 = (bf16[2,3,256,384]{3,2,1,0:T(8,128)(2,1)S(1)}, bf16[2,3,256,384]{3,2,1,0:T(8,128)(2,1)}, u32[]{:S(2)}, u32[]{:S(2)}) collective-permute-start(bf16[2,3,256,384]{3,2,1,0:T(8,128)(2,1)S(1)} %shard_map.187), channel_id=1, source_target_pairs={{0,1},{1,0},{2,3},{3,2},{4,5},{5,4},{6,7},{7,6},{8,9},{9,8},{10,11... | collective-permute-start | bytes 3538952 | tf_op jit(solution)/shard_map/ppermute | solution.py:562
  23.2 15.8 %collective-permute-start.8 = (bf16[1,48,3072]{2,1,0:T(8,128)(2,1)S(1)}, bf16[1,48,3072]{2,1,0:T(8,128)(2,1)S(1)}, u32[]{:S(2)}, u32[]{:S(2)}) collective-permute-start(bf16[1,48,3072]{2,1,0:T(8,128)(2,1)S(1)} %bitcast.110), channel_id=1, source_target_pairs={{0,16},{2,18},{4,20},{6,22},{8,24},{10,26},{12,28},{14,30},{16,0},... | collective-permute-start | bytes 884744 | tf_op jit(solution)/shard_map/ppermute | solution.py:408
  26.9 12.5 %collective-permute-start.6 = (bf16[4,48,640]{2,1,0:T(8,128)(2,1)S(1)}, bf16[4,48,640]{2,1,0:T(8,128)(2,1)S(1)}, u32[]{:S(2)}, u32[]{:S(2)}) collective-permute-start(bf16[4,48,640]{2,1,0:T(8,128)(2,1)S(1)} %bitcast.161), channel_id=1, source_target_pairs={{0,8},{2,10},{4,12},{6,14},{8,0},{10,2},{12,4},{14,6},{16,24},{18,... | collective-permute-start | bytes 737288 | tf_op jit(solution)/shard_map/ppermute | solution.py:408
  40.0 10.2 %collective-permute-start.11 = (bf16[8,48,512]{2,1,0:T(8,128)(2,1)S(1)}, bf16[8,48,512]{2,1,0:T(8,128)(2,1)S(1)}, u32[]{:S(2)}, u32[]{:S(2)}) collective-permute-start(bf16[8,48,512]{2,1,0:T(8,128)(2,1)S(1)} %bitcast.158), channel_id=1, source_target_pairs={{0,4},{2,6},{4,0},{6,2},{8,12},{10,14},{12,8},{14,10},{16,20},{18,... | collective-permute-start | bytes 1179656 | tf_op jit(solution)/shard_map/ppermute | solution.py:408
  40.8 10.0 %collective-permute-start.9 = (bf16[8,48,512]{2,1,0:T(8,128)(2,1)S(1)}, bf16[8,48,512]{2,1,0:T(8,128)(2,1)S(1)}, u32[]{:S(2)}, u32[]{:S(2)}) collective-permute-start(bf16[8,48,512]{2,1,0:T(8,128)(2,1)S(1)} %bitcast.128), channel_id=1, source_target_pairs={{0,8},{2,10},{4,12},{6,14},{8,0},{10,2},{12,4},{14,6},{16,24},{18,... | collective-permute-start | bytes 1179656 | tf_op jit(solution)/shard_map/ppermute | solution.py:408
  40.8 13.9 %collective-permute-start.10 = (bf16[8,48,640]{2,1,0:T(8,128)(2,1)S(1)}, bf16[8,48,640]{2,1,0:T(8,128)(2,1)S(1)}, u32[]{:S(2)}, u32[]{:S(2)}) collective-permute-start(bf16[8,48,640]{2,1,0:T(8,128)(2,1)S(1)} %bitcast.146), channel_id=1, source_target_pairs={{0,2},{2,0},{4,6},{6,4},{8,10},{10,8},{12,14},{14,12},{16,18},{18,... | collective-permute-start | bytes 1474568 | tf_op jit(solution)/shard_map/ppermute | solution.py:408
  43.3 13.6 %collective-permute-start.12 = (bf16[2,48,1024]{2,1,0:T(8,128)(2,1)S(1)}, bf16[2,48,1024]{2,1,0:T(8,128)(2,1)}, u32[]{:S(2)}, u32[]{:S(2)}) collective-permute-start(bf16[2,48,1024]{2,1,0:T(8,128)(2,1)S(1)} %get-tuple-element.110.refs_1_), channel_id=1, source_target_pairs={{0,2},{2,0},{4,6},{6,4},{8,10},{10,8},{12,14},{14,12},{16,18},{18,... | collective-permute-start | bytes 589832 | tf_op jit(solution)/shard_map/ppermute | solution.py:408
  58.9 12.2 %collective-permute-start.16 = (bf16[4,48,1024]{2,1,0:T(8,128)(2,1)S(1)}, bf16[4,48,1024]{2,1,0:T(8,128)(2,1)S(1)}, u32[]{:S(2)}, u32[]{:S(2)}) collective-permute-start(bf16[4,48,1024]{2,1,0:T(8,128)(2,1)S(1)} %bitcast.119), channel_id=1, source_target_pairs={{0,4},{2,6},{4,0},{6,2},{8,12},{10,14},{12,8},{14,10},{16,20},{18,... | collective-permute-start | bytes 1179656 | tf_op jit(solution)/shard_map/ppermute | solution.py:408
  60.5 10.6 %collective-permute-start.17 = (bf16[4,48,1024]{2,1,0:T(8,128)(2,1)S(1)}, bf16[4,48,1024]{2,1,0:T(8,128)(2,1)S(1)}, u32[]{:S(2)}, u32[]{:S(2)}) collective-permute-start(bf16[4,48,1024]{2,1,0:T(8,128)(2,1)S(1)} %bitcast.122), channel_id=1, source_target_pairs={{0,8},{2,10},{4,12},{6,14},{8,0},{10,2},{12,4},{14,6},{16,24},{18,... | collective-permute-start | bytes 1179656 | tf_op jit(solution)/shard_map/ppermute | solution.py:408
  71.0 15.6 %collective-permute-start.15 = (bf16[768,768]{1,0:T(8,128)(2,1)S(1)}, bf16[768,768]{1,0:T(8,128)(2,1)S(1)}, u32[]{:S(2)}, u32[]{:S(2)}) collective-permute-start(bf16[768,768]{1,0:T(8,128)(2,1)S(1)} %mix_forward.1.refs_2_.refs_1_), channel_id=1, source_target_pairs={{0,1},{1,0},{2,3},{3,2},{4,5},{5,4},{6,7},{7,6},{8,9},{9,8},{10,11... | collective-permute-start | bytes 3538952 | tf_op jit(solution)/shard_map/ppermute | solution.py:562
  71.9 12.0 %collective-permute-start.19 = (bf16[8,48,512]{2,1,0:T(8,128)(2,1)S(1)}, bf16[8,48,512]{2,1,0:T(8,128)(2,1)S(1)}, u32[]{:S(2)}, u32[]{:S(2)}) collective-permute-start(bf16[8,48,512]{2,1,0:T(8,128)(2,1)S(1)} %get-tuple-element.198.refs_1_), channel_id=1, source_target_pairs={{0,8},{2,10},{4,12},{6,14},{8,0},{10,2},{12,4},{14,6},{16,24},{18,... | collective-permute-start | bytes 1179656 | tf_op jit(solution)/shard_map/ppermute | solution.py:408
  72.9 12.5 %collective-permute-start.20 = (bf16[8,48,512]{2,1,0:T(8,128)(2,1)S(1)}, bf16[8,48,512]{2,1,0:T(8,128)(2,1)S(1)}, u32[]{:S(2)}, u32[]{:S(2)}) collective-permute-start(bf16[8,48,512]{2,1,0:T(8,128)(2,1)S(1)} %get-tuple-element.196.refs_3_), channel_id=1, source_target_pairs={{0,2},{2,0},{4,6},{6,4},{8,10},{10,8},{12,14},{14,12},{16,18},{18,... | collective-permute-start | bytes 1179656 | tf_op jit(solution)/shard_map/ppermute | solution.py:408
  74.6 11.3 %collective-permute-start.21 = (bf16[8,48,512]{2,1,0:T(8,128)(2,1)S(1)}, bf16[8,48,512]{2,1,0:T(8,128)(2,1)S(1)}, u32[]{:S(2)}, u32[]{:S(2)}) collective-permute-start(bf16[8,48,512]{2,1,0:T(8,128)(2,1)S(1)} %get-tuple-element.194.refs_5_), channel_id=1, source_target_pairs={{0,4},{2,6},{4,0},{6,2},{8,12},{10,14},{12,8},{14,10},{16,20},{18,... | collective-permute-start | bytes 1179656 | tf_op jit(solution)/shard_map/ppermute | solution.py:408
  75.1 18.9 %collective-permute-start.22 = (bf16[8,48,512]{2,1,0:T(8,128)(2,1)S(1)}, bf16[8,48,512]{2,1,0:T(8,128)(2,1)S(1)}, u32[]{:S(2)}, u32[]{:S(2)}) collective-permute-start(bf16[8,48,512]{2,1,0:T(8,128)(2,1)S(1)} %get-tuple-element.197.refs_1_), channel_id=1, source_target_pairs={{0,8},{2,10},{4,12},{6,14},{8,0},{10,2},{12,4},{14,6},{16,24},{18,... | collective-permute-start | bytes 1179656 | tf_op jit(solution)/shard_map/ppermute | solution.py:408
  83.9 10.3 %collective-permute-start.23 = (bf16[8,48,512]{2,1,0:T(8,128)(2,1)S(1)}, bf16[8,48,512]{2,1,0:T(8,128)(2,1)S(1)}, u32[]{:S(2)}, u32[]{:S(2)}) collective-permute-start(bf16[8,48,512]{2,1,0:T(8,128)(2,1)S(1)} %get-tuple-element.195.refs_3_), channel_id=1, source_target_pairs={{0,2},{2,0},{4,6},{6,4},{8,10},{10,8},{12,14},{14,12},{16,18},{18,... | collective-permute-start | bytes 1179656 | tf_op jit(solution)/shard_map/ppermute | solution.py:408
  85.4 10.0 %collective-permute-start.24 = (bf16[8,48,512]{2,1,0:T(8,128)(2,1)S(1)}, bf16[8,48,512]{2,1,0:T(8,128)(2,1)S(1)}, u32[]{:S(2)}, u32[]{:S(2)}) collective-permute-start(bf16[8,48,512]{2,1,0:T(8,128)(2,1)S(1)} %get-tuple-element.193.refs_5_), channel_id=1, source_target_pairs={{0,4},{2,6},{4,0},{6,2},{8,12},{10,14},{12,8},{14,10},{16,20},{18,... | collective-permute-start | bytes 1179656 | tf_op jit(solution)/shard_map/ppermute | solution.py:408
  104.8 16.0 %collective-permute-start.25 = (bf16[768,768]{1,0:T(8,128)(2,1)S(1)}, bf16[768,768]{1,0:T(8,128)(2,1)S(1)}, u32[]{:S(2)}, u32[]{:S(2)}) collective-permute-start(bf16[768,768]{1,0:T(8,128)(2,1)S(1)} %get-tuple-element.127.refs_1_.refs_4_), channel_id=1, source_target_pairs={{0,1},{1,0},{2,3},{3,2},{4,5},{5,4},{6,7},{7,6},{8,9},{9,8},{10,11... | collective-permute-start | bytes 3538952 | tf_op jit(solution)/shard_map/ppermute | solution.py:562
  106.3 19.5 %collective-permute-start.27 = (bf16[8,48,1024]{2,1,0:T(8,128)(2,1)S(1)}, bf16[8,48,1024]{2,1,0:T(8,128)(2,1)S(1)}, u32[]{:S(2)}, u32[]{:S(2)}) collective-permute-start(bf16[8,48,1024]{2,1,0:T(8,128)(2,1)S(1)} %get-tuple-element.140), channel_id=1, source_target_pairs={{0,8},{2,10},{4,12},{6,14},{8,0},{10,2},{12,4},{14,6},{16,24},{18,... | collective-permute-start | bytes 2359304 | tf_op jit(solution)/shard_map/ppermute | solution.py:408
  107.3 19.2 %collective-permute-start.28 = (bf16[8,48,1024]{2,1,0:T(8,128)(2,1)S(1)}, bf16[8,48,1024]{2,1,0:T(8,128)(2,1)S(1)}, u32[]{:S(2)}, u32[]{:S(2)}) collective-permute-start(bf16[8,48,1024]{2,1,0:T(8,128)(2,1)S(1)} %get-tuple-element.142), channel_id=1, source_target_pairs={{0,2},{2,0},{4,6},{6,4},{8,10},{10,8},{12,14},{14,12},{16,18},{18,... | collective-permute-start | bytes 2359304 | tf_op jit(solution)/shard_map/ppermute | solution.py:408
  108.3 18.9 %collective-permute-start.29 = (bf16[8,48,1024]{2,1,0:T(8,128)(2,1)S(1)}, bf16[8,48,1024]{2,1,0:T(8,128)(2,1)S(1)}, u32[]{:S(2)}, u32[]{:S(2)}) collective-permute-start(bf16[8,48,1024]{2,1,0:T(8,128)(2,1)S(1)} %get-tuple-element.144), channel_id=1, source_target_pairs={{0,4},{2,6},{4,0},{6,2},{8,12},{10,14},{12,8},{14,10},{16,20},{18,... | collective-permute-start | bytes 2359304 | tf_op jit(solution)/shard_map/ppermute | solution.py:408
  128.3 12.0 %collective-permute-start.41 = (bf16[4,48,1024]{2,1,0:T(8,128)(2,1)S(1)}, bf16[4,48,1024]{2,1,0:T(8,128)(2,1)S(1)}, u32[]{:S(2)}, u32[]{:S(2)}) collective-permute-start(bf16[4,48,1024]{2,1,0:T(8,128)(2,1)S(1)} %get-tuple-element.173), channel_id=1, source_target_pairs={{0,4},{2,6},{4,0},{6,2},{8,12},{10,14},{12,8},{14,10},{16,20},{18,... | collective-permute-start | bytes 1179656 | tf_op jit(solution)/shard_map/ppermute | solution.py:408
  128.8 12.4 %collective-permute-start.42 = (bf16[4,48,1024]{2,1,0:T(8,128)(2,1)S(1)}, bf16[4,48,1024]{2,1,0:T(8,128)(2,1)S(1)}, u32[]{:S(2)}, u32[]{:S(2)}) collective-permute-start(bf16[4,48,1024]{2,1,0:T(8,128)(2,1)S(1)} %get-tuple-element.175), channel_id=1, source_target_pairs={{0,8},{2,10},{4,12},{6,14},{8,0},{10,2},{12,4},{14,6},{16,24},{18,... | collective-permute-start | bytes 1179656 | tf_op jit(solution)/shard_map/ppermute | solution.py:408
  129.7 11.6 %collective-permute-start.43 = (bf16[4,48,1024]{2,1,0:T(8,128)(2,1)S(1)}, bf16[4,48,1024]{2,1,0:T(8,128)(2,1)S(1)}, u32[]{:S(2)}, u32[]{:S(2)}) collective-permute-start(bf16[4,48,1024]{2,1,0:T(8,128)(2,1)S(1)} %get-tuple-element.177), channel_id=1, source_target_pairs={{0,2},{2,0},{4,6},{6,4},{8,10},{10,8},{12,14},{14,12},{16,18},{18,... | collective-permute-start | bytes 1179656 | tf_op jit(solution)/shard_map/ppermute | solution.py:408
  133.9 14.6 %collective-permute-start.31 = (bf16[8,48,512]{2,1,0:T(8,128)(2,1)S(1)}, bf16[8,48,512]{2,1,0:T(8,128)(2,1)S(1)}, u32[]{:S(2)}, u32[]{:S(2)}) collective-permute-start(bf16[8,48,512]{2,1,0:T(8,128)(2,1)S(1)} %get-tuple-element.152), channel_id=1, source_target_pairs={{0,8},{2,10},{4,12},{6,14},{8,0},{10,2},{12,4},{14,6},{16,24},{18,... | collective-permute-start | bytes 1179656 | tf_op jit(solution)/shard_map/ppermute | solution.py:408
  134.8 19.5 %collective-permute-start.33 = (bf16[8,48,640]{2,1,0:T(8,128)(2,1)S(1)}, bf16[8,48,640]{2,1,0:T(8,128)(2,1)S(1)}, u32[]{:S(2)}, u32[]{:S(2)}) collective-permute-start(bf16[8,48,640]{2,1,0:T(8,128)(2,1)S(1)} %get-tuple-element.156), channel_id=1, source_target_pairs={{0,4},{2,6},{4,0},{6,2},{8,12},{10,14},{12,8},{14,10},{16,20},{18,... | collective-permute-start | bytes 1474568 | tf_op jit(solution)/shard_map/ppermute | solution.py:408
  140.3 14.1 %collective-permute-start.32 = (bf16[8,48,512]{2,1,0:T(8,128)(2,1)S(1)}, bf16[8,48,512]{2,1,0:T(8,128)(2,1)S(1)}, u32[]{:S(2)}, u32[]{:S(2)}) collective-permute-start(bf16[8,48,512]{2,1,0:T(8,128)(2,1)S(1)} %get-tuple-element.154), channel_id=1, source_target_pairs={{0,2},{2,0},{4,6},{6,4},{8,10},{10,8},{12,14},{14,12},{16,18},{18,... | collective-permute-start | bytes 1179656 | tf_op jit(solution)/shard_map/ppermute | solution.py:408
  142.0 18.4 %collective-permute-start.44 = (bf16[2,48,1024]{2,1,0:T(8,128)(2,1)S(1)}, bf16[2,48,1024]{2,1,0:T(8,128)(2,1)S(1)}, u32[]{:S(2)}, u32[]{:S(2)}) collective-permute-start(bf16[2,48,1024]{2,1,0:T(8,128)(2,1)S(1)} %get-tuple-element.179), channel_id=1, source_target_pairs={{0,2},{2,0},{4,6},{6,4},{8,10},{10,8},{12,14},{14,12},{16,18},{18,... | collective-permute-start | bytes 589832 | tf_op jit(solution)/shard_map/ppermute | solution.py:408
  143.1 18.2 %collective-permute-start.45 = (bf16[2,48,1024]{2,1,0:T(8,128)(2,1)S(1)}, bf16[2,48,1024]{2,1,0:T(8,128)(2,1)S(1)}, u32[]{:S(2)}, u32[]{:S(2)}) collective-permute-start(bf16[2,48,1024]{2,1,0:T(8,128)(2,1)S(1)} %get-tuple-element.181), channel_id=1, source_target_pairs={{0,4},{2,6},{4,0},{6,2},{8,12},{10,14},{12,8},{14,10},{16,20},{18,... | collective-permute-start | bytes 589832 | tf_op jit(solution)/shard_map/ppermute | solution.py:408
  148.4 12.8 %collective-permute-start.46 = (bf16[2,48,1024]{2,1,0:T(8,128)(2,1)S(1)}, bf16[2,48,1024]{2,1,0:T(8,128)(2,1)S(1)}, u32[]{:S(2)}, u32[]{:S(2)}) collective-permute-start(bf16[2,48,1024]{2,1,0:T(8,128)(2,1)S(1)} %get-tuple-element.183), channel_id=1, source_target_pairs={{0,8},{2,10},{4,12},{6,14},{8,0},{10,2},{12,4},{14,6},{16,24},{18,... | collective-permute-start | bytes 589832 | tf_op jit(solution)/shard_map/ppermute | solution.py:408
  157.5 11.8 %collective-permute-start.36 = (bf16[4,48,640]{2,1,0:T(8,128)(2,1)S(1)}, bf16[4,48,640]{2,1,0:T(8,128)(2,1)S(1)}, u32[]{:S(2)}, u32[]{:S(2)}) collective-permute-start(bf16[4,48,640]{2,1,0:T(8,128)(2,1)S(1)} %get-tuple-element.162), channel_id=1, source_target_pairs={{0,2},{2,0},{4,6},{6,4},{8,10},{10,8},{12,14},{14,12},{16,18},{18,... | collective-permute-start | bytes 737288 | tf_op jit(solution)/shard_map/ppermute | solution.py:408
  161.9 17.0 %collective-permute-start.47 = (bf16[1,48,3072]{2,1,0:T(8,128)(2,1)S(1)}, bf16[1,48,3072]{2,1,0:T(8,128)(2,1)S(1)}, u32[]{:S(2)}, u32[]{:S(2)}) collective-permute-start(bf16[1,48,3072]{2,1,0:T(8,128)(2,1)S(1)} %get-tuple-element.185), channel_id=1, source_target_pairs={{0,16},{2,18},{4,20},{6,22},{8,24},{10,26},{12,28},{14,30},{16,0},... | collective-permute-start | bytes 884744 | tf_op jit(solution)/shard_map/ppermute | solution.py:408
  (33 other events, 242.2 us)

commit v5 on v4

--- a/solution.py
+++ b/solution.py
@@ -68,15 +68,18 @@
     gain = gains_ref[0:1, :]
     scale = HD ** (-0.5)
 
-    @pl.loop(0, rows)
+    for row in range(rows):
+        here = slice(row * sel, (row + 1) * sel)
+        states = states_ref[here, :].astype(F32)
+        normed_ref[here, :] = (states * inverse_rms(states) * gain).astype(BF)
+    for start in range(0, 3 * half, 384):
+        packed_ref[:, start : start + 384] = mm(normed_ref[...], weights_ref[:, start : start + 384]).astype(BF)
+    first = first_head()
+
+    @pl.loop(0, rows, unroll=True)
     def _(row):
         here = pl.ds(pl.multiple_of(row * sel, sel), sel)
-        states = states_ref[here, :].astype(F32)
-        normed = (states * inverse_rms(states) * gain).astype(BF)
-        normed_ref[here, :] = normed
-        packed_ref[here, :] = mm(normed, weights_ref[:, : 3 * half]).astype(BF)
         bias = bias_ref[row]
-        first = first_head()
         for pair in range(half // (2 * HD)):
             at = pair * 2 * HD
             queries = packed_ref[here, at : at + 2 * HD]
@@ -114,40 +117,41 @@
         middle = states + (own_ref[here, :].astype(F32) + other_ref[here, :].astype(F32))
         normed = (middle * inverse_rms(middle) * mid_gain).astype(BF)
         normed_ref[here, :] = normed
-        chunk = 512
-        for at in range(0, up_ref.shape[1], chunk):
-            hidden = mm(normed, up_ref[:, at : at + chunk])
-            square = hidden * hidden
-            bent = jnp.tanh(c * hidden * (1.0 + a * square))
-            activated_ref[here, at : at + chunk] = (0.5 * hidden * (1.0 + bent)).astype(BF)
-            slope = 0.5 * (1.0 + bent) + 0.5 * c * hidden * (1.0 - bent * bent) * (1.0 + 3.0 * a * square)
-            slope_ref[here, at : at + chunk] = slope.astype(BF)
-
-    tall = 256
-    for at in range(0, grad_ref.shape[0], tall):
-        grad_ref[at : at + tall, :] = mm_tn(feed_grad_ref[:, at : at + tall], activated_ref[...]).astype(BF)
-
-
-def down_backward(rows, sel, feed_grad_ref, down_ref, slope_ref, up_ref, hidden_grad_ref, out_ref):
-    @pl.loop(0, rows)
-    def _(row):
-        here = pl.ds(pl.multiple_of(row * sel, sel), sel)
-        feed_grad = feed_grad_ref[here, :]
-        chunk = 512
-        for at in range(0, down_ref.shape[1], chunk):
-            act_grad = mm(feed_grad, down_ref[:, at : at + chunk])
-            hidden_grad_ref[here, at : at + chunk] = (
-                act_grad * slope_ref[here, at : at + chunk].astype(F32)
-            ).astype(BF)
-        out_ref[here, :] = mm_nt(hidden_grad_ref[here, :], up_ref[...]).astype(BF)
+
+    upright_grad = feed_grad_ref[...].T
+    chunk = 256
+    for at in range(0, up_ref.shape[1], chunk):
+        here = slice(at, at + chunk)
+        hidden = mm(normed_ref[...], up_ref[:, here])
+        square = hidden * hidden
+        share = 0.5 * jnp.tanh(hidden * (c + c * a * square)) + 0.5
+        activated = hidden * share
+        activated_ref[:, here] = activated.astype(BF)
+        slope = share + activated * (1.0 - share) * (2.0 * c + 6.0 * a * c * square)
+        slope_ref[:, here] = slope.astype(BF)
+        grad_ref[:, here] = mm(upright_grad, activated_ref[:, here]).astype(BF)
+
+
+def down_backward(feed_grad_ref, down_ref, slope_ref, up_ref, hidden_grad_ref, out_ref):
+    chunk = 256
+    for at in range(0, down_ref.shape[1], chunk):
+        here = slice(at, at + chunk)
+        act_grad = mm(feed_grad_ref[...], down_ref[:, here])
+        hidden_grad_ref[:, here] = (act_grad * slope_ref[:, here].astype(F32)).astype(BF)
+    for at in range(0, out_ref.shape[1], chunk):
+        here = slice(at, at + chunk)
+        out_ref[:, here] = mm_nt(hidden_grad_ref[...], up_ref[here, :]).astype(BF)
 
 
 def down_forward(normed_ref, hidden_grad_ref, activated_ref, down_ref, grad_ref, out_ref):
-    tall = 256
-    for at in range(0, grad_ref.shape[0], tall):
-        grad_ref[at : at + tall, :] = mm_tn(normed_ref[:, at : at + tall], hidden_grad_ref[...]).astype(BF)
-    for at in range(0, out_ref.shape[0], tall):
-        out_ref[at : at + tall, :] = mm_nt(activated_ref[at : at + tall, :], down_ref[...]).astype(BF)
+    upright_normed = normed_ref[...].T
+    chunk = 256
+    for at in range(0, grad_ref.shape[1], chunk):
+        here = slice(at, at + chunk)
+        grad_ref[:, here] = mm(upright_normed, hidden_grad_ref[:, here]).astype(BF)
+    for at in range(0, out_ref.shape[1], chunk):
+        here = slice(at, at + chunk)
+        out_ref[:, here] = mm_nt(activated_ref[...], down_ref[here, :]).astype(BF)
 
 
 def norm_backward(values, grads, gain):
@@ -161,7 +165,7 @@
 def attention_backward(
     rows, sel, states_ref, own_ref, other_ref, mid_own_ref, mid_other_ref, upstream_ref, keep_ref, gains_ref,
     mix_ref, weights_ref, packed_ref, probs_ref,
-    mixed_ref, packed_grad_ref, out_ref, middle_grad_ref, gain_grad_ref,
+    mixed_ref, packed_grad_ref, out_ref, middle_grad_ref, gain_grad_ref, context_grad_ref,
 ):
     mid_gain, router = gains_ref[1:2, :], gains_ref[2:3, :]
     half = mix_ref.shape[1]
@@ -180,42 +184,54 @@
         gate = jax.nn.sigmoid(jnp.sum(states * router, axis=-1, keepdims=True)) * keep_ref[here, :]
         mixed = (gate * upstream_ref[here, :].astype(F32) + middle_grad).astype(BF)
         mixed_ref[here, :] = mixed
-        context_grad = mm(mixed, mix_ref[...]).astype(BF)
-        first = first_head()
+
+    context_grad_ref[...] = mm(mixed_ref[...], mix_ref[...]).astype(BF)
+    first = first_head()
+
+    @pl.loop(0, rows, unroll=True)
+    def _(row):
+        here = pl.ds(pl.multiple_of(row * sel, sel), sel)
         for pair in range(half // (2 * HD)):
             at = pair * 2 * HD
             queries = packed_ref[here, at : at + 2 * HD]
             keys = packed_ref[here, half + at : half + at + 2 * HD]
             vals = packed_ref[here, 2 * half + at : 2 * half + at + 2 * HD]
-            grads = context_grad[:, at : at + 2 * HD]
+            grads = context_grad_ref[here, at : at + 2 * HD]
+            queries_up, grads_up = queries.T, grads.T
             by_query, by_key, by_value = [], [], []
             for head in range(2):
                 mine = first if head == 0 else ~first
+                lanes = slice(head * HD, (head + 1) * HD)
                 probs = probs_ref[row, 2 * pair + head]
                 prob_grad = mm_nt(jnp.where(mine, grads, jnp.zeros_like(grads)), vals)
                 centre = jnp.sum(probs * prob_grad, axis=-1, keepdims=True)
                 score_grad = (probs * (prob_grad - centre)).astype(BF)
                 by_query.append(mm(score_grad, keys))
-                by_key.append(mm_tn(score_grad, queries))
-                by_value.append(mm_tn(probs.astype(BF), grads))
+                by_key.append(mm(queries_up[lanes], score_grad))
+                by_value.append(mm(grads_up[lanes], probs.astype(BF)))
             packed_grad_ref[here, at : at + 2 * HD] = (
                 jnp.where(first, by_query[0], by_query[1]) * scale
             ).astype(BF)
             packed_grad_ref[here, half + at : half + at + 2 * HD] = (
-                jnp.where(first, by_key[0], by_key[1]) * scale
-            ).astype(BF)
-            packed_grad_ref[here, 2 * half + at : 2 * half + at + 2 * HD] = jnp.where(
-                first, by_value[0], by_value[1]
-            ).astype(BF)
-        out_ref[here, :] = mm_nt(packed_grad_ref[here, :], weights_ref[:, : 3 * half]).astype(BF)
+                (jnp.concatenate(by_key, axis=0) * scale).astype(BF).T
+            )
+            packed_grad_ref[here, 2 * half + at : 2 * half + at + 2 * HD] = (
+                jnp.concatenate(by_value, axis=0).astype(BF).T
+            )
+
+    chunk = 256
+    for at in range(0, out_ref.shape[1], chunk):
+        here = slice(at, at + chunk)
+        out_ref[:, here] = mm_nt(packed_grad_ref[...], weights_ref[here, : 3 * half]).astype(BF)
 
 
 def projection_grads(normed_ref, packed_grad_ref, mixed_ref, context_ref, grad_ref):
-    tall = 256
-    wide = packed_grad_ref.shape[1]
-    for at in range(0, grad_ref.shape[0], tall):
-        grad_ref[at : at + tall, :wide] = mm_tn(normed_ref[:, at : at + tall], packed_grad_ref[...]).astype(BF)
-        grad_ref[at : at + tall, wide:] = mm_tn(mixed_ref[:, at : at + tall], context_ref[...]).astype(BF)
+    wide, chunk = packed_grad_ref.shape[1], 384
+    upright_normed, upright_mixed = normed_ref[...].T, mixed_ref[...].T
+    for at in range(0, wide, chunk):
+        here = slice(at, at + chunk)
+        grad_ref[:, here] = mm(upright_normed, packed_grad_ref[:, here]).astype(BF)
+    grad_ref[:, wide:] = mm(upright_mixed, context_ref[...]).astype(BF)
 
 
 def final_forward(
@@ -332,12 +348,13 @@
     long = length // 2
 
     def body(*refs):
-        put_rows(*refs[:4], refs[-1])
+        put_rows(*refs[:4], refs[-2])
+        refs[-1][...] = jnp.zeros_like(refs[-1])
 
     return pl.pallas_call(
         body,
         grid=(rows, length // long),
-        out_shape=shape(base.shape),
+        out_shape=(shape(base.shape), shape((8, 128), F32)),
         in_specs=[
             pl.BlockSpec(memory_space=pltpu.SMEM),
             pl.BlockSpec(chosen.shape, lambda row, part: (0, 0)),
@@ -345,7 +362,10 @@
             pl.BlockSpec((1, long, half), lambda row, part: (row, part, 0)),
         ]
         + [pl.BlockSpec(memory_space=pl.ANY)] * len(after),
-        out_specs=pl.BlockSpec((1, long, half), lambda row, part: (row, part, 0)),
+        out_specs=[
+            pl.BlockSpec((1, long, half), lambda row, part: (row, part, 0)),
+            pl.BlockSpec((8, 128), lambda row, part: (0, 0)),
+        ],
         compiler_params=pltpu.CompilerParams(vmem_limit_bytes=24 << 20),
         cost_estimate=pl.CostEstimate(
             flops=2 * rows * sel * length * half, bytes_accessed=4 * base.size, transcendentals=0
@@ -638,7 +658,7 @@
     first_parts = send(first_parts, 0)
     second_far = start_exchange(cube, Part(tie(second_own, *arrived([first_far]))[None], []), cube.far[-1])
     for step in range(1, steps):
-        after = arrived([second_far]) if step == steps - 1 else []
+        after = arrived([second_far]) if step == steps - 1 else [states, upstream] if step == 1 else []
         first_parts = send(stack(cube, first_parts, step_bits(step - 1), after), step)
     first_last = [p.value for p in first_parts]
     first = whole(cube, first_parts, step_bits(steps - 1))
@@ -689,7 +709,7 @@
     down = whole(cube, down_parts, step_bits(steps - 1), [activated])
 
     hidden_grad, mid_own = call(
-        functools.partial(down_backward, *by_row),
+        down_backward,
         (tall, wide),
         (feed_grad, down, slope, up),
         flops=4 * token_count * width * hidden_here,
@@ -725,26 +745,26 @@
         ),
         (states, att_own, att_other, mid_own, mid_other, upstream, keep, gains, mix, first, packed, probs),
         after=[both_grads[0].value],
+        scratch=[pltpu.VMEM((token_count, half_width), BF)],
         flops=10 * token_count * width * half_width,
         name="attention_backward",
     )
+    (first_grad,) = call(
+        projection_grads,
+        (shape((width, 4 * half_width)),),
+        (normed, packed_grad, mixed, context),
+        flops=8 * token_count * width * half_width,
+        name="projection_grads",
+    )
+    both_grads = fold(cube, alone(both_grads), back_bits(1), [first_grad])
+    pre_other = other_core(tie(pre_own, both_grads[0].value))
     finished, logit_grad, router_grad = call(
         functools.partial(final_forward, *by_row),
         (wide, shape((token_count, 1), F32), vector),
         (states, upstream, att_own, att_other, feed_own, feed_other, gains, keep),
-        after=[packed_grad],
+        after=[both_grads[0].value],
         name="final_forward",
     )
-    (first_grad,) = call(
-        projection_grads,
-        (shape((width, 4 * half_width)),),
-        (normed, packed_grad, mixed, context),
-        after=[finished],
-        flops=8 * token_count * width * half_width,
-        name="projection_grads",
-    )
-    both_grads = fold(cube, alone(both_grads), back_bits(1), [first_grad])
-    pre_other = other_core(tie(pre_own, both_grads[0].value))
     total_grad, vector_grads = call(
         functools.partial(final_backward, *by_row),
         (wide, shape((width, 128))),
@@ -755,12 +775,12 @@
     first_grads = alone(cut(cube, first_grad))
     first_grads[-1] += cut(cube, vector_grads)
     first_grads = fold(cube, first_grads, back_bits(0))
-    result = put(tokens, chosen, finished, cube.bits, [first_grads[0].value])
-    tokens_grad = put(cotangent, chosen, total_grad, cube.bits, [result])
+    result, done = put(tokens, chosen, finished, cube.bits, [first_grads[0].value])
+    tokens_grad, _ = put(cotangent, chosen, total_grad, cube.bits, [done])
     for step in range(2, steps):
         both_grads = fold(cube, alone(both_grads), back_bits(step), [first_grad] if step == 2 else [])
     for step in range(1, steps):
-        first_grads = fold(cube, alone(first_grads), back_bits(step), [result] if step == 1 else [])
+        first_grads = fold(cube, alone(first_grads), back_bits(step), [done] if step == 1 else [])
     both_grads, first_grads = [both_grads], [first_grads]
     for bit in cube.far:
         both_grads = [fold(cube, both_grads, [bit])]

time: 187 us -> 178 us (0.952)
  local copies, waits for them, and re-layouts: 9.64 us -> 5.57 us
  Pallas kernels: 74.1 us -> 70.5 us
    unnamed x35 -> x27, local copies, waits for them, and re-layouts: 8.71 us -> 4.68 us
    pallas_call x32, Pallas kernels: 55.4 us -> 51.8 us  [call(): pl.pallas_call(body, out_shape=outs, in_specs=[pl.BlockSpec(memory_space=...]
    ppermute x43, starting transfers between devices: 44.6 us -> 46.9 us  [swap(): lax.ppermute(value, 'dp', [(i, i ^ 1 << bit) for i in range(self.count)])]
  transfers between devices with their start and end apart: 48 -> 48, of which waited for: 23 -> 22; matrix products, arithmetic and copies ran while one was open for 1% -> 0% of each run, Pallas kernels for 36% -> 36%
where the time goes in v5:
time: 178 us
  Pallas kernels  70.5 us (40%)
  waiting for transfers between devices  52.3 us (29%)
  starting transfers between devices  47.1 us (26%)
  local copies, waits for them, and re-layouts  5.57 us (3%)
    ppermute x43, waiting for transfers between devices, swap(): lax.ppermute(value, 'dp', [(i, i ^ 1 << bit) for i in range(self.count)])  52.3 us
    pallas_call x32, Pallas kernels, call(): pl.pallas_call(body, out_shape=outs, in_specs=[pl.BlockSpec(memory_space=...  51.8 us
    ppermute x43, starting transfers between devices, swap(): lax.ppermute(value, 'dp', [(i, i ^ 1 << bit) for i in range(self.count)])  46.9 us
    pallas_call x2, Pallas kernels, put(): pl.pallas_call(body, grid=(rows, length // long), out_shape=(shape(base.s...  10 us
    pallas_call x1, Pallas kernels, select(): pl.pallas_call(select_rows, grid=(rows,), out_shape=(shape((2, rows, sel,...  8.64 us
    unnamed x27, local copies, waits for them, and re-layouts  4.68 us
  transfers between devices with their start and end apart: 48, of which 22 were waited for; matrix products, arithmetic and copies ran while one was open for 0% of the time, Pallas kernels for 36%

profile of v5, /device:TPU:0, one launch (start us, length us, event | category | flops | bytes accessed | tf_op | source)
XLA Modules:
  0.0 177.8 jit_solution(11828503858378108505)
XLA Ops:
  3.1 4.1 %collective-permute-start = (bf16[1,48,1664]{2,1,0:T(8,128)(2,1)S(1)}, bf16[1,48,1664]{2,1,0:T(8,128)(2,1)S(1)}, u32[]{:S(2)}, u32[]{:S(2)}) collective-permute-start(bf16[1,48,1664]{2,1,0:T(8,128)(2,1)S(1)} %bitcast.144), channel_id=1, source_target_pairs={{0,16},{2,18},{4,20},{6,22},{8,24},{10,26},{12,28},{14,30},{16,0},... | collective-permute-start | bytes 479240 | tf_op jit(solution)/shard_map/ppermute | solution.py:428
  7.3 8.6 %select_rows.1 = (bf16[2,3,256,384]{3,2,1,0:T(8,128)(2,1)}, f32[3,256,256]{2,1,0:T(8,128)}, f32[768,1]{1,0:T(8,128)}) custom-call(bf16[3,2048,384]{2,1,0:T(8,128)(2,1)} %refs_3_.2, bf16[3,2048,384]{2,1,0:T(8,128)(2,1)} %refs_3_.3, s32[3,256]{1,0:T(4,128)} %refs_1_.3, s32[3,2048]{1,0:T(4,128)} %segments_ref.1, s32[3,2048]{1,0:T(4,128)} %present_ref.1), custom_call_target="tpu_custom_call" | custom-call | flops 2415919104 | bytes 9437184 | tf_op jit(solution)/shard_map/select_rows/pallas_call | solution.py:311
  19.5 1.6 collective-permute-start.2
  22.6 1.6 collective-permute-start.4
  26.0 1.9 %collective-permute-done.4.refs_6_ = bf16[2,48,512]{2,1,0:T(8,128)(2,1)S(1)} collective-permute-done((bf16[2,48,512]{2,1,0:T(8,128)(2,1)S(1)}, bf16[2,48,512]{2,1,0:T(8,128)(2,1)S(1)}, u32[]{:S(2)}, u32[]{:S(2)}) %collective-permute-start.4) | collective-permute-done | bytes 98336 | tf_op jit(solution)/shard_map/ppermute | solution.py:428
  28.5 1.9 %collective-permute-start.6 = (bf16[4,48,640]{2,1,0:T(8,128)(2,1)S(1)}, bf16[4,48,640]{2,1,0:T(8,128)(2,1)S(1)}, u32[]{:S(2)}, u32[]{:S(2)}) collective-permute-start(bf16[4,48,640]{2,1,0:T(8,128)(2,1)S(1)} %bitcast.163), channel_id=1, source_target_pairs={{0,8},{2,10},{4,12},{6,14},{8,0},{10,2},{12,4},{14,6},{16,24},{18,... | collective-permute-start | bytes 737288 | tf_op jit(solution)/shard_map/ppermute | solution.py:428
  31.5 7.6 %collective-permute-done.8.refs_7_.refs_2_ = bf16[1,48,3072]{2,1,0:T(8,128)(2,1)S(1)} collective-permute-done((bf16[1,48,3072]{2,1,0:T(8,128)(2,1)S(1)}, bf16[1,48,3072]{2,1,0:T(8,128)(2,1)S(1)}, u32[]{:S(2)}, u32[]{:S(2)}) %collective-permute-start.8) | collective-permute-done | bytes 294944 | tf_op jit(solution)/shard_map/ppermute | solution.py:428
  42.4 1.6 collective-permute-start.12
  45.5 6.3 %collective-permute-done.11.refs_6_ = bf16[8,48,512]{2,1,0:T(8,128)(2,1)S(1)} collective-permute-done((bf16[8,48,512]{2,1,0:T(8,128)(2,1)S(1)}, bf16[8,48,512]{2,1,0:T(8,128)(2,1)S(1)}, u32[]{:S(2)}, u32[]{:S(2)}) %collective-permute-start.11) | collective-permute-done | bytes 393248 | tf_op jit(solution)/shard_map/ppermute | solution.py:428
  52.4 1.7 collective-permute-done.10.refs_4_
  59.9 4.8 %attention_forward.1 = (bf16[768,768]{1,0:T(8,128)(2,1)S(1)}, bf16[768,1152]{1,0:T(8,128)(2,1)S(1)}, f32[3,6,256,256]{3,2,1,0:T(8,128)S(1)}, bf16[768,384]{1,0:T(8,128)(2,1)S(1)}, f32[8,768]{1,0:T(8,128)S(1)}) custom-call(bf16[768,768]{1,0:T(8,128)(2,1)S(1)} %bitcast.89, bf16[768,1664]{1,0:T(8,128)(2,1)S(1)} %bitcast.86, f32[3,256,256]{2,1,0:T(8,128)S(1)} %copy-done.3, ...), custom_call_target="tpu_custom_call" | custom-call | flops 1358954496 | bytes 12804096 | tf_op jit(solution)/shard_map/attention_forward/pallas_call | solution.py:42
  70.1 1.6 collective-permute-start.21
  72.3 7.7 %collective-permute-done.19.refs_2_ = bf16[8,48,512]{2,1,0:T(8,128)(2,1)S(1)} collective-permute-done((bf16[8,48,512]{2,1,0:T(8,128)(2,1)S(1)}, bf16[8,48,512]{2,1,0:T(8,128)(2,1)S(1)}, u32[]{:S(2)}, u32[]{:S(2)}) %collective-permute-start.19) | collective-permute-done | bytes 393248 | tf_op jit(solution)/shard_map/ppermute | solution.py:428
  82.7 6.7 %up_forward.1 = (bf16[768,768]{1,0:T(8,128)(2,1)S(1)}, bf16[768,1536]{1,0:T(8,128)(2,1)S(1)}, bf16[768,1536]{1,0:T(8,128)(2,1)S(1)}, bf16[768,768]{1,0:T(8,128)(2,1)S(1)}, bf16[768,1536]{1,0:T(8,128)(2,1)S(1)}) custom-call(bf16[768,768]{1,0:T(8,128)(2,1)S(1)} %bitcast.90, bf16[768,768]{1,0:T(8,128)(2,1)S(1)} %bitcast.95, ...), custom_call_target="tpu_custom_call" | custom-call | flops 3623878656 | bytes 16542720 | tf_op jit(solution)/shard_map/up_forward/pallas_call | solution.py:42
  90.1 4.0 %down_backward.1 = (bf16[768,1536]{1,0:T(8,128)(2,1)S(1)}, bf16[768,768]{1,0:T(8,128)(2,1)S(1)}) custom-call(bf16[768,768]{1,0:T(8,128)(2,1)S(1)} %get-tuple-element.126.refs_0_, bf16[768,1536]{1,0:T(8,128)(2,1)S(1)} %bitcast.114, bf16[768,1536]{1,0:T(8,128)(2,1)S(1)} %get-tuple-element.128.refs_2_, bf16[768,1536]{1,0:T(8,128)(2,1)S(1)} %bitcast.117), custom_call_target="tpu_custom_call" | custom-call | flops 3623878656 | bytes 11796480 | tf_op jit(solution)/shard_map/down_backward/pallas_call | solution.py:42
  94.2 3.8 %down_forward.1 = (bf16[768,1536]{1,0:T(8,128)(2,1)S(1)}, bf16[768,768]{1,0:T(8,128)(2,1)S(1)}) custom-call(bf16[768,768]{1,0:T(8,128)(2,1)S(1)} %get-tuple-element.125.refs_0_, bf16[768,1536]{1,0:T(8,128)(2,1)S(1)} %get-tuple-element.129.refs_1_, bf16[768,1536]{1,0:T(8,128)(2,1)S(1)} %get-tuple-element.127.refs_7_.refs_2_, bf16[768,1536]{1,0:T(8,128)(2,1)S(1)} %bitcast.115), custom_call_target="tpu_custom_call" | custom-call | flops 3623878656 | bytes 11796480 | tf_op jit(solution)/shard_map/down_forward/pallas_call | solution.py:42
  100.5 1.6 collective-permute-start.27
  102.6 11.7 %attention_backward.1 = (bf16[768,768]{1,0:T(8,128)(2,1)S(1)}, bf16[768,1152]{1,0:T(8,128)(2,1)S(1)}, bf16[768,768]{1,0:T(8,128)(2,1)S(1)}, f32[768,768]{1,0:T(8,128)S(1)}, f32[8,768]{1,0:T(8,128)S(1)}) custom-call(bf16[768,768]{1,0:T(8,128)(2,1)S(1)} %bitcast.91, bf16[768,768]{1,0:T(8,128)(2,1)S(1)} %mix_forward.1.refs_2_.refs_1_, ...), custom_call_target="tpu_custom_call" | custom-call | flops 2264924160 | bytes 23251968 | tf_op jit(solution)/shard_map/attention_backward/pallas_call | solution.py:42
  114.4 2.6 %projection_grads.1.refs_7_ = bf16[768,1536]{1,0:T(8,128)(2,1)S(1)} custom-call(bf16[768,768]{1,0:T(8,128)(2,1)S(1)} %get-tuple-element.139.refs_0_, bf16[768,1152]{1,0:T(8,128)(2,1)S(1)} %get-tuple-element.143.refs_1_, bf16[768,768]{1,0:T(8,128)(2,1)S(1)} %get-tuple-element.144.refs_2_, bf16[768,384]{1,0:T(8,128)(2,1)S(1)} %get-tuple-element.119.refs_0_.refs_3_), custom_call_target="tpu_custom_call" | custom-call | flops 1811939328 | bytes 7077888 | tf_op jit(solution)/shard_map/projection_grads/pallas_call | solution.py:42
  117.1 2.0 %collective-permute-done.26 = bf16[8,48,1024]{2,1,0:T(8,128)(2,1)S(1)} collective-permute-done((bf16[8,48,1024]{2,1,0:T(8,128)(2,1)S(1)}, bf16[8,48,1024]{2,1,0:T(8,128)(2,1)S(1)}, u32[]{:S(2)}, u32[]{:S(2)}) %collective-permute-start.26) | collective-permute-done | bytes 786464 | tf_op jit(solution)/shard_map/ppermute | solution.py:428
  125.2 1.7 final_forward.1
  126.9 1.9 %final_backward.1 = (bf16[768,768]{1,0:T(8,128)(2,1)S(1)}, bf16[768,128]{1,0:T(8,128)(2,1)S(1)}) custom-call(bf16[768,768]{1,0:T(8,128)(2,1)S(1)} %bitcast.93, bf16[768,768]{1,0:T(8,128)(2,1)S(1)} %bitcast.98, f32[768,768]{1,0:T(8,128)S(1)} %get-tuple-element.147.refs_2_, bf16[768,768]{1,0:T(8,128)(2,1)S(1)} %get-tuple-element.148.refs_3_, ...), custom_call_target="tpu_custom_call" | custom-call | bytes 8530944 | tf_op jit(solution)/shard_map/final_backward/pallas_call | solution.py:42
  131.7 2.9 %collective-permute-done.41 = bf16[4,48,1024]{2,1,0:T(8,128)(2,1)S(1)} collective-permute-done((bf16[4,48,1024]{2,1,0:T(8,128)(2,1)S(1)}, bf16[4,48,1024]{2,1,0:T(8,128)(2,1)S(1)}, u32[]{:S(2)}, u32[]{:S(2)}) %collective-permute-start.41) | collective-permute-done | bytes 393248 | tf_op jit(solution)/shard_map/ppermute | solution.py:428
  138.0 4.8 %collective-permute-done.31 = bf16[8,48,512]{2,1,0:T(8,128)(2,1)S(1)} collective-permute-done((bf16[8,48,512]{2,1,0:T(8,128)(2,1)S(1)}, bf16[8,48,512]{2,1,0:T(8,128)(2,1)S(1)}, u32[]{:S(2)}, u32[]{:S(2)}) %collective-permute-start.31) | collective-permute-done | bytes 393248 | tf_op jit(solution)/shard_map/ppermute | solution.py:428
  144.0 5.0 %put_rows.2 = (bf16[3,2048,384]{2,1,0:T(8,128)(2,1)}, f32[8,128]{1,0:T(8,128)S(1)}) custom-call(s32[5]{0:T(128)S(1)} %pad_add_fusion.refs_0_, s32[3,256]{1,0:T(4,128)S(1)} %copy-done.7, bf16[768,768]{1,0:T(8,128)(2,1)S(1)} %get-tuple-element.146.refs_2_, bf16[3,2048,384]{2,1,0:T(8,128)(2,1)S(1)} %bitcast.106, f32[8,48,512]{2,1,0:T(8,128)S(1)} %get-tuple-element.153.refs_4_), custom_call_target="tpu_custom_call" | custom-call | flops 1207959552 | bytes 9437184 | tf_op jit(solution)/shard_map/put_rows/pallas_call | solution.py:354
  154.6 1.8 %collective-permute-done.34 = bf16[4,48,512]{2,1,0:T(8,128)(2,1)S(1)} collective-permute-done((bf16[4,48,512]{2,1,0:T(8,128)(2,1)S(1)}, bf16[4,48,512]{2,1,0:T(8,128)(2,1)S(1)}, u32[]{:S(2)}, u32[]{:S(2)}) %collective-permute-start.34) | collective-permute-done | bytes 196640 | tf_op jit(solution)/shard_map/ppermute | solution.py:428
  156.4 3.7 %collective-permute-done.35 = bf16[4,48,512]{2,1,0:T(8,128)(2,1)S(1)} collective-permute-done((bf16[4,48,512]{2,1,0:T(8,128)(2,1)S(1)}, bf16[4,48,512]{2,1,0:T(8,128)(2,1)S(1)}, u32[]{:S(2)}, u32[]{:S(2)}) %collective-permute-start.35) | collective-permute-done | bytes 196640 | tf_op jit(solution)/shard_map/ppermute | solution.py:428
  161.3 1.6 collective-permute-start.37
  163.4 2.5 %collective-permute-done.37 = bf16[2,48,512]{2,1,0:T(8,128)(2,1)S(1)} collective-permute-done((bf16[2,48,512]{2,1,0:T(8,128)(2,1)S(1)}, bf16[2,48,512]{2,1,0:T(8,128)(2,1)S(1)}, u32[]{:S(2)}, u32[]{:S(2)}) %collective-permute-start.37) | collective-permute-done | bytes 98336 | tf_op jit(solution)/shard_map/ppermute | solution.py:428
  165.9 1.6 collective-permute-done.38
  168.1 2.6 %collective-permute-start.40 = (bf16[1,48,1664]{2,1,0:T(8,128)(2,1)S(1)}, bf16[1,48,1664]{2,1,0:T(8,128)(2,1)S(1)}, u32[]{:S(2)}, u32[]{:S(2)}) collective-permute-start(bf16[1,48,1664]{2,1,0:T(8,128)(2,1)S(1)} %get-tuple-element.176), channel_id=1, source_target_pairs={{0,16},{2,18},{4,20},{6,22},{8,24},{10,26},{12,28},{14,30},{16,0},... | collective-permute-start | bytes 479240 | tf_op jit(solution)/shard_map/ppermute | solution.py:428
  171.5 5.0 %put_rows.3 = (bf16[3,2048,384]{2,1,0:T(8,128)(2,1)}, f32[8,128]{1,0:T(8,128)}) custom-call(s32[5]{0:T(128)S(1)} %pad_add_fusion.refs_0_, s32[3,256]{1,0:T(4,128)S(1)} %copy-done.7, bf16[768,768]{1,0:T(8,128)(2,1)S(1)} %get-tuple-element.155.refs_2_, bf16[3,2048,384]{2,1,0:T(8,128)(2,1)S(1)} %bitcast.108, f32[8,128]{1,0:T(8,128)S(1)} %get-tuple-element.156.refs_4_.refs_7_), custom_call_target="tpu_custom_call" | custom-call | flops 1207959552 | bytes 9437184 | tf_op jit(solution)/shard_map/put_rows/pallas_call | solution.py:354
  (144 shorter events, 58.4 us)
Async XLA Ops:
  3.1 12.8 %collective-permute-start = (bf16[1,48,1664]{2,1,0:T(8,128)(2,1)S(1)}, bf16[1,48,1664]{2,1,0:T(8,128)(2,1)S(1)}, u32[]{:S(2)}, u32[]{:S(2)}) collective-permute-start(bf16[1,48,1664]{2,1,0:T(8,128)(2,1)S(1)} %bitcast.144), channel_id=1, source_target_pairs={{0,16},{2,18},{4,20},{6,22},{8,24},{10,26},{12,28},{14,30},{16,0},... | collective-permute-start | bytes 479240 | tf_op jit(solution)/shard_map/ppermute | solution.py:428
  24.2 14.9 %collective-permute-start.8 = (bf16[1,48,3072]{2,1,0:T(8,128)(2,1)S(1)}, bf16[1,48,3072]{2,1,0:T(8,128)(2,1)S(1)}, u32[]{:S(2)}, u32[]{:S(2)}) collective-permute-start(bf16[1,48,3072]{2,1,0:T(8,128)(2,1)S(1)} %bitcast.112), channel_id=1, source_target_pairs={{0,16},{2,18},{4,20},{6,22},{8,24},{10,26},{12,28},{14,30},{16,0},... | collective-permute-start | bytes 884744 | tf_op jit(solution)/shard_map/ppermute | solution.py:428
  28.5 11.5 %collective-permute-start.6 = (bf16[4,48,640]{2,1,0:T(8,128)(2,1)S(1)}, bf16[4,48,640]{2,1,0:T(8,128)(2,1)S(1)}, u32[]{:S(2)}, u32[]{:S(2)}) collective-permute-start(bf16[4,48,640]{2,1,0:T(8,128)(2,1)S(1)} %bitcast.163), channel_id=1, source_target_pairs={{0,8},{2,10},{4,12},{6,14},{8,0},{10,2},{12,4},{14,6},{16,24},{18,... | collective-permute-start | bytes 737288 | tf_op jit(solution)/shard_map/ppermute | solution.py:428
  30.4 8.6 %collective-permute-start.5 = (bf16[4,48,512]{2,1,0:T(8,128)(2,1)S(1)}, bf16[4,48,512]{2,1,0:T(8,128)(2,1)S(1)}, u32[]{:S(2)}, u32[]{:S(2)}) collective-permute-start(bf16[4,48,512]{2,1,0:T(8,128)(2,1)S(1)} %bitcast.173), channel_id=1, source_target_pairs={{0,4},{2,6},{4,0},{6,2},{8,12},{10,14},{12,8},{14,10},{16,20},{18,... | collective-permute-start | bytes 589832 | tf_op jit(solution)/shard_map/ppermute | solution.py:428
  40.7 11.2 %collective-permute-start.11 = (bf16[8,48,512]{2,1,0:T(8,128)(2,1)S(1)}, bf16[8,48,512]{2,1,0:T(8,128)(2,1)S(1)}, u32[]{:S(2)}, u32[]{:S(2)}) collective-permute-start(bf16[8,48,512]{2,1,0:T(8,128)(2,1)S(1)} %bitcast.160), channel_id=1, source_target_pairs={{0,4},{2,6},{4,0},{6,2},{8,12},{10,14},{12,8},{14,10},{16,20},{18,... | collective-permute-start | bytes 1179656 | tf_op jit(solution)/shard_map/ppermute | solution.py:428
  41.3 12.9 %collective-permute-start.10 = (bf16[8,48,640]{2,1,0:T(8,128)(2,1)S(1)}, bf16[8,48,640]{2,1,0:T(8,128)(2,1)S(1)}, u32[]{:S(2)}, u32[]{:S(2)}) collective-permute-start(bf16[8,48,640]{2,1,0:T(8,128)(2,1)S(1)} %bitcast.148), channel_id=1, source_target_pairs={{0,2},{2,0},{4,6},{6,4},{8,10},{10,8},{12,14},{14,12},{16,18},{18,... | collective-permute-start | bytes 1474568 | tf_op jit(solution)/shard_map/ppermute | solution.py:428
  41.8 10.6 %collective-permute-start.9 = (bf16[8,48,512]{2,1,0:T(8,128)(2,1)S(1)}, bf16[8,48,512]{2,1,0:T(8,128)(2,1)S(1)}, u32[]{:S(2)}, u32[]{:S(2)}) collective-permute-start(bf16[8,48,512]{2,1,0:T(8,128)(2,1)S(1)} %bitcast.130), channel_id=1, source_target_pairs={{0,8},{2,10},{4,12},{6,14},{8,0},{10,2},{12,4},{14,6},{16,24},{18,... | collective-permute-start | bytes 1179656 | tf_op jit(solution)/shard_map/ppermute | solution.py:428
  42.4 13.8 %collective-permute-start.12 = (bf16[2,48,1024]{2,1,0:T(8,128)(2,1)S(1)}, bf16[2,48,1024]{2,1,0:T(8,128)(2,1)S(1)}, u32[]{:S(2)}, u32[]{:S(2)}) collective-permute-start(bf16[2,48,1024]{2,1,0:T(8,128)(2,1)S(1)} %get-tuple-element.113.refs_1_), channel_id=1, source_target_pairs={{0,2},{2,0},{4,6},{6,4},{8,10},{10,8},{12,14},{14,12},{16,18},{18,... | collective-permute-start | bytes 589832 | tf_op jit(solution)/shard_map/ppermute | solution.py:428
  44.0 12.3 %collective-permute-start.13 = (bf16[2,48,1024]{2,1,0:T(8,128)(2,1)S(1)}, bf16[2,48,1024]{2,1,0:T(8,128)(2,1)S(1)}, u32[]{:S(2)}, u32[]{:S(2)}) collective-permute-start(bf16[2,48,1024]{2,1,0:T(8,128)(2,1)S(1)} %get-tuple-element.114.refs_3_), channel_id=1, source_target_pairs={{0,4},{2,6},{4,0},{6,2},{8,12},{10,14},{12,8},{14,10},{16,20},{18,... | collective-permute-start | bytes 589832 | tf_op jit(solution)/shard_map/ppermute | solution.py:428
  65.5 17.2 %collective-permute-start.15 = (bf16[768,768]{1,0:T(8,128)(2,1)S(1)}, bf16[768,768]{1,0:T(8,128)(2,1)S(1)}, u32[]{:S(2)}, u32[]{:S(2)}) collective-permute-start(bf16[768,768]{1,0:T(8,128)(2,1)S(1)} %mix_forward.1.refs_2_.refs_1_), channel_id=1, source_target_pairs={{0,1},{1,0},{2,3},{3,2},{4,5},{5,4},{6,7},{7,6},{8,9},{9,8},{10,11... | collective-permute-start | bytes 3538952 | tf_op jit(solution)/shard_map/ppermute | solution.py:582
  67.9 12.1 %collective-permute-start.19 = (bf16[8,48,512]{2,1,0:T(8,128)(2,1)S(1)}, bf16[8,48,512]{2,1,0:T(8,128)(2,1)S(1)}, u32[]{:S(2)}, u32[]{:S(2)}) collective-permute-start(bf16[8,48,512]{2,1,0:T(8,128)(2,1)S(1)} %get-tuple-element.204.refs_1_), channel_id=1, source_target_pairs={{0,8},{2,10},{4,12},{6,14},{8,0},{10,2},{12,4},{14,6},{16,24},{18,... | collective-permute-start | bytes 1179656 | tf_op jit(solution)/shard_map/ppermute | solution.py:428
  69.5 11.0 %collective-permute-start.20 = (bf16[8,48,512]{2,1,0:T(8,128)(2,1)S(1)}, bf16[8,48,512]{2,1,0:T(8,128)(2,1)S(1)}, u32[]{:S(2)}, u32[]{:S(2)}) collective-permute-start(bf16[8,48,512]{2,1,0:T(8,128)(2,1)S(1)} %get-tuple-element.202.refs_3_), channel_id=1, source_target_pairs={{0,2},{2,0},{4,6},{6,4},{8,10},{10,8},{12,14},{14,12},{16,18},{18,... | collective-permute-start | bytes 1179656 | tf_op jit(solution)/shard_map/ppermute | solution.py:428
  70.1 11.9 %collective-permute-start.21 = (bf16[8,48,512]{2,1,0:T(8,128)(2,1)S(1)}, bf16[8,48,512]{2,1,0:T(8,128)(2,1)S(1)}, u32[]{:S(2)}, u32[]{:S(2)}) collective-permute-start(bf16[8,48,512]{2,1,0:T(8,128)(2,1)S(1)} %get-tuple-element.200.refs_5_), channel_id=1, source_target_pairs={{0,4},{2,6},{4,0},{6,2},{8,12},{10,14},{12,8},{14,10},{16,20},{18,... | collective-permute-start | bytes 1179656 | tf_op jit(solution)/shard_map/ppermute | solution.py:428
  71.7 17.7 %collective-permute-start.22 = (bf16[8,48,512]{2,1,0:T(8,128)(2,1)S(1)}, bf16[8,48,512]{2,1,0:T(8,128)(2,1)S(1)}, u32[]{:S(2)}, u32[]{:S(2)}) collective-permute-start(bf16[8,48,512]{2,1,0:T(8,128)(2,1)S(1)} %get-tuple-element.203.refs_1_), channel_id=1, source_target_pairs={{0,8},{2,10},{4,12},{6,14},{8,0},{10,2},{12,4},{14,6},{16,24},{18,... | collective-permute-start | bytes 1179656 | tf_op jit(solution)/shard_map/ppermute | solution.py:428
  80.0 9.4 %collective-permute-start.23 = (bf16[8,48,512]{2,1,0:T(8,128)(2,1)S(1)}, bf16[8,48,512]{2,1,0:T(8,128)(2,1)S(1)}, u32[]{:S(2)}, u32[]{:S(2)}) collective-permute-start(bf16[8,48,512]{2,1,0:T(8,128)(2,1)S(1)} %get-tuple-element.201.refs_3_), channel_id=1, source_target_pairs={{0,2},{2,0},{4,6},{6,4},{8,10},{10,8},{12,14},{14,12},{16,18},{18,... | collective-permute-start | bytes 1179656 | tf_op jit(solution)/shard_map/ppermute | solution.py:428
  80.5 8.9 %collective-permute-start.24 = (bf16[8,48,512]{2,1,0:T(8,128)(2,1)S(1)}, bf16[8,48,512]{2,1,0:T(8,128)(2,1)S(1)}, u32[]{:S(2)}, u32[]{:S(2)}) collective-permute-start(bf16[8,48,512]{2,1,0:T(8,128)(2,1)S(1)} %get-tuple-element.199.refs_5_), channel_id=1, source_target_pairs={{0,4},{2,6},{4,0},{6,2},{8,12},{10,14},{12,8},{14,10},{16,20},{18,... | collective-permute-start | bytes 1179656 | tf_op jit(solution)/shard_map/ppermute | solution.py:428
  99.0 20.0 %collective-permute-start.26 = (bf16[8,48,1024]{2,1,0:T(8,128)(2,1)S(1)}, bf16[8,48,1024]{2,1,0:T(8,128)(2,1)S(1)}, u32[]{:S(2)}, u32[]{:S(2)}) collective-permute-start(bf16[8,48,1024]{2,1,0:T(8,128)(2,1)S(1)} %get-tuple-element.134), channel_id=1, source_target_pairs={{0,8},{2,10},{4,12},{6,14},{8,0},{10,2},{12,4},{14,6},{16,24},{18,... | collective-permute-start | bytes 2359304 | tf_op jit(solution)/shard_map/ppermute | solution.py:428
  100.5 19.7 %collective-permute-start.27 = (bf16[8,48,1024]{2,1,0:T(8,128)(2,1)S(1)}, bf16[8,48,1024]{2,1,0:T(8,128)(2,1)S(1)}, u32[]{:S(2)}, u32[]{:S(2)}) collective-permute-start(bf16[8,48,1024]{2,1,0:T(8,128)(2,1)S(1)} %get-tuple-element.136), channel_id=1, source_target_pairs={{0,2},{2,0},{4,6},{6,4},{8,10},{10,8},{12,14},{14,12},{16,18},{18,... | collective-permute-start | bytes 2359304 | tf_op jit(solution)/shard_map/ppermute | solution.py:428
  102.1 19.4 %collective-permute-start.28 = (bf16[8,48,1024]{2,1,0:T(8,128)(2,1)S(1)}, bf16[8,48,1024]{2,1,0:T(8,128)(2,1)S(1)}, u32[]{:S(2)}, u32[]{:S(2)}) collective-permute-start(bf16[8,48,1024]{2,1,0:T(8,128)(2,1)S(1)} %get-tuple-element.138), channel_id=1, source_target_pairs={{0,4},{2,6},{4,0},{6,2},{8,12},{10,14},{12,8},{14,10},{16,20},{18,... | collective-permute-start | bytes 2359304 | tf_op jit(solution)/shard_map/ppermute | solution.py:428
  102.6 22.6 %collective-permute-start.25 = (bf16[768,768]{1,0:T(8,128)(2,1)S(1)}, bf16[768,768]{1,0:T(8,128)(2,1)S(1)}, u32[]{:S(2)}, u32[]{:S(2)}) collective-permute-start(bf16[768,768]{1,0:T(8,128)(2,1)S(1)} %get-tuple-element.130.refs_1_.refs_4_), channel_id=1, source_target_pairs={{0,1},{1,0},{2,3},{3,2},{4,5},{5,4},{6,7},{7,6},{8,9},{9,8},{10,11... | collective-permute-start | bytes 3538952 | tf_op jit(solution)/shard_map/ppermute | solution.py:582
  122.6 12.0 %collective-permute-start.41 = (bf16[4,48,1024]{2,1,0:T(8,128)(2,1)S(1)}, bf16[4,48,1024]{2,1,0:T(8,128)(2,1)S(1)}, u32[]{:S(2)}, u32[]{:S(2)}) collective-permute-start(bf16[4,48,1024]{2,1,0:T(8,128)(2,1)S(1)} %get-tuple-element.179), channel_id=1, source_target_pairs={{0,4},{2,6},{4,0},{6,2},{8,12},{10,14},{12,8},{14,10},{16,20},{18,... | collective-permute-start | bytes 1179656 | tf_op jit(solution)/shard_map/ppermute | solution.py:428
  123.2 12.0 %collective-permute-start.42 = (bf16[4,48,1024]{2,1,0:T(8,128)(2,1)S(1)}, bf16[4,48,1024]{2,1,0:T(8,128)(2,1)S(1)}, u32[]{:S(2)}, u32[]{:S(2)}) collective-permute-start(bf16[4,48,1024]{2,1,0:T(8,128)(2,1)S(1)} %get-tuple-element.181), channel_id=1, source_target_pairs={{0,8},{2,10},{4,12},{6,14},{8,0},{10,2},{12,4},{14,6},{16,24},{18,... | collective-permute-start | bytes 1179656 | tf_op jit(solution)/shard_map/ppermute | solution.py:428
  124.4 10.9 %collective-permute-start.43 = (bf16[4,48,1024]{2,1,0:T(8,128)(2,1)S(1)}, bf16[4,48,1024]{2,1,0:T(8,128)(2,1)S(1)}, u32[]{:S(2)}, u32[]{:S(2)}) collective-permute-start(bf16[4,48,1024]{2,1,0:T(8,128)(2,1)S(1)} %get-tuple-element.183), channel_id=1, source_target_pairs={{0,2},{2,0},{4,6},{6,4},{8,10},{10,8},{12,14},{14,12},{16,18},{18,... | collective-permute-start | bytes 1179656 | tf_op jit(solution)/shard_map/ppermute | solution.py:428
  129.6 13.2 %collective-permute-start.31 = (bf16[8,48,512]{2,1,0:T(8,128)(2,1)S(1)}, bf16[8,48,512]{2,1,0:T(8,128)(2,1)S(1)}, u32[]{:S(2)}, u32[]{:S(2)}) collective-permute-start(bf16[8,48,512]{2,1,0:T(8,128)(2,1)S(1)} %get-tuple-element.158), channel_id=1, source_target_pairs={{0,8},{2,10},{4,12},{6,14},{8,0},{10,2},{12,4},{14,6},{16,24},{18,... | collective-permute-start | bytes 1179656 | tf_op jit(solution)/shard_map/ppermute | solution.py:428
  131.1 18.0 %collective-permute-start.33 = (bf16[8,48,640]{2,1,0:T(8,128)(2,1)S(1)}, bf16[8,48,640]{2,1,0:T(8,128)(2,1)S(1)}, u32[]{:S(2)}, u32[]{:S(2)}) collective-permute-start(bf16[8,48,640]{2,1,0:T(8,128)(2,1)S(1)} %get-tuple-element.162), channel_id=1, source_target_pairs={{0,4},{2,6},{4,0},{6,2},{8,12},{10,14},{12,8},{14,10},{16,20},{18,... | collective-permute-start | bytes 1474568 | tf_op jit(solution)/shard_map/ppermute | solution.py:428
  134.6 14.5 %collective-permute-start.32 = (bf16[8,48,512]{2,1,0:T(8,128)(2,1)S(1)}, bf16[8,48,512]{2,1,0:T(8,128)(2,1)S(1)}, u32[]{:S(2)}, u32[]{:S(2)}) collective-permute-start(bf16[8,48,512]{2,1,0:T(8,128)(2,1)S(1)} %get-tuple-element.160), channel_id=1, source_target_pairs={{0,2},{2,0},{4,6},{6,4},{8,10},{10,8},{12,14},{14,12},{16,18},{18,... | collective-permute-start | bytes 1179656 | tf_op jit(solution)/shard_map/ppermute | solution.py:428
  136.1 15.2 %collective-permute-start.44 = (bf16[2,48,1024]{2,1,0:T(8,128)(2,1)S(1)}, bf16[2,48,1024]{2,1,0:T(8,128)(2,1)S(1)}, u32[]{:S(2)}, u32[]{:S(2)}) collective-permute-start(bf16[2,48,1024]{2,1,0:T(8,128)(2,1)S(1)} %get-tuple-element.185), channel_id=1, source_target_pairs={{0,2},{2,0},{4,6},{6,4},{8,10},{10,8},{12,14},{14,12},{16,18},{18,... | collective-permute-start | bytes 589832 | tf_op jit(solution)/shard_map/ppermute | solution.py:428
  137.5 15.3 %collective-permute-start.45 = (bf16[2,48,1024]{2,1,0:T(8,128)(2,1)S(1)}, bf16[2,48,1024]{2,1,0:T(8,128)(2,1)S(1)}, u32[]{:S(2)}, u32[]{:S(2)}) collective-permute-start(bf16[2,48,1024]{2,1,0:T(8,128)(2,1)S(1)} %get-tuple-element.187), channel_id=1, source_target_pairs={{0,4},{2,6},{4,0},{6,2},{8,12},{10,14},{12,8},{14,10},{16,20},{18,... | collective-permute-start | bytes 589832 | tf_op jit(solution)/shard_map/ppermute | solution.py:428
  142.8 9.9 %collective-permute-start.46 = (bf16[2,48,1024]{2,1,0:T(8,128)(2,1)S(1)}, bf16[2,48,1024]{2,1,0:T(8,128)(2,1)S(1)}, u32[]{:S(2)}, u32[]{:S(2)}) collective-permute-start(bf16[2,48,1024]{2,1,0:T(8,128)(2,1)S(1)} %get-tuple-element.189), channel_id=1, source_target_pairs={{0,8},{2,10},{4,12},{6,14},{8,0},{10,2},{12,4},{14,6},{16,24},{18,... | collective-permute-start | bytes 589832 | tf_op jit(solution)/shard_map/ppermute | solution.py:428
  149.8 10.3 %collective-permute-start.36 = (bf16[4,48,640]{2,1,0:T(8,128)(2,1)S(1)}, bf16[4,48,640]{2,1,0:T(8,128)(2,1)S(1)}, u32[]{:S(2)}, u32[]{:S(2)}) collective-permute-start(bf16[4,48,640]{2,1,0:T(8,128)(2,1)S(1)} %get-tuple-element.168), channel_id=1, source_target_pairs={{0,2},{2,0},{4,6},{6,4},{8,10},{10,8},{12,14},{14,12},{16,18},{18,... | collective-permute-start | bytes 737288 | tf_op jit(solution)/shard_map/ppermute | solution.py:428
  151.3 8.8 %collective-permute-start.35 = (bf16[4,48,512]{2,1,0:T(8,128)(2,1)S(1)}, bf16[4,48,512]{2,1,0:T(8,128)(2,1)S(1)}, u32[]{:S(2)}, u32[]{:S(2)}) collective-permute-start(bf16[4,48,512]{2,1,0:T(8,128)(2,1)S(1)} %get-tuple-element.166), channel_id=1, source_target_pairs={{0,8},{2,10},{4,12},{6,14},{8,0},{10,2},{12,4},{14,6},{16,24},{18,... | collective-permute-start | bytes 589832 | tf_op jit(solution)/shard_map/ppermute | solution.py:428
  153.4 17.2 %collective-permute-start.47 = (bf16[1,48,3072]{2,1,0:T(8,128)(2,1)S(1)}, bf16[1,48,3072]{2,1,0:T(8,128)(2,1)S(1)}, u32[]{:S(2)}, u32[]{:S(2)}) collective-permute-start(bf16[1,48,3072]{2,1,0:T(8,128)(2,1)S(1)} %get-tuple-element.191), channel_id=1, source_target_pairs={{0,16},{2,18},{4,20},{6,22},{8,24},{10,26},{12,28},{14,30},{16,0},... | collective-permute-start | bytes 884744 | tf_op jit(solution)/shard_map/ppermute | solution.py:428
  (29 other events, 206.8 us)
